TPU v7x, 32 devices: a whole 2x2x4 slice. The times are simulated.
32 devices in a mesh: wide: 8 (over z, x), narrow: 4 (over y, core).
Axes of the slice: x: 2, y: 2, z: 4, core: 2. Of those that a mesh axis runs over, the one named last changes fastest.
Arguments:
- tokens: bfloat16 [8192, 1024], P(('wide', 'narrow')), may hold values from -10 to 10
- doc_ids: int32 [8192], P(('wide', 'narrow')), may hold values from 0 to 1023, as said below
- valid_mask: int32 [8192], P(('wide', 'narrow')), may hold values 0 or 1
- routes: int32 [8192, 1], P(('wide', 'narrow')), may hold values from 0 to 15; in each aligned block of 256 rows (0 to 255, 256 to 511, ...) at most 24 rows name the same one
- cotangent: bfloat16 [8192, 1024], P(('wide', 'narrow')), may hold values from -6 to 6
- attend_gain: bfloat16 [1024], P('wide'), may hold values from 0.5 to 1.5
- attend_weight: bfloat16 [1024, 3072], P('wide'), may hold values from -0.1875 to 0.1875
- output_weight: bfloat16 [1024, 1024], P('wide'), may hold values from -1.5 to 1.5
- mixer_gain: bfloat16 [1024], P('wide'), may hold values from 0.5 to 1.5
- router_weight: bfloat16 [1024, 16], P('wide'), may hold values from -0.125 to 0.125
- blend_weight: bfloat16 [1024, 2], P('wide'), may hold values from -0.1875 to 0.1875
- up_weight: bfloat16 [1024, 4096], P('wide'), may hold values from -0.1875 to 0.1875
- down_weight: bfloat16 [4096, 1024], P('wide'), may hold values from -0.09375 to 0.09375
- expert_up: bfloat16 [16, 1024, 4096], P('wide', None, 'narrow'), may hold values from -0.1875 to 0.1875
- expert_down: bfloat16 [16, 4096, 1024], P('wide', 'narrow'), may hold values from -1.5 to 1.5
Outputs:
- layer_out: bfloat16 [8192, 1024], P(('wide', 'narrow'))
- grad_tokens: bfloat16 [8192, 1024], P(('wide', 'narrow'))
- grad_attend_gain: float32 [1024], P('wide')
- grad_attend_weight: float32 [1024, 3072], P('wide')
- grad_output_weight: float32 [1024, 1024], P('wide')
- grad_mixer_gain: float32 [1024], P('wide')
- grad_router_weight: float32 [1024, 16], P('wide')
- grad_blend_weight: float32 [1024, 2], P('wide')
- grad_up_weight: float32 [1024, 4096], P('wide')
- grad_down_weight: float32 [4096, 1024], P('wide')
- grad_expert_up: float32 [16, 1024, 4096], P('wide', None, 'narrow')
- grad_expert_down: float32 [16, 4096, 1024], P('wide', 'narrow')
- root_means: float32 [4], replicated
Inputs may be any that keep to these rules, and one draw needn't show every extreme that they name: `routes`: in each aligned block of 256 rows (the rows of one device) no expert is named by more than 24 rows, a bound that some block reaches. `doc_ids`: along each sequence of 1024 rows the ids never fall; rows of one sequence with equal ids form one document, and each id is the position of its document's last row within the sequence.
All inputs are finite; a program needn't handle non-finite values. No bound on the sum of `valid_mask` on one device may be relied on, other than what follows from the above.
Results may differ from a plain program's by a relative error of at most 0.013.
Values may be sent and summed in bfloat16 or wider, within the bound.
A program may use at most 256 MiB of HBM per device.

v0:
```python
import jax
import jax.numpy as jnp
from jax import lax
from jax.sharding import PartitionSpec as P

HEAD_DIM = 64


eps_norm = 1e-05
masked_score = -1e30
heads_block = 4
highest = lax.Precision.HIGHEST


def layer_norm(values, gain_vec):
    center = values - jnp.mean(values, axis=-1, keepdims=True)
    spread = jnp.mean(center * center, axis=-1, keepdims=True)
    return center * lax.rsqrt(spread + eps_norm) * gain_vec


def smooth_gelu(values):
    tanh_input = 0.7978845608028654 * (values + 0.044715 * values * values * values)
    return 0.5 * values * (1.0 + jnp.tanh(tanh_input))


def gelu_back(values, grad_in):
    return jax.vjp(smooth_gelu, values)[1](grad_in)[0]


def soft_max(logits):
    row_max = jnp.max(logits, axis=-1, keepdims=True)
    exp_shift = jnp.exp(logits - row_max)
    return exp_shift / jnp.sum(exp_shift, axis=-1, keepdims=True)


def soft_max_back(prob_rows, grad_in):
    return prob_rows * (grad_in - jnp.sum(prob_rows * grad_in, axis=-1, keepdims=True))


def owner_send(packed):
    return lax.all_to_all(packed, "wide", split_axis=1, concat_axis=1, tiled=True)


def group_gather(packed):
    return lax.all_gather(packed, "narrow", axis=0, tiled=True)


def owner_return(partial_value):
    return lax.all_to_all(partial_value, "wide", split_axis=1, concat_axis=1, tiled=True)


def group_sum(partial_value):
    return lax.psum_scatter(partial_value, "narrow", scatter_dimension=0, tiled=True)


def per_device(
    tokens,
    doc_ids,
    valid_mask,
    routes,
    cotangent,
    attend_gain,
    attend_weight,
    output_weight,
    mixer_gain,
    router_weight,
    blend_weight,
    up_weight,
    down_weight,
    expert_up,
    expert_down,
):
    row_count = tokens.shape[0]
    model_width = tokens.shape[1]
    narrow_count = lax.axis_size("narrow")
    wide_count = lax.axis_size("wide")
    narrow_index = lax.axis_index("narrow")
    local_experts = expert_up.shape[0]
    expert_count = local_experts * wide_count
    capacity = max(2, (3 * row_count + 2 * expert_count - 1) // (2 * expert_count))
    seq_len = row_count * narrow_count
    group_count = model_width // HEAD_DIM // heads_block
    block_cols = heads_block * HEAD_DIM
    score_scale = HEAD_DIM ** (-0.5)
    dense_shards = (
        attend_gain,
        attend_weight,
        output_weight,
        mixer_gain,
        router_weight,
        blend_weight,
        up_weight,
        down_weight,
    )
    dense_full = (
        lax.all_gather(dense_shards[0], "wide", axis=0, tiled=True),
        lax.all_gather(dense_shards[1], "wide", axis=0, tiled=True),
        lax.all_gather(dense_shards[2], "wide", axis=0, tiled=True),
        lax.all_gather(dense_shards[3], "wide", axis=0, tiled=True),
        lax.all_gather(dense_shards[4], "wide", axis=0, tiled=True),
        lax.all_gather(dense_shards[5], "wide", axis=0, tiled=True),
        lax.all_gather(dense_shards[6], "wide", axis=0, tiled=True),
        lax.all_gather(dense_shards[7], "wide", axis=0, tiled=True),
    )
    (
        full_attend_gain,
        full_attend,
        full_output,
        full_mixer_gain,
        full_router,
        full_blend,
        full_up,
        full_down,
    ) = dense_full
    inputs = tokens.astype(jnp.float32)
    normed_attend = layer_norm(inputs, full_attend_gain.astype(jnp.float32))
    normed_attend_low = normed_attend.astype(jnp.bfloat16)
    projected = jnp.dot(normed_attend_low, full_attend, preferred_element_type=jnp.float32).astype(
        jnp.bfloat16
    )
    queries = projected[:, :model_width]
    keys_local = projected[:, model_width : 2 * model_width]
    values_local = projected[:, 2 * model_width :]
    keys_all, values_all, docs_all = (
        lax.all_gather(keys_local, "narrow", axis=0, tiled=True),
        lax.all_gather(values_local, "narrow", axis=0, tiled=True),
        lax.all_gather(doc_ids, "narrow", axis=0, tiled=True),
    )
    query_pos = narrow_index * row_count + jnp.arange(row_count, dtype=jnp.int32)
    key_pos = jnp.arange(seq_len, dtype=jnp.int32)
    allowed = (key_pos[None, :] <= query_pos[:, None]) & (docs_all[None, :] == doc_ids[:, None])

    def block_slice(matrix, group_index):
        picked = lax.dynamic_slice_in_dim(matrix, group_index * block_cols, block_cols, 1)
        return picked.reshape(matrix.shape[0], heads_block, HEAD_DIM)

    def block_scores(group_index):
        scores = (
            jnp.einsum(
                "thd,shd->hts",
                block_slice(queries, group_index),
                block_slice(keys_all, group_index),
                preferred_element_type=jnp.float32,
            )
            * score_scale
        )
        return jnp.where(allowed[None], scores, masked_score)

    def forward_block(group_index):
        scores = block_scores(group_index)
        row_max = jnp.max(scores, axis=2, keepdims=True)
        exp_shift = jnp.exp(scores - row_max)
        exp_total = jnp.sum(exp_shift, axis=2, keepdims=True)
        prob_low = (exp_shift / exp_total).astype(jnp.bfloat16)
        block_out = jnp.einsum(
            "hts,shd->thd",
            prob_low,
            block_slice(values_all, group_index),
            preferred_element_type=jnp.float32,
        )
        return (block_out.reshape(row_count, block_cols), row_max + jnp.log(exp_total))

    mixed_blocks, log_totals = lax.map(forward_block, jnp.arange(group_count))
    attn_low = jnp.moveaxis(mixed_blocks, 0, 1).reshape(row_count, model_width).astype(jnp.bfloat16)
    attention_out = jnp.dot(attn_low, full_output, preferred_element_type=jnp.float32)
    residual_mid = inputs + attention_out
    normed_mix = layer_norm(residual_mid, full_mixer_gain.astype(jnp.float32))
    normed_mix_low = normed_mix.astype(jnp.bfloat16)
    router_probs = soft_max(
        jnp.dot(normed_mix_low, full_router, preferred_element_type=jnp.float32)
    )
    route_col = routes[:, 0]
    route_hits = (route_col[:, None] == jnp.arange(expert_count, dtype=jnp.int32)[None, :]).astype(
        jnp.int32
    )
    onehot = route_hits.astype(jnp.float32)
    chosen = jnp.sum(router_probs * onehot, axis=1, keepdims=True)
    blend_probs = soft_max(jnp.dot(normed_mix_low, full_blend, preferred_element_type=jnp.float32))
    up_pre = jnp.dot(normed_mix_low, full_up, preferred_element_type=jnp.float32)
    up_act = smooth_gelu(up_pre).astype(jnp.bfloat16)
    dense_out = jnp.dot(up_act, full_down, preferred_element_type=jnp.float32)
    slot_rank = jnp.sum((jnp.cumsum(route_hits, axis=0) - 1) * route_hits, axis=1)
    slot_of = route_col * capacity + slot_rank
    place_map = (
        slot_of[None, :] == jnp.arange(expert_count * capacity, dtype=jnp.int32)[:, None]
    ).astype(jnp.bfloat16)
    place_float = place_map.astype(jnp.float32)

    def dispatch(token_rows):
        packed = jnp.dot(place_map, token_rows, preferred_element_type=jnp.float32).astype(
            jnp.bfloat16
        )
        packed = packed.reshape(1, wide_count, local_experts, capacity, model_width)
        return owner_send(group_gather(packed))

    def combine(partial_value):
        summed = group_sum(owner_return(partial_value))
        flat = summed.reshape(expert_count * capacity, model_width)
        return jnp.einsum("sr,sd->rd", place_float, flat, precision=highest)

    received = dispatch(normed_mix_low)
    expert_hidden = jnp.einsum(
        "nwecd,edf->nwecf", received, expert_up, preferred_element_type=jnp.float32
    )
    expert_act = smooth_gelu(expert_hidden).astype(jnp.bfloat16)
    expert_partial = jnp.einsum(
        "nwecf,efd->nwecd", expert_act, expert_down, preferred_element_type=jnp.float32
    )
    expert_tok = combine(expert_partial)
    ffn_out = blend_probs[:, 0:1] * chosen * expert_tok + blend_probs[:, 1:2] * dense_out
    layer_full = residual_mid + ffn_out
    layer_out = layer_full.astype(jnp.bfloat16)
    valid_rows = valid_mask.astype(jnp.float32)[:, None]
    square_sums = jnp.stack(
        [
            jnp.sum(valid_rows * branch_value * branch_value)
            for branch_value in (residual_mid, layer_full, attention_out, ffn_out)
        ]
    )
    square_sums, valid_count = lax.psum((square_sums, jnp.sum(valid_rows)), ("wide", "narrow"))
    root_means = jnp.sqrt(square_sums / (jnp.maximum(valid_count, 1.0) * model_width))
    dense_back = (
        lax.all_gather(dense_shards[0], "wide", axis=0, tiled=True),
        lax.all_gather(dense_shards[1], "wide", axis=0, tiled=True),
        lax.all_gather(dense_shards[2], "wide", axis=0, tiled=True),
        lax.all_gather(dense_shards[3], "wide", axis=0, tiled=True),
        lax.all_gather(dense_shards[4], "wide", axis=0, tiled=True),
        lax.all_gather(dense_shards[5], "wide", axis=0, tiled=True),
        lax.all_gather(dense_shards[6], "wide", axis=0, tiled=True),
        lax.all_gather(dense_shards[7], "wide", axis=0, tiled=True),
    )
    (
        back_attend_gain,
        back_attend,
        back_output,
        back_mixer_gain,
        back_router,
        back_blend,
        back_up,
        back_down,
    ) = dense_back
    grad_layer = cotangent.astype(jnp.float32) * valid_rows
    expert_dot = jnp.sum(grad_layer * expert_tok, axis=1, keepdims=True)
    grad_tok_expert = (blend_probs[:, 0:1] * chosen * grad_layer).astype(jnp.bfloat16)
    grad_dense = (blend_probs[:, 1:2] * grad_layer).astype(jnp.bfloat16)
    grad_chosen = blend_probs[:, 0:1] * expert_dot
    grad_blend_probs = jnp.concatenate(
        [chosen * expert_dot, jnp.sum(grad_layer * dense_out, axis=1, keepdims=True)], axis=1
    )
    grad_router_logits = soft_max_back(router_probs, onehot * grad_chosen)
    grad_blend_logits = soft_max_back(blend_probs, grad_blend_probs)
    normed_mix_float = normed_mix_low.astype(jnp.float32)
    grad_router = jnp.einsum("td,te->de", normed_mix_float, grad_router_logits, precision=highest)
    grad_blend = jnp.einsum("td,te->de", normed_mix_float, grad_blend_logits, precision=highest)
    grad_up_act = jnp.einsum("td,fd->tf", grad_dense, back_down, preferred_element_type=jnp.float32)
    grad_down = jnp.einsum("tf,td->fd", up_act, grad_dense, preferred_element_type=jnp.float32)
    grad_up_pre = gelu_back(up_pre, grad_up_act).astype(jnp.bfloat16)
    grad_up = jnp.einsum(
        "td,tf->df", normed_mix_low, grad_up_pre, preferred_element_type=jnp.float32
    )
    grad_from_up = jnp.einsum("tf,df->td", grad_up_pre, back_up, preferred_element_type=jnp.float32)
    grad_received = dispatch(grad_tok_expert)
    grad_expert_act = jnp.einsum(
        "nwecd,efd->nwecf", grad_received, expert_down, preferred_element_type=jnp.float32
    )
    grad_expert_down = jnp.einsum(
        "nwecf,nwecd->efd", expert_act, grad_received, preferred_element_type=jnp.float32
    )
    grad_expert_hidden = gelu_back(expert_hidden, grad_expert_act).astype(jnp.bfloat16)
    grad_expert_up = jnp.einsum(
        "nwecd,nwecf->edf", received, grad_expert_hidden, preferred_element_type=jnp.float32
    )
    grad_expert_rows = combine(
        jnp.einsum(
            "nwecf,edf->nwecd", grad_expert_hidden, expert_up, preferred_element_type=jnp.float32
        )
    )
    grad_normed_mix = grad_from_up
    grad_normed_mix = grad_normed_mix + jnp.einsum(
        "te,de->td", grad_router_logits, back_router.astype(jnp.float32), precision=highest
    )
    grad_normed_mix = grad_normed_mix + jnp.einsum(
        "te,de->td", grad_blend_logits, back_blend.astype(jnp.float32), precision=highest
    )
    grad_normed_mix = grad_normed_mix + grad_expert_rows
    grad_mid_norm, grad_mixer_gain = jax.vjp(
        layer_norm, residual_mid, back_mixer_gain.astype(jnp.float32)
    )[1](grad_normed_mix)
    grad_mid = grad_layer + grad_mid_norm
    grad_attn_low = grad_mid.astype(jnp.bfloat16)
    grad_output = jnp.einsum(
        "td,te->de", attn_low, grad_attn_low, preferred_element_type=jnp.float32
    )
    grad_mixed_low = jnp.einsum(
        "te,de->td", grad_attn_low, back_output, preferred_element_type=jnp.float32
    ).astype(jnp.bfloat16)

    def backward_block(pieces):
        group_index, log_total = pieces
        scores = block_scores(group_index)
        prob_rows = jnp.exp(scores - log_total)
        grad_block = block_slice(grad_mixed_low, group_index)
        grad_probs = jnp.einsum(
            "thd,shd->hts",
            grad_block,
            block_slice(values_all, group_index),
            preferred_element_type=jnp.float32,
        )
        row_sums = jnp.sum(prob_rows * grad_probs, axis=2, keepdims=True)
        grad_scores = (prob_rows * (grad_probs - row_sums)).astype(jnp.bfloat16)
        grad_query = (
            jnp.einsum(
                "hts,shd->thd",
                grad_scores,
                block_slice(keys_all, group_index),
                preferred_element_type=jnp.float32,
            )
            * score_scale
        )
        grad_key = (
            jnp.einsum(
                "hts,thd->shd",
                grad_scores,
                block_slice(queries, group_index),
                preferred_element_type=jnp.float32,
            )
            * score_scale
        )
        grad_value = jnp.einsum(
            "hts,thd->shd",
            prob_rows.astype(jnp.bfloat16),
            grad_block,
            preferred_element_type=jnp.float32,
        )
        return (
            grad_query.reshape(row_count, block_cols),
            grad_key.reshape(seq_len, block_cols),
            grad_value.reshape(seq_len, block_cols),
        )

    query_blocks, key_blocks, value_blocks = lax.map(
        backward_block, (jnp.arange(group_count), log_totals)
    )
    grad_queries = jnp.moveaxis(query_blocks, 0, 1).reshape(row_count, model_width)
    key_grads_full = jnp.moveaxis(key_blocks, 0, 1).reshape(seq_len, model_width)
    value_grads_full = jnp.moveaxis(value_blocks, 0, 1).reshape(seq_len, model_width)
    grad_keys, grad_values = (
        lax.psum_scatter(key_grads_full, "narrow", scatter_dimension=0, tiled=True),
        lax.psum_scatter(value_grads_full, "narrow", scatter_dimension=0, tiled=True),
    )
    grad_projected = jnp.concatenate([grad_queries, grad_keys, grad_values], axis=1).astype(
        jnp.bfloat16
    )
    grad_attend = jnp.einsum(
        "td,te->de", normed_attend_low, grad_projected, preferred_element_type=jnp.float32
    )
    grad_normed_attend = jnp.einsum(
        "te,de->td", grad_projected, back_attend, preferred_element_type=jnp.float32
    )
    grad_in_norm, grad_attend_gain = jax.vjp(
        layer_norm, inputs, back_attend_gain.astype(jnp.float32)
    )[1](grad_normed_attend)
    grad_tokens = (grad_mid + grad_in_norm).astype(jnp.bfloat16)
    dense_grads = (
        grad_attend_gain,
        grad_attend,
        grad_output,
        grad_mixer_gain,
        grad_router,
        grad_blend,
        grad_up,
        grad_down,
    )
    dense_grads = (
        lax.psum_scatter(dense_grads[0], "wide", scatter_dimension=0, tiled=True),
        lax.psum_scatter(dense_grads[1], "wide", scatter_dimension=0, tiled=True),
        lax.psum_scatter(dense_grads[2], "wide", scatter_dimension=0, tiled=True),
        lax.psum_scatter(dense_grads[3], "wide", scatter_dimension=0, tiled=True),
        lax.psum_scatter(dense_grads[4], "wide", scatter_dimension=0, tiled=True),
        lax.psum_scatter(dense_grads[5], "wide", scatter_dimension=0, tiled=True),
        lax.psum_scatter(dense_grads[6], "wide", scatter_dimension=0, tiled=True),
        lax.psum_scatter(dense_grads[7], "wide", scatter_dimension=0, tiled=True),
    )
    dense_grads = lax.psum(
        (
            dense_grads[0],
            dense_grads[1],
            dense_grads[2],
            dense_grads[3],
            dense_grads[4],
            dense_grads[5],
            dense_grads[6],
            dense_grads[7],
        ),
        "narrow",
    )
    return (
        layer_out,
        grad_tokens,
        dense_grads[0],
        dense_grads[1],
        dense_grads[2],
        dense_grads[3],
        dense_grads[4],
        dense_grads[5],
        dense_grads[6],
        dense_grads[7],
        grad_expert_up,
        grad_expert_down,
        root_means,
    )


def solution(mesh):
    return jax.shard_map(
        per_device,
        mesh=mesh,
        in_specs=(
            P(("wide", "narrow"), None),
            P(("wide", "narrow")),
            P(("wide", "narrow")),
            P(("wide", "narrow"), None),
            P(("wide", "narrow"), None),
            P("wide"),
            P("wide", None),
            P("wide", None),
            P("wide"),
            P("wide", None),
            P("wide", None),
            P("wide", None),
            P("wide", None),
            P("wide", None, "narrow"),
            P("wide", "narrow", None),
        ),
        out_specs=(
            P(("wide", "narrow"), None),
            P(("wide", "narrow"), None),
            P("wide"),
            P("wide", None),
            P("wide", None),
            P("wide"),
            P("wide", None),
            P("wide", None),
            P("wide", None),
            P("wide", None),
            P("wide", None, "narrow"),
            P("wide", "narrow", None),
            P(),
        ),
        check_vma=False,
    )
```

profile of v0, /device:TPU:0, one launch (start us, length us, event | category | flops | bytes accessed | tf_op | source)
XLA Modules:
  0.0 2511.1 jit_solution(10794463142647167771)
XLA Ops:
  8.0 22.5 all-gather
  33.0 78.9 %all-gather.12.cloned.1.call-done = bf16[1024,3072]{1,0:T(8,128)(2,1)} async-done(((bf16[128,3072]{1,0:T(8,128)(2,1)}), bf16[1024,3072]{1,0:T(8,128)(2,1)}) %all-gather.12.cloned.1.call-update) | async-done | bytes 6291472 | tf_op jit(solution)/shard_map/all_gather | solution.py:97
  112.0 4.9 convolution_convert_fusion
  119.4 5.1 all-gather.1
  124.5 17.6 all-gather.2
  144.0 2.9 copy.50
  146.8 16.8 all-gather.16.cloned.1.call-done
  163.7 3.9 copy.52
  167.7 29.8 %while.28 = (s32[]{:T(128)}, bf16[4,256,256]{1,2,0:T(8,128)(2,1)S(1)}, f32[4,4,256,1]{2,1,3,0:T(4,128)S(1)}, s32[4]{0:T(128)S(1)}, bf16[1024,1024]{0,1:T(8,128)(...) while((s32[]{:T(128)}, ...), condition=%wide.region_5.6_spmd.clone, body=%wide.region_2.5_spmd.clone.sunk | while | flops 281803776 | bytes 17602776 | solution.py:163
  197.5 17.4 all-gather.18.cloned.1.call-done
  215.0 3.3 fusion.109
  220.1 27.3 %all-gather.20.cloned.1.call-done = bf16[4,8,2,24,1024]{4,3,0,2,1:T(8,128)(2,1)} async-done(((bf16[1,8,2,24,1024]{4,3,0,2,1:T(8,128)(2,1)}), bf16[4,8,2,24,1024]{4,3,0,2,1:T(8,128)(2,1)}) %all-gather.20.cloned.1.call-update) | async-done | bytes 3145744 | tf_op jit(solution)/shard_map/all_gather | solution.py:45
  247.3 5.5 all-to-all-start
  253.7 113.0 %all-to-all-done = bf16[4,8,2,24,1024]{4,3,0,2,1:T(8,128)(2,1)} async-done(((bf16[4,8,2,24,1024]{4,3,0,2,1:T(8,128)(2,1)}), bf16[4,8,2,24,1024]{4,3,0,2,1:T(8,128)(2,1)}, u32[]{:S(2)}, u32[]{:S(2)}) %all-to-all-start) | async-done | bytes 3145760 | tf_op jit(solution)/shard_map/all_to_all | solution.py:41
  366.7 10.5 multiply_convert_fusion.1
  377.2 3.5 fusion.49
  381.8 178.4 %all_to_all.20 = f32[4,8,2,24,1024]{4,3,0,2,1:T(8,128)S(1)} all-to-all(f32[4,8,2,24,1024]{4,3,0,2,1:T(8,128)S(1)} %copy.56), channel_id=1, replica_groups=mesh['wide'=8,'narrow'=4] {'wide'}, dimensions={1} | all-to-all | bytes 12582912 | tf_op jit(solution)/shard_map/all_to_all | solution.py:49
  560.2 3.3 copy.57
  565.0 18.7 all_gather.54
  583.7 26.2 %all_gather.55 = bf16[1024,16]{0,1:T(8,128)(2,1)S(1)} all-gather(bf16[128,16]{0,1:T(8,128)(2,1)S(1)} %copy-done.32), channel_id=1, replica_groups=mesh['wide'=8,'narrow'=4] {'wide'}, dimensions={0}, use_global_device_ids=true | all-gather | bytes 36864 | tf_op jit(solution)/shard_map/all_gather | solution.py:100
  610.6 7.9 fusion.114
  618.4 63.3 %all-reduce.12.cloned.1.call-done = f32[4,8,2,24,1024]{4,3,1,0,2:T(8,128)} async-done(((f32[4,8,2,24,1024]{4,3,1,0,2:T(8,128)}), f32[4,8,2,24,1024]{4,3,1,0,2:T(8,128)}) %all-reduce.12.cloned.1.call-update) | async-done | bytes 6291472
  686.3 122.7 %all-gather.24.cloned.1.call-done = bf16[4096,1024]{1,0:T(8,128)(2,1)} async-done(((bf16[512,1024]{1,0:T(8,128)(2,1)}), bf16[4096,1024]{1,0:T(8,128)(2,1)}) %all-gather.24.cloned.1.call-update) | async-done | bytes 8388624 | tf_op jit(solution)/shard_map/all_gather | solution.py:103
  809.1 8.5 multiply_reduce_fusion.3
  819.1 26.8 %all-gather.26.cloned.1.call-done = bf16[4,8,2,24,1024]{4,3,0,2,1:T(8,128)(2,1)} async-done(((bf16[1,8,2,24,1024]{4,3,0,2,1:T(8,128)(2,1)}), bf16[4,8,2,24,1024]{4,3,0,2,1:T(8,128)(2,1)}) %all-gather.26.cloned.1.call-update) | async-done | bytes 3145744 | tf_op jit(solution)/shard_map/all_gather | solution.py:45
  845.9 77.3 %all_to_all.21 = bf16[4,8,2,24,1024]{4,3,0,2,1:T(8,128)(2,1)S(1)} all-to-all(bf16[4,8,2,24,1024]{4,3,0,2,1:T(8,128)(2,1)} %all-gather.26.cloned.1.call-done), channel_id=1, replica_groups=mesh['wide'=8,'narrow'=4] {'wide'}, dimensions={1} | all-to-all | bytes 6291456 | tf_op jit(solution)/shard_map/all_to_all | solution.py:41
  924.9 9.9 fusion.21
  934.8 3.4 fusion.52
  939.4 141.5 %all_to_all.22 = f32[4,8,2,24,1024]{4,3,0,2,1:T(8,128)S(1)} all-to-all(f32[4,8,2,24,1024]{4,3,0,2,1:T(8,128)S(1)} %copy.61), channel_id=1, replica_groups=mesh['wide'=8,'narrow'=4] {'wide'}, dimensions={1} | all-to-all | bytes 12582912 | tf_op jit(solution)/shard_map/all_to_all | solution.py:49
  1080.9 3.3 copy.62
  1084.5 8.7 fusion.33
  1093.2 6.6 fusion.115
  1102.2 99.8 %all-reduce.14.cloned.1.call-done = f32[4,8,2,24,1024]{4,3,1,0,2:T(8,128)} async-done(((f32[4,8,2,24,1024]{4,3,1,0,2:T(8,128)}), f32[4,8,2,24,1024]{4,3,1,0,2:T(8,128)}) %all-reduce.14.cloned.1.call-update) | async-done | bytes 6291472
  1204.4 4.4 fusion.65
  1213.7 73.9 %while.29 = (s32[]{:T(128)}, bf16[4,256,256]{1,2,0:T(8,128)(2,1)}, f32[4,1024,256]{1,2,0:T(8,128)}, f32[4,1024,256]{1,2,0:T(8,128)}, s32[4]{0:T(128)S(1)}, /*ind...) while((s32[]{:T(128)}, bf16[4,256,256]{1,2,0:T(8,128)(2,1)}, ...), condition=%wide.region_26.27_spmd.clone, body=%wide.region_24.26_spmd.clone.sunk | while | flops 687995904 | bytes 60983576 | solution.py:341
  1217.1 2.8 fusion.197
  1222.3 4.0 multiply_reduce_fusion.10
  1235.6 2.8 fusion.197
  1240.7 4.0 multiply_reduce_fusion.10
  1254.0 2.8 fusion.197
  1259.2 4.0 multiply_reduce_fusion.10
  1272.4 2.8 fusion.197
  1277.6 4.0 multiply_reduce_fusion.10
  1289.8 2.7 fusion.116
  1292.6 10.3 fusion.117
  1303.0 10.9 fusion.100
  1314.2 18.3 reduce-scatter.19.cloned.1.call-done
  1333.8 46.4 %reduce-scatter.17.cloned.1.call-done = f32[256,1024]{0,1:T(8,128)} async-done(((f32[1024,1024]{0,1:T(8,128)}), f32[256,1024]{0,1:T(8,128)}) %reduce-scatter.17.cloned.1.call-update) | async-done | bytes 1048592 | tf_op jit(solution)/shard_map/reduce_scatter | solution.py:348
  1381.5 6.5 fusion.69
  1391.5 54.5 %reduce-scatter.31.cloned.1.call-done = f32[128,2]{1,0:T(8,128)} async-done(((f32[1024,2]{1,0:T(8,128)}), f32[128,2]{1,0:T(8,128)}) %reduce-scatter.31.cloned.1.call-update) | async-done | bytes 1040
  1446.9 9.7 convolution_bitcast_fusion.1
  1456.6 2.6 pad_maximum_fusion.4
  1459.3 78.4 %reduce-scatter.23.cloned.1.call-done = f32[128,1024]{1,0:T(8,128)} async-done(((f32[1024,1024]{1,0:T(8,128)}), f32[128,1024]{1,0:T(8,128)}) %reduce-scatter.23.cloned.1.call-update) | async-done | bytes 524304 | tf_op jit(solution)/shard_map/reduce_scatter | solution.py:377
  1537.7 285.4 %reduce-scatter.27.cloned.1.call-done = f32[128,4096]{1,0:T(8,128)} async-done(((f32[1024,4096]{1,0:T(8,128)}), f32[128,4096]{1,0:T(8,128)}) %reduce-scatter.27.cloned.1.call-update) | async-done | bytes 2097168 | tf_op jit(solution)/shard_map/reduce_scatter | solution.py:381
  1823.1 285.4 %reduce-scatter.29.cloned.1.call-done = f32[512,1024]{1,0:T(8,128)} async-done(((f32[4096,1024]{1,0:T(8,128)}), f32[512,1024]{1,0:T(8,128)}) %reduce-scatter.29.cloned.1.call-update) | async-done | bytes 2097168 | tf_op jit(solution)/shard_map/reduce_scatter | solution.py:382
  2108.5 209.8 %reduce-scatter.21.cloned.1.call-done = f32[128,3072]{1,0:T(8,128)} async-done(((f32[1024,3072]{1,0:T(8,128)}), f32[128,3072]{1,0:T(8,128)}) %reduce-scatter.21.cloned.1.call-update) | async-done | bytes 1572880 | tf_op jit(solution)/shard_map/reduce_scatter | solution.py:376
  2318.4 9.8 convolution_bitcast_fusion
  2328.1 39.8 %all-reduce.4 = (f32[4]{0:T(128)S(1)}, f32[]{:T(128)}) all-reduce(f32[4]{0:T(128)S(1)} %pad_maximum_fusion.4, f32[]{:T(128)} %convert_reduce_fusion.1), channel_id=1, replica_groups=mesh['wide'=8,'narrow'=4] {'wide','narrow'}, use_global_device_ids=true, to_apply=%region_53.54 | all-reduce | flops 5 | bytes 40 | tf_op jit(solution)/shard_map/psum | solution.py:220
  2369.1 5.0 fusion.64
  2375.7 21.4 all-reduce.5
  2397.3 12.5 all-reduce.6
  2409.8 2.5 add_convert_fusion
  2412.3 84.4 %all-reduce.16.cloned.1.call-done = (f32[128,3072]{1,0:T(8,128)}, f32[128,1024]{1,0:T(8,128)}, f32[128,4096]{1,0:T(8,128)}, f32[512,1024]{1,0:T(8,128)}) async-done(((f32[128,3072]{1,0:T(8,128)}, f32[128,1024]{1,0:T(8,128)}, f32[128,4096]{1,0:T(8,128)}, f32[512,1024]{1,0:T(8,128)}), (f32[128,3072]{1,0:T(8,128)}, f32[128,1024]{1,0:T(8,128)}, f32[128,4096]{1,0:T(8,128)}, ...) | async-done | bytes 6291472 | tf_op jit(solution)/shard_map/psum | solution.py:384
  2496.7 2.9 copy.134
  (297 shorter events, 118.4 us)
Async XLA Ops:
  7.2 104.8 %all-gather.12.cloned.1.call-start = ((), (), s32[]{:S(2)}) async-start(), calls=%async_computation.12 | async-start | bytes 7077888 | tf_op jit(solution)/shard_map/all_gather | solution.py:97
  7.9 136.1 %all-gather.14.cloned.1.call-start = ((), (), s32[]{:S(2)}) async-start(), calls=%async_computation.13 | async-start | bytes 2621440 | tf_op jit(solution)/shard_map/all_gather | solution.py:126
  30.5 81.5 %copy-start.19 = (f32[8,1,128]{2,1,0:T(1,128)}, f32[8,1,128]{2,1,0:T(1,128)S(1)}, u32[]{:S(2)}) copy-start(f32[8,1,128]{2,1,0:T(1,128)S(1)} %convert_element_type.122) | copy-start | bytes 12292
  31.7 80.3 %copy-start.22 = (f32[256]{0:T(256)}, f32[256]{0:T(256)S(1)}, u32[]{:S(2)}) copy-start(f32[256]{0:T(256)S(1)} %broadcast_multiply_fusion.1) | copy-start | bytes 3076
  33.0 78.9 %copy-start.30 = (f32[256]{0:T(256)}, f32[256]{0:T(256)S(1)}, u32[]{:S(2)}) copy-start(f32[256]{0:T(256)S(1)} %fusion.63) | copy-start | bytes 3076
  33.0 78.9 %copy-start.25 = (f32[256]{0:T(256)}, f32[256]{0:T(256)S(1)}, u32[]{:S(2)}) copy-start(f32[256]{0:T(256)S(1)} %fusion.93) | copy-start | bytes 3076
  116.8 2.5 copy-start.21
  116.9 7.6 copy-start.35
  116.9 25.2 %copy-start.24 = (s32[256,1]{0,1:T(1,128)S(1)}, s32[256,1]{0,1:T(1,128)}, u32[]{:S(2)}) copy-start(s32[256,1]{0,1:T(1,128)} %param.22) | copy-start | bytes 3076
  118.0 45.7 %all-gather.16.cloned.1.call-start = ((), (), s32[]{:S(2)}) async-start(), calls=%async_computation.14 | async-start | bytes 2621440 | tf_op jit(solution)/shard_map/all_gather | solution.py:125
  118.7 96.3 %all-gather.18.cloned.1.call-start = ((), (), s32[]{:S(2)}) async-start(), calls=%async_computation.15 | async-start | bytes 2359296 | tf_op jit(solution)/shard_map/all_gather | solution.py:98
  119.3 128.0 %all-gather.20.cloned.1.call-start = ((), (), s32[]{:S(2)}) async-start(), calls=%async_computation.16 | async-start | bytes 3932160 | tf_op jit(solution)/shard_map/all_gather | solution.py:45
  167.7 47.3 %copy-start.2 = (bf16[256,1024]{1,0:T(8,128)(2,1)S(1)}, bf16[256,1024]{1,0:T(8,128)(2,1)}, u32[]{:S(2)}) copy-start(bf16[256,1024]{1,0:T(8,128)(2,1)} %param.19) | copy-start | bytes 1572868
  197.5 17.5 copy-start.1
  197.5 179.7 %copy-start.6 = (bf16[4,256,256]{1,2,0:T(8,128)(2,1)}, bf16[4,256,256]{1,2,0:T(8,128)(2,1)S(1)}, u32[]{:S(2)}) copy-start(bf16[4,256,256]{1,2,0:T(8,128)(2,1)S(1)} %get-tuple-element.115) | copy-start | bytes 1572868
  247.3 119.3 %all-to-all-start = ((bf16[4,8,2,24,1024]{4,3,0,2,1:T(8,128)(2,1)}), bf16[4,8,2,24,1024]{4,3,0,2,1:T(8,128)(2,1)}, u32[]{:S(2)}, u32[]{:S(2)}) async-start(bf16[4,8,2,24,1024]{4,3,0,2,1:T(8,128)(2,1)} %all-gather.20.cloned.1.call-done), calls=%async_computation | async-start | bytes 6291456 | tf_op jit(solution)/shard_map/all_to_all | solution.py:41
  252.8 357.7 %all-gather.22.cloned.1.call-start = ((), (), s32[]{:S(2)}) async-start(), calls=%async_computation.17 | async-start | bytes 9437184 | tf_op jit(solution)/shard_map/all_gather | solution.py:102
  253.4 428.3 %all-reduce.12.cloned.1.call-start = ((), (), s32[]{:S(2)}) async-start(), calls=%async_computation.28 | async-start | bytes 12582912
  366.7 10.5 copy-start.37
  377.2 3.5 copy-start.42
  563.5 1.5 copy-start.36
  563.5 20.2 copy-start.32
  563.5 245.5 %all-gather.24.cloned.1.call-start = ((), (), s32[]{:S(2)}) async-start(), calls=%async_computation.18 | async-start | bytes 9437184 | tf_op jit(solution)/shard_map/all_gather | solution.py:103
  564.3 281.7 %all-gather.26.cloned.1.call-start = ((), (), s32[]{:S(2)}) async-start(), calls=%async_computation.19 | async-start | bytes 3932160 | tf_op jit(solution)/shard_map/all_gather | solution.py:45
  681.8 127.3 %copy-start.8 = (bf16[256,1024]{1,0:T(8,128)(2,1)S(1)}, bf16[256,1024]{1,0:T(8,128)(2,1)}, u32[]{:S(2)}) copy-start(bf16[256,1024]{1,0:T(8,128)(2,1)} %param.23) | copy-start | bytes 1572868
  819.0 383.0 %all-reduce.14.cloned.1.call-start = ((), (), s32[]{:S(2)}) async-start(), calls=%async_computation.29 | async-start | bytes 12582912
  845.9 79.0 %copy-start.38 = (bf16[2,1024,1024]{2,1,0:T(8,128)(2,1)S(1)}, bf16[2,1024,1024]{2,1,0:T(8,128)(2,1)}, u32[]{:S(2)}) copy-start(bf16[2,1024,1024]{2,1,0:T(8,128)(2,1)} %param.33) | copy-start | bytes 12582916
  923.2 1.7 copy-start.11
  924.9 9.9 copy-start.39
  934.8 3.5 copy-start.43
  1084.2 248.2 %reduce-scatter.19.cloned.1.call-start = ((), (), s32[]{:S(2)}) async-start(), calls=%async_computation.21 | async-start | bytes 5242880 | tf_op jit(solution)/shard_map/reduce_scatter | solution.py:349
  1093.2 6.6 copy-start.15
  1202.1 2.4 copy-start.10
  1208.9 2.4 copy-start.12
  1210.1 1.0 copy-start.4
  1210.1 3.6 copy-start.28
  1222.3 4.1 copy-start
  1240.7 4.1 copy-start
  1259.1 4.1 copy-start
  1277.6 4.1 copy-start
  1287.6 2.2 copy-start.7
  1287.6 92.5 %reduce-scatter.17.cloned.1.call-start = ((), (), s32[]{:S(2)}) async-start(), calls=%async_computation.20 | async-start | bytes 5242880 | tf_op jit(solution)/shard_map/reduce_scatter | solution.py:348
  1288.2 157.8 %reduce-scatter.31.cloned.1.call-start = ((), (), s32[]{:S(2)}) async-start(), calls=%async_computation.27 | async-start | bytes 589824
  1289.7 247.9 %reduce-scatter.23.cloned.1.call-start = ((), (), s32[]{:S(2)}) async-start(), calls=%async_computation.23 | async-start | bytes 4718592 | tf_op jit(solution)/shard_map/reduce_scatter | solution.py:377
  1292.6 530.5 %reduce-scatter.27.cloned.1.call-start = ((), (), s32[]{:S(2)}) async-start(), calls=%async_computation.25 | async-start | bytes 18874368 | tf_op jit(solution)/shard_map/reduce_scatter | solution.py:381
  1303.0 805.5 %reduce-scatter.29.cloned.1.call-start = ((), (), s32[]{:S(2)}) async-start(), calls=%async_computation.26 | async-start | bytes 18874368 | tf_op jit(solution)/shard_map/reduce_scatter | solution.py:382
  1313.9 67.5 %copy-start.3 = (bf16[256,1024]{1,0:T(8,128)(2,1)S(1)}, bf16[256,1024]{1,0:T(8,128)(2,1)}, u32[]{:S(2)}) copy-start(bf16[256,1024]{1,0:T(8,128)(2,1)} %param.19) | copy-start | bytes 1572868
  1313.9 67.6 %copy-start.18 = (bf16[4,256,256]{1,2,0:T(8,128)(2,1)S(1)}, bf16[4,256,256]{1,2,0:T(8,128)(2,1)}, u32[]{:S(2)}) copy-start(bf16[4,256,256]{1,2,0:T(8,128)(2,1)} %get-tuple-element.117) | copy-start | bytes 1572868
  1313.9 67.6 %copy-start.20 = (f32[8,1,128]{2,1,0:T(1,128)S(1)}, f32[8,1,128]{2,1,0:T(1,128)}, u32[]{:S(2)}) copy-start(f32[8,1,128]{2,1,0:T(1,128)} %copy-done.19) | copy-start | bytes 12292
  1313.9 67.6 %copy-start.23 = (f32[256]{0:T(256)S(1)}, f32[256]{0:T(256)}, u32[]{:S(2)}) copy-start(f32[256]{0:T(256)} %copy-done.22) | copy-start | bytes 3076
  1313.9 67.6 %copy-start.26 = (f32[256]{0:T(256)S(1)}, f32[256]{0:T(256)}, u32[]{:S(2)}) copy-start(f32[256]{0:T(256)} %copy-done.25) | copy-start | bytes 3076
  1313.9 1004.4 %reduce-scatter.21.cloned.1.call-start = ((), (), s32[]{:S(2)}) async-start(), calls=%async_computation.22 | async-start | bytes 14155776 | tf_op jit(solution)/shard_map/reduce_scatter | solution.py:376
  1381.4 6.6 copy-start.16
  1388.0 1.9 copy-start.34
  1388.0 1009.3 %reduce-scatter.25.cloned.1.call-start = ((), (), s32[]{:S(2)}) async-start(), calls=%async_computation.24 | async-start | bytes 73728 | tf_op jit(solution)/shard_map/reduce_scatter | solution.py:379
  1391.5 1105.2 %all-reduce.16.cloned.1.call-start = ((), (), s32[]{:S(2)}) async-start(), calls=%async_computation.30 | async-start | bytes 12582912 | tf_op jit(solution)/shard_map/psum | solution.py:384
  2318.3 50.8 %copy-start.17 = (bf16[256,1024]{0,1:T(8,128)(2,1)S(1)}, bf16[256,1024]{0,1:T(8,128)(2,1)}, u32[]{:S(2)}) copy-start(bf16[256,1024]{0,1:T(8,128)(2,1)} %copy-done.16) | copy-start | bytes 1572868
  2369.1 5.1 copy-start.31
  2369.1 6.6 copy-start.27
  2369.1 40.6 %copy-start.5 = (f32[256,1024]{1,0:T(8,128)S(1)}, f32[256,1024]{1,0:T(8,128)}, u32[]{:S(2)}) copy-start(f32[256,1024]{1,0:T(8,128)} %copy-done.4) | copy-start | bytes 3145732
  2369.1 40.6 %copy-start.29 = (f32[256]{0:T(256)S(1)}, f32[256]{0:T(256)}, u32[]{:S(2)}) copy-start(f32[256]{0:T(256)} %copy-done.28) | copy-start | bytes 3076
  2374.2 1.0 copy-start.9
  2496.7 4.7 copy-start.14
  2496.7 6.1 copy-start.13
  (3 other events, 2.4 us)
Sparse Core Ops, SparseCore 0:
  10.2 101.7 all-gather.11
  118.1 20.7 all-gather.13
  141.1 22.5 all-gather.15
  165.7 49.2 all-gather.17
  220.2 27.0 all-gather.19
  255.5 226.0 all-gather.21
  563.6 118.0 all-reduce.11
  683.9 125.1 all-gather.23
  819.2 26.7 all-gather.25
  1084.4 117.6 all-reduce.13
  1287.7 44.7 reduce-scatter.18
  1335.6 44.4 reduce-scatter.16
  1384.0 61.9 reduce-scatter.30
  1450.5 87.1 reduce-scatter.22
  1541.3 281.7 reduce-scatter.26
  1827.2 281.2 reduce-scatter.28
  2111.9 206.3 reduce-scatter.20
  2321.9 52.7 reduce-scatter.24
  2377.2 119.4 all-reduce.15
where the time goes:
time: 2520 us; the launch traced here: 2510 us
  waiting for transfers between devices  1630 us (65%)
  blocking collectives  561 us (22%)
  matrix products  186 us (7%)
  local copies, waits for them, and re-layouts  75.2 us (3%)
  other arithmetic  27.2 us (1%)
    all_to_all x2, blocking collectives, owner_return(): lax.all_to_all(partial_value, 'wide', split_axis=1, concat_axis=1, tiled=...  320 us
    reduce_scatter x1, waiting for transfers between devices, per_device(): lax.psum_scatter(dense_grads[7], 'wide', scatter_dimension=0, tiled=True)  285 us
    reduce_scatter x1, waiting for transfers between devices, per_device(): lax.psum_scatter(dense_grads[6], 'wide', scatter_dimension=0, tiled=True)  285 us
    unnamed x22, waiting for transfers between devices  221 us
    reduce_scatter x1, waiting for transfers between devices, per_device(): lax.psum_scatter(dense_grads[1], 'wide', scatter_dimension=0, tiled=True)  210 us
    all_gather x1, waiting for transfers between devices, per_device(): lax.all_gather(dense_shards[7], 'wide', axis=0, tiled=True)  123 us
    all_to_all x1, waiting for transfers between devices, owner_send(): lax.all_to_all(packed, 'wide', split_axis=1, concat_axis=1, tiled=True)  113 us
    psum x1, waiting for transfers between devices, per_device(): lax.psum((dense_grads[0], dense_grads[1], dense_grads[2], dense_grads[3],...  84.4 us
  transfers between devices with their start and end apart: 20, of which 17 were waited for; matrix products, arithmetic and copies ran while one was open for 6% of the time, Pallas kernels for 0%

commit v1 on v0

v1 whole, which is shorter than its diff:
```python
import functools

import jax
import jax.numpy as jnp
from jax import lax
from jax.experimental import pallas as pl
from jax.experimental.pallas import tpu as pltpu
from jax.sharding import PartitionSpec as P

HEAD_DIM = 64
PAIR = 2 * HEAD_DIM
Q_TILE = 256
SMALL = 128
eps_norm = 1e-05
masked_score = -1e30
f32 = jnp.float32
bf16 = jnp.bfloat16


def mm(a, b, ca=1, cb=0):
    return lax.dot_general(a, b, (((ca,), (cb,)), ((), ())), preferred_element_type=f32)


def norm_stats(values):
    center = values - jnp.mean(values, axis=-1, keepdims=True)
    scale = lax.rsqrt(jnp.mean(center * center, axis=-1, keepdims=True) + eps_norm)
    return center * scale, scale


def norm_back(normed, scale, gain, grad):
    u = grad * gain
    return scale * (
        u
        - jnp.mean(u, axis=-1, keepdims=True)
        - normed * jnp.mean(u * normed, axis=-1, keepdims=True)
    )


GELU_A = 0.7978845608028654
GELU_B = 0.044715


def gelu(v):
    return 0.5 * v * (1.0 + jnp.tanh(GELU_A * (v + GELU_B * v * v * v)))


def gelu_both(v):
    t = jnp.tanh(GELU_A * (v + GELU_B * v * v * v))
    value = 0.5 * v * (1.0 + t)
    slope = 0.5 * (1.0 + t) + 0.5 * v * (1.0 - t * t) * (GELU_A * (1.0 + 3.0 * GELU_B * v * v))
    return value, slope


def soft_max(logits):
    shifted = jnp.exp(logits - jnp.max(logits, axis=-1, keepdims=True))
    return shifted / jnp.sum(shifted, axis=-1, keepdims=True)


def head_mask(half):
    lanes = lax.broadcasted_iota(jnp.int32, (1, PAIR), 1)
    return (lanes // HEAD_DIM) == half


def attend_tile(tile, qkv_ref, doc_cols, out_ref, lse_ref, mask_ref, vt_ref):
    cols = out_ref.shape[1]
    extent = (tile + 1) * Q_TILE
    here, seen = pl.ds(tile * Q_TILE, Q_TILE), pl.ds(0, extent)
    mask_tile(tile, doc_cols, mask_ref)

    def pair_step(pair, carry):
        q_cols = pl.ds(pl.multiple_of(pair * PAIR, PAIR), PAIR)
        k_cols = pl.ds(pl.multiple_of(cols + pair * PAIR, PAIR), PAIR)
        v_cols = pl.ds(pl.multiple_of(2 * cols + pair * PAIR, PAIR), PAIR)
        if tile == 0:
            vt_ref[pair] = qkv_ref[:, v_cols].T
        queries = qkv_ref[here, q_cols] * jnp.asarray(HEAD_DIM**-0.5, bf16)
        mixed = jnp.zeros((PAIR, Q_TILE), f32)
        for half in range(2):
            one = jnp.where(head_mask(half), queries, jnp.zeros_like(queries))
            scores = mm(qkv_ref[seen, k_cols], one, 1, 1) + mask_ref[seen, :]
            top = jnp.max(scores, axis=0, keepdims=True)
            shifted = jnp.exp(scores - top)
            total = jnp.sum(shifted, axis=0, keepdims=True)
            low = (shifted * (1.0 / total)).astype(bf16)
            lse_ref[pair, pl.ds(half, 1), here] = top + jnp.log(total)
            got = mm(vt_ref[pair, :, seen], low)
            sublanes = lax.broadcasted_iota(jnp.int32, (PAIR, 1), 0)
            mixed = jnp.where((sublanes // HEAD_DIM) == half, got, mixed)
        out_ref[here, q_cols] = mixed.T.astype(bf16)
        return carry

    lax.fori_loop(0, cols // PAIR, pair_step, 0)


def mask_tile(tile, doc_cols, mask_ref):
    row = (tile * Q_TILE + lax.broadcasted_iota(jnp.int32, (Q_TILE, Q_TILE), 1)).astype(f32)
    for block in range(tile + 1):
        allowed = doc_cols[block] >= row
        if block == tile:
            key = (tile * Q_TILE + lax.broadcasted_iota(jnp.int32, (Q_TILE, Q_TILE), 0)).astype(f32)
            allowed = allowed & (key <= row)
        mask_ref[pl.ds(block * Q_TILE, Q_TILE), :] = jnp.where(allowed, 0.0, masked_score)


def attend_back_kernel(qkv_ref, doc_ref, lse_ref, grad_ref, out_ref, mask_ref, dk_ref, dv_ref):
    rows, cols = grad_ref.shape
    pairs = cols // PAIR
    dk_ref[...] = jnp.zeros_like(dk_ref)
    dv_ref[...] = jnp.zeros_like(dv_ref)
    for tile in range(rows // Q_TILE):
        extent = (tile + 1) * Q_TILE
        here = pl.ds(tile * Q_TILE, Q_TILE)
        seen = pl.ds(0, extent)
        mask_tile(tile, [doc_ref[pl.ds(b * Q_TILE, Q_TILE), :] for b in range(tile + 1)], mask_ref)

        def pair_step(pair, carry):
            q_cols = pl.ds(pl.multiple_of(pair * PAIR, PAIR), PAIR)
            k_cols = pl.ds(pl.multiple_of(cols + pair * PAIR, PAIR), PAIR)
            v_cols = pl.ds(pl.multiple_of(2 * cols + pair * PAIR, PAIR), PAIR)
            queries = qkv_ref[here, q_cols] * jnp.asarray(HEAD_DIM**-0.5, bf16)
            keys, values = qkv_ref[seen, k_cols], qkv_ref[seen, v_cols]
            grads = grad_ref[here, q_cols]
            dq = jnp.zeros((PAIR, Q_TILE), f32)
            for half in range(2):
                on = head_mask(half)
                q_one = jnp.where(on, queries, jnp.zeros_like(queries))
                g_one = jnp.where(on, grads, jnp.zeros_like(grads))
                probs = jnp.exp(mm(keys, q_one, 1, 1) + mask_ref[seen, :] - lse_ref[pair, pl.ds(half, 1), here])
                dv_ref[pair, seen, :] += mm(probs.astype(bf16), g_one)
                back = mm(values, g_one, 1, 1)
                low = (probs * (back - jnp.sum(probs * back, axis=0, keepdims=True))).astype(bf16)
                dk_ref[pair, seen, :] += mm(low, q_one)
                got = mm(keys, low, 0, 0)
                sublanes = lax.broadcasted_iota(jnp.int32, (PAIR, 1), 0)
                dq = jnp.where((sublanes // HEAD_DIM) == half, got, dq)
            out_ref[here, q_cols] = (dq.T * HEAD_DIM**-0.5).astype(bf16)
            return carry

        lax.fori_loop(0, pairs, pair_step, 0)
    for pair in range(pairs):
        out_ref[:, cols + pair * PAIR : cols + (pair + 1) * PAIR] = dk_ref[pair].astype(bf16)
        out_ref[:, 2 * cols + pair * PAIR : 2 * cols + (pair + 1) * PAIR] = dv_ref[pair].astype(bf16)


def attend_back(qkv, doc_col, lse, grad):
    rows, cols = grad.shape
    vmem = pl.BlockSpec(memory_space=pltpu.VMEM)
    return pl.pallas_call(
        attend_back_kernel,
        out_shape=jax.ShapeDtypeStruct((rows, 3 * cols), bf16),
        in_specs=[vmem] * 4,
        out_specs=vmem,
        scratch_shapes=[
            pltpu.VMEM((rows, Q_TILE), f32),
            pltpu.VMEM((cols // PAIR, rows, PAIR), f32),
            pltpu.VMEM((cols // PAIR, rows, PAIR), f32),
        ],
        compiler_params=pltpu.CompilerParams(vmem_limit_bytes=56 * 2**20),
        cost_estimate=pl.CostEstimate(flops=20 * rows * rows * cols, bytes_accessed=16 * rows * cols, transcendentals=0),
        name="attend_back",
    )(qkv, doc_col, lse, grad)


MESH = pl.DeviceIdType.MESH


class Spot:
    def __init__(self, groups, lanes):
        self.W, self.L = groups, lanes
        self.X = 1 << ((groups.bit_length() - 1) // 2)
        self.Z, self.Y = groups // self.X, lanes // 2
        self.g, self.l = lax.axis_index("wide"), lax.axis_index("narrow")
        self.z, self.x = self.g // self.X, self.g % self.X
        self.y, self.c = self.l // 2, self.l % 2

    def zx_peer(self, dz, dx):
        return lax.rem(self.z + dz, self.Z) * self.X + lax.rem(self.x + dx, self.X)

    def z_peer(self, d):
        return self.zx_peer(d, 0)

    def x_peer(self, d):
        return self.zx_peer(0, d)

    def y_peer(self, d):
        return lax.rem(self.y + d, self.Y) * 2 + self.c

    def core_peer(self):
        return self.y * 2 + 1 - self.c

    def w_peer(self, d):
        return lax.rem(self.g + d, self.W)

    def l_peer(self, d):
        return lax.rem(self.l + d, self.L)

    def greet(self, lane_peers=True):
        barrier = pltpu.get_barrier_semaphore()
        met = self.L - 1
        for d in range(1, self.L):
            pl.semaphore_signal(barrier, 1, device_id=(self.g, self.l_peer(d)), device_id_type=MESH)
        if lane_peers:
            met += self.W - 1
            for d in range(1, self.W):
                pl.semaphore_signal(barrier, 1, device_id=(self.w_peer(d), self.l), device_id_type=MESH)
        pl.semaphore_wait(barrier, met)


def remote(src, dst, send_sem, recv_sem, group, lane):
    return pltpu.make_async_remote_copy(src, dst, send_sem, recv_sem, device_id=(group, lane), device_id_type=MESH)


class LaneGather:
    def __init__(self, spot, src, place, sems):
        self.s, self.src, self.place = spot, src, place
        self.z_sem, self.x_sem, self.r_sem, self.own_sem = sems

    @staticmethod
    def sems(W, X):
        dma = pltpu.SemaphoreType.DMA
        return [dma((W // X,)), dma((W // X, X)), dma((W,)), dma((1,))]

    def z_copy(self, d):
        s = self.s
        return remote(self.src, self.place(s.g), self.z_sem.at[d], self.r_sem.at[s.g], s.z_peer(d), s.l)

    def x_copy(self, d, e):
        s = self.s
        w = s.z_peer(d)
        src = self.src if d == 0 else self.place(w)
        return remote(src, self.place(w), self.x_sem.at[d, e], self.r_sem.at[w], s.x_peer(e), s.l)

    def got(self, w):
        s = self.s
        remote(self.src, self.place(w), self.z_sem.at[0], self.r_sem.at[w], s.x_peer(1), s.l).wait_recv()

    def own(self):
        return pltpu.make_async_copy(self.src, self.place(self.s.g), self.own_sem.at[0])

    def start(self):
        for d in range(1, self.s.Z):
            self.z_copy(d).start()
        for e in range(1, self.s.X):
            self.x_copy(0, e).start()
        self.own().start()

    def forward(self):
        for d in range(1, self.s.Z):
            self.got(self.s.z_peer(d))
            for e in range(1, self.s.X):
                self.x_copy(d, e).start()

    def arrive(self):
        s = self.s
        for d in range(s.Z):
            for e in range(1, s.X):
                self.got(s.zx_peer(d, e))
        self.own().wait()

    def sent(self):
        for d in range(1, self.s.Z):
            self.z_copy(d).wait_send()
        for d in range(self.s.Z):
            for e in range(1, self.s.X):
                self.x_copy(d, e).wait_send()


class GroupGather:
    def __init__(self, spot, src, place, sems, own=True):
        self.s, self.src, self.place, self.has_own = spot, src, place, own
        self.y_sem, self.c_sem, self.r_sem, self.own_sem = sems

    @staticmethod
    def sems(L):
        dma = pltpu.SemaphoreType.DMA
        return [dma((L // 2,)), dma((L // 2,)), dma((L,)), dma((1,))]

    def y_copy(self, d):
        s = self.s
        return remote(self.src, self.place(s.l), self.y_sem.at[d], self.r_sem.at[s.l], s.g, s.y_peer(d))

    def c_copy(self, d):
        s = self.s
        l = s.y_peer(d)
        src = self.src if d == 0 else self.place(l)
        return remote(src, self.place(l), self.c_sem.at[d], self.r_sem.at[l], s.g, s.core_peer())

    def got(self, l):
        s = self.s
        remote(self.src, self.place(l), self.y_sem.at[0], self.r_sem.at[l], s.g, s.core_peer()).wait_recv()

    def own(self):
        return pltpu.make_async_copy(self.src, self.place(self.s.l), self.own_sem.at[0])

    def start(self):
        for d in range(1, self.s.Y):
            self.y_copy(d).start()
        self.c_copy(0).start()
        if self.has_own:
            self.own().start()

    def forward(self):
        for d in range(1, self.s.Y):
            self.got(self.s.y_peer(d))
            self.c_copy(d).start()

    def arrive(self):
        s = self.s
        for d in range(s.Y):
            self.got(lax.rem(s.y + d, s.Y) * 2 + 1 - s.c)
        if self.has_own:
            self.own().wait()

    def sent(self):
        for d in range(1, self.s.Y):
            self.y_copy(d).wait_send()
        for d in range(self.s.Y):
            self.c_copy(d).wait_send()


class LaneSwap:
    def __init__(self, spot, src, dst, sems):
        self.s, self.src, self.dst = spot, src, dst
        self.s_sem, self.r_sem = sems

    @staticmethod
    def sems(W):
        return [pltpu.SemaphoreType.DMA((W,)), pltpu.SemaphoreType.DMA((W,))]

    def copy(self, d):
        s = self.s
        w = s.w_peer(d)
        return remote(self.src(w), self.dst(s.g), self.s_sem.at[d], self.r_sem.at[s.g], w, s.l)

    def own(self):
        return pltpu.make_async_copy(self.src(self.s.g), self.dst(self.s.g), self.s_sem.at[0])

    def start(self):
        for d in range(1, self.s.W):
            self.copy(d).start()
        self.own().start()

    def got(self, w):
        s = self.s
        remote(self.src(w), self.dst(w), self.s_sem.at[0], self.r_sem.at[w], s.w_peer(1), s.l).wait_recv()

    def arrive(self):
        for d in range(1, self.s.W):
            self.got(self.s.w_peer(self.s.W - d))
        self.own().wait()

    def sent(self):
        for d in range(1, self.s.W):
            self.copy(d).wait_send()


class GroupSwap:
    def __init__(self, spot, src, dst, sems):
        self.s, self.src, self.dst = spot, src, dst
        self.s_sem, self.r_sem = sems

    @staticmethod
    def sems(L):
        return [pltpu.SemaphoreType.DMA((L,)), pltpu.SemaphoreType.DMA((L,))]

    def copy(self, l):
        s = self.s
        return remote(self.src(l), self.dst(s.l), self.s_sem.at[l], self.r_sem.at[s.l], s.g, l)

    def own(self):
        s = self.s
        return pltpu.make_async_copy(self.src(s.l), self.dst(s.l), self.s_sem.at[s.l])

    def send(self, l):
        @pl.when(self.s.l == l)
        def _():
            self.own().start()

        @pl.when(self.s.l != l)
        def _():
            self.copy(l).start()

    def arrive(self):
        s = self.s
        for d in range(1, s.L):
            l = s.l_peer(d)
            remote(self.src(l), self.dst(l), self.s_sem.at[l], self.r_sem.at[l], s.g, l).wait_recv()
        self.own().wait()

    def sent(self):
        for d in range(1, self.s.L):
            self.copy(self.s.l_peer(d)).wait_send()


def rows_norm(src, gain, dst, count, step=64):
    def body(i, carry):
        at = pl.ds(pl.multiple_of(i * step, step), step)
        normed, _ = norm_stats(src[at, :].astype(f32))
        dst[at, :] = (normed * gain).astype(bf16)
        return carry

    lax.fori_loop(0, count // step, body, 0)


def front_kernel(
    groups, lanes, local, cap, slots,
    tokens, cot, meta, small, attend_w, output_w, up_w, down_w,
    normed_out, qkv, lse, attn_mixed, attention_out, mix_all, small_all, meta_all, place,
    attend_all, output_all, got_mix, got_cot, cot_all, up_all, down_all,
    tok_all, attend_mine, up_mine, mixed, mask, vt, packed_mix, packed_cot, stage_sem, spread_y, spread_c, spread_r, *sems,
):
    s = Spot(groups, lanes)
    rows, width = tokens.shape
    head_cols = width // lanes
    shard = attend_w.shape[0]
    depth = down_all.shape[0] // groups
    sems = list(sems)

    def take(n):
        out = sems[:n]
        del sems[:n]
        return out

    def blocks(ref, n):
        return lambda i: ref.at[pl.ds(pl.multiple_of(i * n, n), n)]

    def cols(i):
        return pl.ds(pl.multiple_of(i * head_cols, head_cols), head_cols)

    staged = [
        pltpu.make_async_copy(
            attend_w.at[:, pl.ds(pl.multiple_of(p * width + s.l * head_cols, head_cols), head_cols)],
            attend_mine.at[:, pl.ds(p * head_cols, head_cols)], stage_sem.at[p])
        for p in range(3)
    ]
    if up_w.shape[1] != up_mine.shape[1]:
        fine = up_mine.shape[1] // groups
        staged += [
            pltpu.make_async_copy(
                up_w.at[:, pl.ds(pl.multiple_of((w * lanes + s.l) * fine, fine), fine)],
                up_mine.at[:, pl.ds(w * fine, fine)], stage_sem.at[3 + w])
            for w in range(groups)
        ]
    else:
        staged += [pltpu.make_async_copy(up_w, up_mine, stage_sem.at[3])]
    for c in staged:
        c.start()

    tok = GroupGather(s, tokens, blocks(tok_all, rows), take(4))
    met = GroupGather(s, meta, lambda l: meta_all.at[l], take(4))
    cots = GroupGather(s, cot, blocks(cot_all, rows), take(4))
    mix = GroupGather(s, blocks(mix_all, rows)(s.l), blocks(mix_all, rows), take(4), own=False)
    outs = GroupGather(s, output_all.at[:, cols(s.l)], lambda l: output_all.at[:, cols(l)], take(4), own=False)
    cot_spread = GroupGather(s, got_cot.at[s.l], lambda l: got_cot.at[l], take(4), own=False)
    att = LaneGather(s, attend_mine, blocks(attend_all, shard), take(4))
    sml = LaneGather(s, small, blocks(small_all, shard), take(4))
    out = LaneGather(s, output_w.at[:, cols(s.l)],
                     lambda w: output_all.at[pl.ds(pl.multiple_of(w * shard, shard), shard), cols(s.l)], take(4))
    up = LaneGather(s, up_mine, blocks(up_all, shard), take(4))
    down = LaneGather(s, down_w.at[pl.ds(pl.multiple_of(s.l * depth, depth), depth)], blocks(down_all, depth), take(4))
    swap = GroupSwap(s, blocks(mixed, rows), lambda l: attn_mixed.at[:, cols(l)], take(2))
    mix_swap = LaneSwap(s, blocks(packed_mix, slots), lambda w: got_mix.at[s.l, w], take(2))
    cot_swap = LaneSwap(s, blocks(packed_cot, slots), lambda w: got_cot.at[s.l, w], take(2))

    def spread(d):
        w = s.w_peer(groups - d)
        return GroupGather(s, got_mix.at[s.l, w], lambda l: got_mix.at[l, w],
                           [spread_y.at[w], spread_c.at[w], spread_r.at[w], None], own=False)

    mix_spread = [spread(d) for d in range(groups)]

    s.greet()
    for c in staged[:3]:
        c.wait()
    sml.start()
    met.start()
    tok.start()
    att.start()
    for c in staged[3:]:
        c.wait()
    mine = meta[...].T
    valid, route = mine[:, 1:2], mine[:, 2:3].astype(jnp.int32)
    column = lax.broadcasted_iota(jnp.int32, (rows, SMALL), 1)
    hits = (column == route).astype(f32)
    earlier = lax.broadcasted_iota(jnp.int32, (rows, rows), 1) < lax.broadcasted_iota(jnp.int32, (rows, rows), 0)
    rank = jnp.sum(hits * mm(earlier.astype(f32).astype(bf16), hits.astype(bf16)), axis=1, keepdims=True).astype(jnp.int32)
    slot = (route // local) * slots + (route % local) * cap + rank
    spots = (slot == lax.broadcasted_iota(jnp.int32, (rows, groups * slots), 1)).astype(f32)
    place[...] = spots.astype(bf16)
    packed_cot[...] = mm((spots * valid).astype(bf16), cot[...], 0, 0).astype(bf16)
    sml.forward()
    met.forward()
    sml.arrive()
    met.arrive()
    tok.forward()
    att.forward()
    cots.start()
    tok.arrive()
    gains = small_all[...].astype(f32).T
    rows_norm(tok_all, gains[0:1, :], normed_out, rows * lanes)
    att.arrive()
    out.start()
    up.start()

    def project(i, carry):
        at = pl.ds(pl.multiple_of(i * Q_TILE, Q_TILE), Q_TILE)
        qkv[at, :] = mm(normed_out[at, :], attend_all[...]).astype(bf16)
        return carry

    lax.fori_loop(0, rows * lanes // Q_TILE, project, 0)
    out.forward()
    doc_cols = [meta_all[l].T[:, 0:1] for l in range(lanes)]
    for tile in range(lanes):
        attend_tile(tile, qkv, doc_cols, mixed, lse, mask, vt)
        swap.send(tile)
        if tile == 0:
            out.arrive()
            outs.start()
        if tile == 1:
            cots.forward()
    outs.forward()
    up.forward()
    down.start()
    outs.arrive()
    swap.arrive()
    attention_out[...] = mm(attn_mixed[...], output_all[...])
    gain = small_all[...].astype(f32).T[1:2, :]
    base = pl.multiple_of(s.l * rows, rows)

    def mid(i, carry):
        at = pl.ds(pl.multiple_of(i * 64, 64), 64)
        normed, _ = norm_stats(tokens[at, :].astype(f32) + attention_out[at, :])
        mix_all[pl.ds(pl.multiple_of(base + i * 64, 64), 64), :] = (normed * gain).astype(bf16)
        return carry

    lax.fori_loop(0, rows // 64, mid, 0)
    mix.start()
    packed_mix[...] = mm(place[...], mix_all[pl.ds(base, rows), :], 0, 0).astype(bf16)
    mix_swap.start()
    cot_swap.start()
    down.forward()
    mix.forward()
    for d in range(groups):
        if d:
            mix_swap.got(s.w_peer(groups - d))
        else:
            mix_swap.own().wait()
        mix_spread[d].start()
    cot_swap.arrive()
    cot_spread.start()
    for task in mix_spread:
        task.forward()
    cot_spread.forward()
    mix.arrive()
    for task in mix_spread:
        task.arrive()
    cot_spread.arrive()
    cots.arrive()
    up.arrive()
    down.arrive()
    for task in [tok, met, cots, mix, outs, cot_spread, att, sml, out, up, down, swap, mix_swap, cot_swap] + mix_spread:
        task.sent()


def front(groups, lanes, local, cap, slots, tokens, cot, meta, small, attend_w, output_w, up_w, down_w):
    rows, width = tokens.shape
    X = 1 << ((groups.bit_length() - 1) // 2)
    Y = lanes // 2
    everyone = rows * lanes
    head_cols = width // lanes
    hidden = down_w.shape[0] // lanes * groups
    shard = attend_w.shape[0]
    vmem, anywhere = pl.BlockSpec(memory_space=pltpu.VMEM), pl.BlockSpec(memory_space=pl.ANY)
    dma = pltpu.SemaphoreType.DMA
    of = jax.ShapeDtypeStruct
    sems = []
    for _ in range(6):
        sems += GroupGather.sems(lanes)
    for _ in range(5):
        sems += LaneGather.sems(groups, X)
    sems += GroupSwap.sems(lanes) + LaneSwap.sems(groups) + LaneSwap.sems(groups)
    outs = [
        (of((everyone, width), bf16), vmem),
        (of((everyone, 3 * head_cols), bf16), vmem),
        (of((head_cols // PAIR, 2, everyone), f32), vmem),
        (of((rows, width), bf16), vmem),
        (of((rows, width), f32), vmem),
        (of((everyone, width), bf16), vmem),
        (of((width, SMALL), bf16), vmem),
        (of((lanes, 8, rows), f32), vmem),
        (of((rows, groups * slots), bf16), vmem),
        (of((width, 3 * head_cols), bf16), vmem),
        (of((width, width), bf16), vmem),
        (of((lanes, groups, slots, width), bf16), anywhere),
        (of((lanes, groups, slots, width), bf16), anywhere),
        (of((everyone, width), bf16), anywhere),
        (of((width, hidden), bf16), anywhere),
        (of((hidden, width), bf16), anywhere),
    ]
    return pl.pallas_call(
        functools.partial(front_kernel, groups, lanes, local, cap, slots),
        out_shape=[o for o, _ in outs],
        in_specs=[vmem] * 4 + [anywhere] * 4,
        out_specs=[p for _, p in outs],
        scratch_shapes=[
            pltpu.VMEM((everyone, width), bf16),
            pltpu.VMEM((shard, 3 * head_cols), bf16),
            pltpu.VMEM((shard, hidden), bf16),
            pltpu.VMEM((everyone, head_cols), bf16),
            pltpu.VMEM((everyone, Q_TILE), f32),
            pltpu.VMEM((head_cols // PAIR, PAIR, everyone), bf16),
            pltpu.VMEM((groups * slots, width), bf16),
            pltpu.VMEM((groups * slots, width), bf16),
            dma((3 + groups,)),
            dma((groups, Y)),
            dma((groups, Y)),
            dma((groups, lanes)),
        ] + sems,
        compiler_params=pltpu.CompilerParams(collective_id=0, has_side_effects=True, vmem_limit_bytes=56 * 2**20),
        cost_estimate=pl.CostEstimate(flops=8 * 10**9, bytes_accessed=10**8, transcendentals=0),
        name="front",
    )(tokens, cot, meta, small, attend_w, output_w, up_w, down_w)


def lane_gather(part):
    return lax.all_gather(part, "wide", axis=0, tiled=True)


def lane_scatter(part):
    return lax.psum_scatter(part.astype(bf16), "wide", scatter_dimension=0, tiled=True)


def group_gather(part, axis=0):
    return lax.all_gather(part, "narrow", axis=axis, tiled=True)


def group_scatter(part, axis=0):
    return lax.psum_scatter(part.astype(bf16), "narrow", scatter_dimension=axis, tiled=True)


def lane_swap(part):
    return lax.all_to_all(part, "wide", split_axis=0, concat_axis=0, tiled=True)


def per_device(
    tokens, doc_ids, valid_mask, routes, cotangent, attend_gain, attend_weight, output_weight, mixer_gain,
    router_weight, blend_weight, up_weight, down_weight, expert_up, expert_down,
):
    rows, width = tokens.shape
    groups, lanes = lax.axis_size("wide"), lax.axis_size("narrow")
    group, lane = lax.axis_index("wide"), lax.axis_index("narrow")
    shard = attend_gain.shape[0]
    local = expert_up.shape[0]
    experts = local * groups
    hidden = up_weight.shape[1]
    fine = hidden // groups // lanes
    cap = max(2, (3 * rows + 2 * experts - 1) // (2 * experts))
    slots = -(-local * cap // 16) * 16
    all_rows = rows * lanes

    small = jnp.concatenate(
        [attend_gain[:, None], mixer_gain[:, None], blend_weight, router_weight,
         jnp.zeros((shard, SMALL - 4 - experts), bf16)], axis=1)
    meta = jnp.stack([doc_ids, valid_mask, routes[:, 0]]).astype(f32)
    meta = jnp.pad(meta, ((0, 5), (0, 0)))
    up_mine = up_weight
    if fine % 128:
        up_mine = lax.dynamic_index_in_dim(up_weight.reshape(shard, groups, lanes, fine), lane, 2, keepdims=False)
        up_mine = up_mine.reshape(shard, groups * fine)
    (
        normed_attend, qkv, lse, attn_mixed, attention_out, mix_all, small, meta_all, place,
        attend_full, output_full, got_mix, got_cot, cot_all, up_full, down_full,
    ) = front(groups, lanes, local, cap, slots, tokens, cotangent, meta, small, attend_weight, output_weight, up_mine, down_weight)
    doc_col = meta_all[:, 0].reshape(all_rows, 1)
    valid_all = meta_all[:, 1].reshape(all_rows, 1)
    attend_gain_row = small[:, 0].astype(f32)
    mixer_gain_row = small[:, 1].astype(f32)
    mix_cols = jnp.where((jnp.arange(SMALL) < 2)[None, :], 0, small)
    residual_mid = tokens.astype(f32) + attention_out
    mid_normed, mid_scale = norm_stats(residual_mid)
    normed_mix = (mid_normed * mixer_gain_row).astype(bf16)
    route = routes[:, 0]

    def give_back(partial):
        return mm(place, lane_swap(group_scatter(partial)))

    valid = valid_mask.astype(f32)[:, None]
    grad_layer = cotangent.astype(f32) * valid

    def coefficients(mix_rows):
        logits = mm(mix_rows, mix_cols)
        columns = jnp.arange(SMALL)[None, :]
        blend = soft_max(jnp.where((columns >= 2) & (columns < 4), logits, masked_score))
        router = soft_max(jnp.where((columns >= 4) & (columns < 4 + experts), logits, masked_score))
        return columns, blend, router

    columns, blend, _ = coefficients(mix_all)
    blend_0, blend_1 = blend[:, 2:3], blend[:, 3:4]
    grad_dense = (blend_1 * (cot_all.astype(f32) * valid_all.astype(f32))).astype(bf16)
    up_act, up_slope = gelu_both(mm(mix_all, up_full))
    up_act = up_act.astype(bf16)
    dense_part = mm(up_act, down_full)
    grad_up_act = mm(grad_dense, down_full, 1, 1)
    dense_dot = jnp.sum(up_act.astype(f32) * grad_up_act, axis=1, keepdims=True)
    grad_up_pre = (up_slope * grad_up_act).astype(bf16)
    dense_logits = (jnp.where(columns == 3, 1.0, 0.0) - jnp.where(columns == 2, 1.0, 0.0)) * (blend_0 * dense_dot)
    grad_mix_part = mm(grad_up_pre, up_full, 1, 1) + mm(dense_logits.astype(bf16), mix_cols, 1, 1)
    grad_small = mm(mix_all, dense_logits.astype(bf16), 0, 0)
    grad_up = mm(mix_all, grad_up_pre, 0, 0)
    grad_down = mm(up_act, grad_dense, 0, 0)

    def by_expert(received):
        split = received.reshape(lanes * groups, slots, width)[:, : local * cap]
        return split.reshape(lanes * groups, local, cap, width).transpose(1, 0, 2, 3).reshape(local, -1, width)

    def by_slot(values):
        split = values.reshape(local, lanes * groups, cap, width).transpose(1, 0, 2, 3)
        split = split.reshape(lanes * groups, local * cap, width)
        return jnp.pad(split, ((0, 0), (0, slots - local * cap), (0, 0))).reshape(-1, width)

    mix_e, cot_e = by_expert(got_mix), by_expert(got_cot)
    tok_parts, back_parts, up_grads, down_grads = [], [], [], []
    for e in range(local):
        _, blend, router = coefficients(mix_e[e])
        own = columns == 4 + group * local + e
        chosen = jnp.sum(jnp.where(own, router, 0.0), axis=1, keepdims=True)
        scale = blend[:, 2:3] * chosen
        grad_tok = (scale * cot_e[e].astype(f32)).astype(bf16)
        act, slope = gelu_both(mm(mix_e[e], expert_up[e]))
        act = act.astype(bf16)
        tok_parts.append((mm(act, expert_down[e])))
        grad_act = mm(grad_tok, expert_down[e], 1, 1)
        dot = jnp.sum(act.astype(f32) * grad_act, axis=1, keepdims=True)
        grad_hidden = (slope * grad_act).astype(bf16)
        logits = dot * (jnp.where(own, 1.0, 0.0) - router)
        logits += dot * blend[:, 3:4] * (jnp.where(columns == 2, 1.0, 0.0) - jnp.where(columns == 3, 1.0, 0.0))
        logits = logits.astype(bf16)
        back_parts.append(mm(grad_hidden, expert_up[e], 1, 1) + mm(logits, mix_cols, 1, 1))
        grad_small += mm(mix_e[e], logits, 0, 0)
        down_grads.append(mm(act, grad_tok, 0, 0))
        up_grads.append(mm(mix_e[e], grad_hidden, 0, 0))
    grad_expert_up, grad_expert_down = jnp.stack(up_grads), jnp.stack(down_grads)
    expert_back = give_back(by_slot(jnp.stack(back_parts)))
    expert_tok = give_back(by_slot(jnp.stack(tok_parts)))

    dense_out = group_scatter(dense_part).astype(f32)
    _, blend, router = coefficients(normed_mix)
    own = columns == 4 + route[:, None]
    chosen = jnp.sum(jnp.where(own, router, 0.0), axis=1, keepdims=True)
    ffn_out = blend[:, 2:3] * chosen * expert_tok + blend[:, 3:4] * dense_out
    layer_full = residual_mid + ffn_out
    sums = jnp.stack(
        [jnp.sum(valid * v * v) for v in (residual_mid, layer_full, attention_out, ffn_out)] + [jnp.sum(valid)])

    grad_mix = group_scatter(grad_mix_part).astype(f32) + expert_back
    grad_mid = grad_layer + norm_back(mid_normed, mid_scale, mixer_gain_row, grad_mix)
    mixer_gain_grad = jnp.sum(grad_mix * mid_normed, axis=0)
    grad_attn = grad_mid.astype(bf16)
    grad_output = mm(attn_mixed, grad_attn, 0, 0)
    grad_mixed = mm(grad_attn, output_full, 1, 1).astype(bf16)
    grad_heads = lax.all_to_all(grad_mixed, "narrow", split_axis=1, concat_axis=0, tiled=True)
    grad_qkv = attend_back(qkv, doc_col, lse, grad_heads)
    grad_attend = mm(normed_attend, grad_qkv, 0, 0)
    grad_normed = group_scatter(mm(grad_qkv, attend_full, 1, 1)).astype(f32)
    in_normed, in_scale = norm_stats(tokens.astype(f32))
    grad_tokens = (grad_mid + norm_back(in_normed, in_scale, attend_gain_row, grad_normed)).astype(bf16)
    attend_gain_grad = jnp.sum(grad_normed * in_normed, axis=0)

    grad_small = jnp.where(columns == 0, attend_gain_grad[:, None], jnp.where(columns == 1, mixer_gain_grad[:, None], grad_small))
    small_out = lax.psum(lax.psum_scatter(grad_small, "wide", scatter_dimension=0, tiled=True), "narrow")
    sums = lax.psum(sums, ("wide", "narrow"))
    root_means = jnp.sqrt(sums[:4] / (jnp.maximum(sums[4], 1.0) * width))

    def widen(part, parts):
        full = group_gather(part.astype(bf16)[None])
        full = full.reshape(lanes, part.shape[0], parts, -1)
        return full.transpose(1, 2, 0, 3).reshape(part.shape[0], -1).astype(f32)

    out_attend = widen(lane_scatter(grad_attend), 3)
    out_output = widen(lane_scatter(group_scatter(grad_output, axis=1)), 1)
    out_up = widen(lane_scatter(grad_up), groups)
    out_down = group_gather(lane_scatter(grad_down).astype(bf16)).astype(f32)
    return (
        layer_full.astype(bf16), grad_tokens, small_out[:, 0], out_attend, out_output, small_out[:, 1],
        small_out[:, 4 : 4 + experts], small_out[:, 2:4], out_up, out_down, grad_expert_up, grad_expert_down, root_means,
    )


def solution(mesh):
    both = ("wide", "narrow")
    row, vec, mat = P(both, None), P("wide"), P("wide", None)
    up, down = P("wide", None, "narrow"), P("wide", "narrow", None)
    return jax.shard_map(
        per_device,
        mesh=mesh,
        in_specs=(row, P(both), P(both), row, row, vec, mat, mat, vec, mat, mat, mat, mat, up, down),
        out_specs=(row, row, vec, mat, mat, vec, mat, mat, mat, mat, up, down, P()),
        check_vma=False,
    )
```

time: 2520 us -> 858 us (0.34)
  waiting for transfers between devices: 1630 us -> 407 us
  blocking collectives: 561 us -> 54.8 us
  Pallas kernels: 0 us -> 160 us
  matrix products: 186 us -> 102 us
  local copies, waits for them, and re-layouts: 75.2 us -> 44.5 us
    reduce_scatter x7 -> x11, waiting for transfers between devices: 924 us -> 363 us  [the longest x4 218 us: lane_scatter(): lax.psum_scatter(part.astype(bf16), 'wide', scatter_dimension=0, tiled=True)]
    all_to_all x3 -> x0, blocking collectives: 397 us -> none  [the longest x2 320 us: owner_return(): lax.all_to_all(partial_value, 'wide', split_axis=1, concat_axis=1, tiled=...]
    all_gather x8 -> x2, waiting for transfers between devices: 290 us -> 0.01 us  [group_gather(): return lax.all_gather(part, 'narrow', axis=axis, tiled=True)]
    unnamed x22 -> x14, waiting for transfers between devices: 221 us -> 0.23 us
    pallas_call x0 -> x2, Pallas kernels: none -> 160 us  [the longest x1 144 us: front(): pl.pallas_call(functools.partial(front_kernel, groups, lanes, local, cap,...]
    all_to_all x1 -> x3, waiting for transfers between devices: 113 us -> 12.1 us  [the longest x1 12.1 us: per_device(): lax.all_to_all(grad_mixed, 'narrow', split_axis=1, concat_axis=0, tiled=T...]
    dot_general x55 -> x34, matrix products: 184 us -> 102 us  [mm(): lax.dot_general(a, b, (((ca,), (cb,)), ((), ())), preferred_element_type=...]
    all_gather x5 -> x2, blocking collectives: 90.1 us -> 15.4 us  [group_gather(): return lax.all_gather(part, 'narrow', axis=axis, tiled=True)]
  transfers between devices with their start and end apart: 20 -> 17, of which waited for: 17 -> 10; matrix products, arithmetic and copies ran while one was open for 6% -> 16% of each run, Pallas kernels for 0% -> 2%
where the time goes in v1:
time: 858 us; the launch traced here: 852 us
  waiting for transfers between devices  407 us (47%)
  Pallas kernels  160 us (19%)
  matrix products  102 us (12%)
  blocking collectives  54.8 us (6%)
  local copies, waits for them, and re-layouts  44.5 us (5%)
  other arithmetic  43.8 us (5%)
  starting transfers between devices  23.6 us (3%)
  between operations  16.1 us (2%)
    reduce_scatter x4, waiting for transfers between devices, lane_scatter(): lax.psum_scatter(part.astype(bf16), 'wide', scatter_dimension=0, tiled=True)  218 us
    pallas_call x1, Pallas kernels, front(): pl.pallas_call(functools.partial(front_kernel, groups, lanes, local, cap,...  144 us
    dot_general x34, matrix products, mm(): lax.dot_general(a, b, (((ca,), (cb,)), ((), ())), preferred_element_type=...  102 us
    reduce_scatter x6, waiting for transfers between devices, group_scatter(): lax.psum_scatter(part.astype(bf16), 'narrow', scatter_dimension=axis, til...  86.1 us
    reduce_scatter x1, waiting for transfers between devices, per_device(): lax.psum_scatter(grad_small, 'wide', scatter_dimension=0, tiled=True)  58.9 us
    psum x1, blocking collectives, per_device(): sums = lax.psum(sums, ('wide', 'narrow'))  39.4 us
    psum x1, waiting for transfers between devices, per_device(): lax.psum(lax.psum_scatter(grad_small, 'wide', scatter_dimension=0, tiled=...  31.1 us
    all_to_all x2, starting transfers between devices, lane_swap(): return lax.all_to_all(part, 'wide', split_axis=0, concat_axis=0, tiled=True)  17.7 us
  transfers between devices with their start and end apart: 17, of which 10 were waited for; matrix products, arithmetic and copies ran while one was open for 16% of the time, Pallas kernels for 2%

profile of v1, /device:TPU:0, one launch (start us, length us, event | category | flops | bytes accessed | tf_op | source)
XLA Modules:
  0.0 851.6 jit_solution(12811409528161947451)
XLA Ops:
  13.6 144.0 %front.1 = (bf16[1024,1024]{1,0:T(8,128)(2,1)}, bf16[1024,768]{1,0:T(8,128)(2,1)}, f32[2,2,1024]{2,1,0:T(2,128)}, bf16[256,1024]{1,0:T(8,128)(2,1)}, f32[256,102...) custom-call(bf16[256,1024]{1,0:T(8,128)(2,1)} %tokens.1, ...), custom_call_target="tpu_custom_call" | custom-call | flops 8000000000 | bytes 100000000 | tf_op jit(solution)/shard_map/front/pallas_call | solution.py:600
  157.6 2.4 fusion.123
  160.7 3.5 fusion.32
  164.2 3.5 fusion.40
  173.7 1.6 copy-done.68
  175.3 6.4 multiply_reduce_fusion.1
  181.7 1.8 fusion.30
  184.3 5.1 multiply_reduce_fusion.2
  190.6 1.8 fusion.38
  194.9 2.0 pad_maximum_fusion.2
  197.0 4.0 fusion.56
  201.0 1.8 fusion.59
  203.2 2.1 copy.56
  210.1 2.4 fusion.126
  212.6 5.6 multiply_reduce_fusion
  219.6 3.7 convolution_convert_fusion.1
  224.2 4.6 fusion.127
  228.8 2.1 add_convert_fusion
  231.2 6.9 convolution_convert_fusion.3
  238.2 7.2 convolution_convert_fusion
  246.0 12.2 %all-to-all-start.1 = ((bf16[8,48,1024]{2,1,0:T(8,128)(2,1)}), bf16[8,48,1024]{2,1,0:T(8,128)(2,1)}, u32[]{:S(2)}, u32[]{:S(2)}) async-start(bf16[8,48,1024]{2,1,0:T(8,128)(2,1)} %bitcast.194), calls=%async_computation.5 | async-start | bytes 1572864 | tf_op jit(solution)/shard_map/all_to_all | solution.py:642
  258.7 2.9 fusion.122
  263.1 19.9 %reduce-scatter.12.cloned.1.call-done = bf16[384,1024]{1,0:T(8,128)(2,1)} async-done(((bf16[1536,1024]{1,0:T(8,128)(2,1)}), bf16[384,1024]{1,0:T(8,128)(2,1)}) %reduce-scatter.12.cloned.1.call-update) | async-done | bytes 786448 | tf_op jit(solution)/shard_map/reduce_scatter | solution.py:638
  283.0 5.5 all-to-all-start
  288.6 1.6 select_reduce_fusion.7
  291.3 71.1 %reduce-scatter.30.cloned.1.call-done = bf16[128,1024]{1,0:T(8,128)(2,1)} async-done(((bf16[1024,1024]{1,0:T(8,128)(2,1)}), bf16[128,1024]{1,0:T(8,128)(2,1)}) %reduce-scatter.30.cloned.1.call-update) | async-done | bytes 262160 | tf_op jit(solution)/shard_map/reduce_scatter | solution.py:630
  362.4 33.4 %reduce-scatter.16.cloned.1.call-done = bf16[256,1024]{1,0:T(8,128)(2,1)} async-done(((bf16[1024,1024]{1,0:T(8,128)(2,1)}), bf16[256,1024]{1,0:T(8,128)(2,1)}) %reduce-scatter.16.cloned.1.call-update) | async-done | bytes 524304 | tf_op jit(solution)/shard_map/reduce_scatter | solution.py:638
  395.8 1.8 convolution_add_fusion
  397.6 32.8 %reduce-scatter.14.cloned.1.call-done = bf16[256,1024]{1,0:T(8,128)(2,1)} async-done(((bf16[1024,1024]{1,0:T(8,128)(2,1)}), bf16[256,1024]{1,0:T(8,128)(2,1)}) %reduce-scatter.14.cloned.1.call-update) | async-done | bytes 524304 | tf_op jit(solution)/shard_map/reduce_scatter | solution.py:638
  430.4 4.6 fusion.81
  435.0 2.0 multiply_add_fusion.3
  437.0 2.1 convolution_convert_fusion.2
  439.2 62.1 %reduce-scatter.32.cloned.1.call-done = bf16[128,1024]{1,0:T(8,128)(2,1)} async-done(((bf16[1024,1024]{1,0:T(8,128)(2,1)}), bf16[128,1024]{1,0:T(8,128)(2,1)}) %reduce-scatter.32.cloned.1.call-update) | async-done | bytes 262160 | tf_op jit(solution)/shard_map/reduce_scatter | solution.py:630
  501.3 2.3 convolution_convert_fusion.6
  504.5 4.1 all-to-all-start.2
  509.1 1.7 copy.60.doc_ref
  510.8 12.1 %all-to-all-done.2 = bf16[256,4,256]{2,0,1:T(8,128)(2,1)} async-done(((bf16[256,4,256]{2,0,1:T(8,128)(2,1)}), bf16[256,4,256]{2,0,1:T(8,128)(2,1)}, u32[]{:S(2)}, u32[]{:S(2)}) %all-to-all-start.2) | async-done | bytes 524320 | tf_op jit(solution)/shard_map/all_to_all | solution.py:761
  522.9 16.4 %attend_back.1 = bf16[1024,768]{1,0:T(8,128)(2,1)} custom-call(bf16[1024,768]{1,0:T(8,128)(2,1)} %get-tuple-element.39.qkv_ref, f32[1024,1]{1,0:T(8,128)} %copy.60.doc_ref, f32[2,2,1024]{2,1,0:T(2,128)} %get-tuple-element.40.lse_ref, bf16[1024,256]{1,0:T(8,128)(2,1)} %bitcast.47.grad_ref), custom_call_target="tpu_custom_call" | custom-call | flops 5368709120 | bytes 4194304 | tf_op jit(solution)/shard_map/attend_back/pallas_call | solution.py:148
  539.3 4.5 convolution_convert_fusion.4
  545.9 1.8 fusion.88
  549.3 3.9 convolution_bitcast_fusion.2
  553.2 3.8 convolution_bitcast_fusion.3
  557.0 3.1 convolution_convert_fusion.5
  561.0 8.7 %pad_maximum_fusion = f32[2,1024,1024]{2,1,0:T(8,128)} fusion(f32[1,1024,1024]{2,1,0:T(8,128)} %convolution_bitcast_fusion.2, f32[1,1024,1024]{2,1,0:T(8,128)} %convolution_bitcast_fusion.3), kind=kLoop, calls=%fused_computation | loop fusion | flops 2097152 | bytes 16777216 | tf_op jit(solution)/shard_map/stack | solution.py:742
  572.0 1.9 convolution_bitcast_fusion
  574.0 1.9 convolution_bitcast_fusion.1
  575.8 4.2 pad_maximum_fusion.1
  583.6 1.9 reshape.269
  585.5 3.9 stack.77
  589.4 2.8 convert_element_type.271
  592.2 39.4 %psum.15 = f32[5]{0:T(128)} all-reduce(f32[5]{0:T(128)} %stack.77), channel_id=1, replica_groups=mesh['wide'=8,'narrow'=4] {'wide','narrow'}, use_global_device_ids=true, to_apply=%region_47.48 | all-reduce | flops 5 | bytes 40 | tf_op jit(solution)/shard_map/psum | solution.py:771
  634.7 2.2 fusion.77
  636.9 2.8 fusion.70
  639.7 38.8 %reduce-scatter.24.cloned.1.call-done = bf16[128,768]{1,0:T(8,128)(2,1)} async-done(((bf16[1024,768]{1,0:T(8,128)(2,1)}), bf16[128,768]{1,0:T(8,128)(2,1)}) %reduce-scatter.24.cloned.1.call-update) | async-done | bytes 196624 | tf_op jit(solution)/shard_map/reduce_scatter | solution.py:630
  678.5 9.4 %all-gather = bf16[512,768]{1,0:T(8,128)(2,1)} all-gather(bf16[128,768]{1,0:T(8,128)(2,1)} %reduce-scatter.24.cloned.1.call-done), channel_id=2, replica_groups=mesh['wide'=8,'narrow'=4] {'narrow'}, dimensions={0}, use_global_device_ids=true | all-gather | bytes 983040 | tf_op jit(solution)/shard_map/all_gather | solution.py:634
  689.3 1.6 reshape.272
  691.0 1.6 copy.62
  692.6 1.6 copy.65
  694.2 2.3 fusion.74
  696.5 46.4 %reduce-scatter.28.cloned.1.call-done = bf16[128,256]{1,0:T(8,128)(2,1)} async-done(((bf16[1024,256]{1,0:T(8,128)(2,1)}), bf16[128,256]{1,0:T(8,128)(2,1)}) %reduce-scatter.28.cloned.1.call-update) | async-done | bytes 65552 | tf_op jit(solution)/shard_map/reduce_scatter | solution.py:630
  742.9 6.0 all-gather.1
  748.9 58.9 %reduce-scatter.22.cloned.1.call-done = f32[128,128]{1,0:T(8,128)} async-done(((f32[1024,128]{1,0:T(8,128)}), f32[128,128]{1,0:T(8,128)}) %reduce-scatter.22.cloned.1.call-update) | async-done | bytes 65552 | tf_op jit(solution)/shard_map/reduce_scatter | solution.py:770
  809.0 31.1 %all-reduce.3.cloned.1.call-done = f32[128,128]{1,0:T(8,128)} async-done(((f32[128,128]{1,0:T(8,128)}), f32[128,128]{1,0:T(8,128)}) %all-reduce.3.cloned.1.call-update) | async-done | bytes 65552 | tf_op jit(solution)/shard_map/psum | solution.py:770
  843.3 1.6 slice_reduce_fusion
  (280 shorter events, 48.5 us)
Async XLA Ops:
  7.2 238.8 %reduce-scatter.18.cloned.1.call-start = ((), (), s32[]{:S(2)}) async-start(), calls=%async_computation.17 | async-start | bytes 3932160 | tf_op jit(solution)/shard_map/reduce_scatter | solution.py:638
  7.2 186.9 %copy-start.27 = (pred[128]{0:T(512)(128)(4,1)}, pred[128]{0:T(512)(128)(4,1)S(1)}, u32[]{:S(2)}) copy-start(pred[128]{0:T(512)(128)(4,1)S(1)} %compare_and_fusion) | copy-start | bytes 388
  7.3 161.1 %copy-start.46 = (pred[128]{0:T(512)(128)(4,1)}, pred[128]{0:T(512)(128)(4,1)S(1)}, u32[]{:S(2)}) copy-start(pred[128]{0:T(512)(128)(4,1)S(1)} %get-tuple-element.147) | copy-start | bytes 388
  7.3 163.8 %copy-start.31 = (pred[128]{0:T(512)(128)(4,1)}, pred[128]{0:T(512)(128)(4,1)S(1)}, u32[]{:S(2)}) copy-start(pred[128]{0:T(512)(128)(4,1)S(1)} %get-tuple-element.146) | copy-start | bytes 388
  160.0 7.7 copy-start.11
  160.0 8.4 copy-start.14
  164.2 3.5 copy-start.1
  168.4 4.7 copy-start.2
  175.3 6.4 copy-start.67
  181.7 11.6 %copy-start.38 = (f32[768]{0:T(1024)}, f32[768]{0:T(1024)S(1)}, u32[]{:S(2)}) copy-start(f32[768]{0:T(1024)S(1)} %get-tuple-element.118) | copy-start | bytes 9220
  184.3 9.0 %copy-start.39 = (f32[768]{0:T(1024)}, f32[768]{0:T(1024)S(1)}, u32[]{:S(2)}) copy-start(f32[768]{0:T(1024)S(1)} %fusion.108) | copy-start | bytes 9220
  189.4 4.7 copy-start.40
  196.9 86.1 %reduce-scatter.12.cloned.1.call-start = ((), (), s32[]{:S(2)}) async-start(), calls=%async_computation.14 | async-start | bytes 3932160 | tf_op jit(solution)/shard_map/reduce_scatter | solution.py:638
  197.0 4.1 copy-start.69
  197.0 4.0 copy-start.71
  205.3 157.0 %reduce-scatter.30.cloned.1.call-start = ((), (), s32[]{:S(2)}) async-start(), calls=%async_computation.24 | async-start | bytes 2359296 | tf_op jit(solution)/shard_map/reduce_scatter | solution.py:630
  205.8 4.4 copy-start.79
  212.5 5.7 copy-start.78
  223.4 172.4 %reduce-scatter.16.cloned.1.call-start = ((), (), s32[]{:S(2)}) async-start(), calls=%async_computation.16 | async-start | bytes 2621440 | tf_op jit(solution)/shard_map/reduce_scatter | solution.py:638
  223.4 5.4 copy-start.62
  224.2 4.6 copy-start.22
  230.9 199.4 %reduce-scatter.14.cloned.1.call-start = ((), (), s32[]{:S(2)}) async-start(), calls=%async_computation.15 | async-start | bytes 2621440 | tf_op jit(solution)/shard_map/reduce_scatter | solution.py:638
  238.1 7.3 copy-start.54
  238.1 263.2 %reduce-scatter.32.cloned.1.call-start = ((), (), s32[]{:S(2)}) async-start(), calls=%async_computation.25 | async-start | bytes 2359296 | tf_op jit(solution)/shard_map/reduce_scatter | solution.py:630
  245.4 13.1 %copy-start.4 = (bf16[256,1024]{1,0:T(8,128)(2,1)S(1)}, bf16[256,1024]{1,0:T(8,128)(2,1)}, u32[]{:S(2)}) copy-start(bf16[256,1024]{1,0:T(8,128)(2,1)} %tokens.1) | copy-start | bytes 1572868
  246.0 37.1 %all-to-all-start.1 = ((bf16[8,48,1024]{2,1,0:T(8,128)(2,1)}), bf16[8,48,1024]{2,1,0:T(8,128)(2,1)}, u32[]{:S(2)}, u32[]{:S(2)}) async-start(bf16[8,48,1024]{2,1,0:T(8,128)(2,1)} %bitcast.194), calls=%async_computation.5 | async-start | bytes 1572864 | tf_op jit(solution)/shard_map/all_to_all | solution.py:642
  258.2 30.4 %copy-start.28 = (pred[128]{0:T(512)(128)(4,1)S(1)}, pred[128]{0:T(512)(128)(4,1)}, u32[]{:S(2)}) copy-start(pred[128]{0:T(512)(128)(4,1)} %copy-done.27) | copy-start | bytes 388
  258.5 31.7 %copy-start.44 = (f32[1024]{0:T(1024)}, f32[1024]{0:T(1024)S(1)}, u32[]{:S(2)}) copy-start(f32[1024]{0:T(1024)S(1)} %get-tuple-element.105) | copy-start | bytes 12292
  258.7 31.6 %copy-start.33 = (f32[256]{0:T(256)}, f32[256]{0:T(256)S(1)}, u32[]{:S(2)}) copy-start(f32[256]{0:T(256)S(1)} %broadcast_multiply_fusion.2) | copy-start | bytes 3076
  258.7 31.7 %copy-start.53 = (s32[256,1]{0,1:T(1,128)S(1)}, s32[256,1]{0,1:T(1,128)}, u32[]{:S(2)}) copy-start(s32[256,1]{0,1:T(1,128)} %param.18) | copy-start | bytes 3076
  261.6 134.2 %copy-start.50 = (f32[256]{0:T(256)}, f32[256]{0:T(256)S(1)}, u32[]{:S(2)}) copy-start(f32[256]{0:T(256)S(1)} %broadcast_multiply_fusion.5) | copy-start | bytes 3076
  263.1 27.1 %copy-start.58 = (f32[256]{0:T(256)}, f32[256]{0:T(256)S(1)}, u32[]{:S(2)}) copy-start(f32[256]{0:T(256)S(1)} %add_rsqrt_fusion.1) | copy-start | bytes 3076
  283.0 147.3 %all-to-all-start = ((bf16[8,48,1024]{2,1,0:T(8,128)(2,1)}), bf16[8,48,1024]{2,1,0:T(8,128)(2,1)}, u32[]{:S(2)}, u32[]{:S(2)}) async-start(bf16[8,48,1024]{2,1,0:T(8,128)(2,1)} %bitcast.193), calls=%async_computation.1 | async-start | bytes 1572864 | tf_op jit(solution)/shard_map/all_to_all | solution.py:642
  288.5 291.6 %all-gather.8.cloned.1.call-start = ((), (), s32[]{:S(2)}) async-start(), calls=%async_computation.27 | async-start | bytes 1310720 | tf_op jit(solution)/shard_map/all_gather | solution.py:634
  362.3 219.7 %reduce-scatter.26.cloned.1.call-start = ((), (), s32[]{:S(2)}) async-start(), calls=%async_computation.22 | async-start | bytes 2621440 | tf_op jit(solution)/shard_map/reduce_scatter | solution.py:638
  397.6 37.4 %copy-start.13 = (f32[256,1024]{1,0:T(8,128)}, f32[256,1024]{1,0:T(8,128)S(1)}, u32[]{:S(2)}) copy-start(f32[256,1024]{1,0:T(8,128)S(1)} %convolution_add_fusion) | copy-start | bytes 3145732
  430.4 4.6 copy-start.19
  430.4 4.6 copy-start.45
  430.4 4.6 copy-start.51
  430.4 4.6 copy-start.57
  430.4 4.6 copy-start.59
  439.1 150.3 %all-gather.6.cloned.1.call-start = ((), (), s32[]{:S(2)}) async-start(), calls=%async_computation.26 | async-start | bytes 1310720 | tf_op jit(solution)/shard_map/all_gather | solution.py:634
  504.5 18.4 %all-to-all-start.2 = ((bf16[256,4,256]{2,0,1:T(8,128)(2,1)}), bf16[256,4,256]{2,0,1:T(8,128)(2,1)}, u32[]{:S(2)}, u32[]{:S(2)}) async-start(bf16[256,4,256]{2,0,1:T(8,128)(2,1)} %bitcast.184), calls=%async_computation.6 | async-start | bytes 1048576 | tf_op jit(solution)/shard_map/all_to_all | solution.py:761
  508.7 126.0 %reduce-scatter.20.cloned.1.call-start = ((), (), s32[]{:S(2)}) async-start(), calls=%async_computation.18 | async-start | bytes 2621440 | tf_op jit(solution)/shard_map/reduce_scatter | solution.py:638
  522.9 16.4 %copy-start.83 = (bf16[1024,768]{1,0:T(8,128)(2,1)S(1)}, bf16[1024,768]{1,0:T(8,128)(2,1)}, u32[]{:S(2)}) copy-start(bf16[1024,768]{1,0:T(8,128)(2,1)} %get-tuple-element.42) | copy-start | bytes 4718596
  543.9 134.6 %reduce-scatter.24.cloned.1.call-start = ((), (), s32[]{:S(2)}) async-start(), calls=%async_computation.21 | async-start | bytes 1769472 | tf_op jit(solution)/shard_map/reduce_scatter | solution.py:630
  544.0 3.8 copy-start.10
  544.0 3.8 copy-start.12
  544.0 3.8 copy-start.29
  544.0 3.8 copy-start.37
  544.0 3.8 copy-start.41
  544.0 3.8 copy-start.43
  544.0 3.8 copy-start.61
  544.0 3.8 copy-start.65
  549.3 3.9 copy-start.77
  553.2 3.8 copy-start.81
  553.2 3.8 copy-start.82
  560.2 182.7 %reduce-scatter.28.cloned.1.call-start = ((), (), s32[]{:S(2)}) async-start(), calls=%async_computation.23 | async-start | bytes 589824 | tf_op jit(solution)/shard_map/reduce_scatter | solution.py:630
  561.0 8.7 %copy-start.3 = (bf16[4,8,48,1024]{3,2,1,0:T(8,128)(2,1)S(1)}, bf16[4,8,48,1024]{3,2,1,0:T(8,128)(2,1)}, u32[]{:S(2)}) copy-start(bf16[4,8,48,1024]{3,2,1,0:T(8,128)(2,1)} %get-tuple-element.38) | copy-start | bytes 9437188
  582.1 225.6 %reduce-scatter.22.cloned.1.call-start = ((), (), s32[]{:S(2)}) async-start(), calls=%async_computation.19 | async-start | bytes 589824 | tf_op jit(solution)/shard_map/reduce_scatter | solution.py:770
  585.5 49.2 %copy-start.5 = (bf16[256,1024]{1,0:T(8,128)(2,1)S(1)}, bf16[256,1024]{1,0:T(8,128)(2,1)}, u32[]{:S(2)}) copy-start(bf16[256,1024]{1,0:T(8,128)(2,1)} %tokens.1) | copy-start | bytes 1572868
  585.5 51.4 %copy-start.16 = (bf16[1,32,24,1024]{3,2,0,1:T(8,128)(2,1)S(1)}, bf16[1,32,24,1024]{3,2,0,1:T(8,128)(2,1)}, u32[]{:S(2)}) copy-start(bf16[1,32,24,1024]{3,2,0,1:T(8,128)(2,1)} %copy-done.14) | copy-start | bytes 4718596
  585.5 51.4 %copy-start.30 = (pred[128]{0:T(512)(128)(4,1)S(1)}, pred[128]{0:T(512)(128)(4,1)}, u32[]{:S(2)}) copy-start(pred[128]{0:T(512)(128)(4,1)} %copy-done.27) | copy-start | bytes 388
  639.7 200.4 %all-reduce.3.cloned.1.call-start = ((), (), s32[]{:S(2)}) async-start(), calls=%async_computation.20 | async-start | bytes 131072 | tf_op jit(solution)/shard_map/psum | solution.py:770
  (39 other events, 77.6 us)
Sparse Core Ops, SparseCore 0:
  197.0 45.2 reduce-scatter.17
  245.0 37.9 reduce-scatter.11
  286.6 75.7 reduce-scatter.29
  365.3 30.4 reduce-scatter.15
  398.9 31.4 reduce-scatter.13
  433.7 67.5 reduce-scatter.31
  502.9 21.2 all-gather.7
  527.3 29.8 reduce-scatter.25
  558.9 16.7 all-gather.5
  578.2 32.0 reduce-scatter.19
  613.7 64.7 reduce-scatter.23
  682.0 60.8 reduce-scatter.27
  746.8 60.8 reduce-scatter.21
  810.0 30.0 all-reduce.2

commit v2 on v1

--- a/solution.py
+++ b/solution.py
@@ -622,6 +622,487 @@
     )(tokens, cot, meta, small, attend_w, output_w, up_w, down_w)
 
 
+def add_rows(dst, sources, step=32):
+    def body(i, carry):
+        at = pl.ds(pl.multiple_of(i * step, step), step)
+        total = sources[0][at, :].astype(f32)
+        for ref in sources[1:]:
+            total += ref[at, :].astype(f32)
+        dst[at, :] = total.astype(dst.dtype)
+        return carry
+
+    lax.fori_loop(0, dst.shape[0] // step, body, 0)
+
+
+class GroupScatter:
+    def __init__(self, spot, part, held, from_core, from_y, sems, fine):
+        self.s, self.part, self.from_core, self.from_y, self.fine = spot, part, from_core, from_y, fine
+        self.staged = held is not None
+        self.held = (lambda d: held.at[d]) if self.staged else (lambda d: part(spot.y_peer(d)))
+        self.stage_sem, self.cs_sem, self.cr_sem, self.ys_sem, self.yr_sem = sems
+        self.chunks = from_core.shape[1]
+
+    @staticmethod
+    def sems(L, chunks):
+        dma = pltpu.SemaphoreType.DMA
+        return [dma((L // 2,))] * 3 + [dma((L // 2, chunks))] * 2
+
+    def stage(self, d):
+        return pltpu.make_async_copy(self.part(self.s.y_peer(d)), self.held(d), self.stage_sem.at[d])
+
+    def core_copy(self, d):
+        s = self.s
+        other = lax.rem(s.y + d, s.Y) * 2 + 1 - s.c
+        return remote(self.part(other), self.from_core.at[d], self.cs_sem.at[d], self.cr_sem.at[d], s.g, s.core_peer())
+
+    def y_copy(self, d, k):
+        s = self.s
+        src, dst = self.held(d), self.from_y.at[d - 1]
+        if self.fine:
+            src, dst = src.at[k], dst.at[k]
+        return remote(src, dst, self.ys_sem.at[d, k], self.yr_sem.at[d, k], s.g, s.y_peer(d))
+
+    def start(self):
+        for d in range(self.s.Y):
+            if self.staged:
+                self.stage(d).start()
+            self.core_copy(d).start()
+
+    def ready(self):
+        for d in range(self.s.Y):
+            if self.staged:
+                self.stage(d).wait()
+            self.core_copy(d).wait_recv()
+
+    def add(self, d, k):
+        self.held(d)[k] = (self.held(d)[k].astype(f32) + self.from_core[d, k].astype(f32)).astype(bf16)
+
+    def relay(self, k=0):
+        for d in range(1, self.s.Y):
+            if self.fine:
+                self.add(d, k)
+            else:
+
+                def body(i, carry, d=d):
+                    self.add(d, i)
+                    return carry
+
+                lax.fori_loop(0, self.chunks, body, 0)
+            self.y_copy(d, k).start()
+
+    def got(self, k=0):
+        for d in range(1, self.s.Y):
+            self.y_copy(d, k).wait_recv()
+
+    def total(self, k):
+        value = self.held(0)[k].astype(f32) + self.from_core[0, k].astype(f32)
+        for d in range(1, self.s.Y):
+            value += self.from_y[d - 1, k].astype(f32)
+        return value
+
+    def sent(self):
+        for d in range(self.s.Y):
+            self.core_copy(d).wait_send()
+        for d in range(1, self.s.Y):
+            for k in range(self.chunks if self.fine else 1):
+                self.y_copy(d, k).wait_send()
+
+
+class LaneScatter:
+    def __init__(self, spot, part, held, from_x, from_z, sems):
+        self.s, self.part, self.from_x, self.from_z = spot, part, from_x, from_z
+        self.staged = held is not None
+        self.held = (lambda d: held.at[d]) if self.staged else (lambda d: part(spot.z_peer(d)))
+        self.stage_sem, self.xs_sem, self.xr_sem, self.zs_sem, self.zr_sem = sems
+
+    @staticmethod
+    def sems(W, X):
+        dma = pltpu.SemaphoreType.DMA
+        Z = W // X
+        return [dma((Z,)), dma((X, Z)), dma((X, Z)), dma((Z,)), dma((Z,))]
+
+    def stage(self, d):
+        return pltpu.make_async_copy(self.part(self.s.z_peer(d)), self.held(d), self.stage_sem.at[d])
+
+    def x_copy(self, e, d):
+        s = self.s
+        return remote(self.part(s.zx_peer(d, e)), self.from_x.at[e - 1, d], self.xs_sem.at[e, d], self.xr_sem.at[e, d],
+                      s.x_peer(e), s.l)
+
+    def z_copy(self, d):
+        s = self.s
+        return remote(self.held(d), self.from_z.at[d - 1], self.zs_sem.at[d], self.zr_sem.at[d], s.z_peer(d), s.l)
+
+    def start(self):
+        for d in [*range(1, self.s.Z), 0]:
+            if self.staged:
+                self.stage(d).start()
+            for e in range(1, self.s.X):
+                self.x_copy(e, d).start()
+
+    def ready(self, d):
+        if self.staged:
+            self.stage(d).wait()
+        for e in range(1, self.s.X):
+            self.x_copy(e, d).wait_recv()
+
+    def relay(self):
+        for d in range(1, self.s.Z):
+            self.ready(d)
+            add_rows(self.held(d), [self.held(d)] + [self.from_x.at[e - 1, d] for e in range(1, self.s.X)])
+            self.z_copy(d).start()
+
+    def finish(self, dst):
+        self.ready(0)
+        for d in range(1, self.s.Z):
+            self.z_copy(d).wait_recv()
+        add_rows(dst, [self.held(0)] + [self.from_x.at[e - 1, 0] for e in range(1, self.s.X)]
+                 + [self.from_z.at[d - 1] for d in range(1, self.s.Z)])
+
+    def sent(self):
+        for d in range(self.s.Z):
+            for e in range(1, self.s.X):
+                self.x_copy(e, d).wait_send()
+        for d in range(1, self.s.Z):
+            self.z_copy(d).wait_send()
+
+
+def attend_back_tile(tile, qkv_ref, doc_cols, lse_ref, grad_ref, out_ref, mask_ref, dk_ref, dv_ref):
+    cols = grad_ref.shape[1]
+    extent = (tile + 1) * Q_TILE
+    here, seen = pl.ds(tile * Q_TILE, Q_TILE), pl.ds(0, extent)
+    mask_tile(tile, doc_cols, mask_ref)
+
+    def pair_step(pair, carry):
+        q_cols = pl.ds(pl.multiple_of(pair * PAIR, PAIR), PAIR)
+        k_cols = pl.ds(pl.multiple_of(cols + pair * PAIR, PAIR), PAIR)
+        v_cols = pl.ds(pl.multiple_of(2 * cols + pair * PAIR, PAIR), PAIR)
+        queries = qkv_ref[here, q_cols] * jnp.asarray(HEAD_DIM**-0.5, bf16)
+        keys, values = qkv_ref[seen, k_cols], qkv_ref[seen, v_cols]
+        grads = grad_ref[here, q_cols]
+        dq = jnp.zeros((PAIR, Q_TILE), f32)
+        for half in range(2):
+            on = head_mask(half)
+            q_one = jnp.where(on, queries, jnp.zeros_like(queries))
+            g_one = jnp.where(on, grads, jnp.zeros_like(grads))
+            probs = jnp.exp(mm(keys, q_one, 1, 1) + mask_ref[seen, :] - lse_ref[pair, pl.ds(half, 1), here])
+            dv_ref[pair, seen, :] += mm(probs.astype(bf16), g_one)
+            back = mm(values, g_one, 1, 1)
+            low = (probs * (back - jnp.sum(probs * back, axis=0, keepdims=True))).astype(bf16)
+            dk_ref[pair, seen, :] += mm(low, q_one)
+            got = mm(keys, low, 0, 0)
+            sublanes = lax.broadcasted_iota(jnp.int32, (PAIR, 1), 0)
+            dq = jnp.where((sublanes // HEAD_DIM) == half, got, dq)
+        out_ref[here, q_cols] = (dq.T * HEAD_DIM**-0.5).astype(bf16)
+        return carry
+
+    lax.fori_loop(0, cols // PAIR, pair_step, 0)
+
+
+def take_from(sems):
+    sems = list(sems)
+
+    def take(n):
+        out = sems[:n]
+        del sems[:n]
+        return out
+
+    return take
+
+
+def picked(logits, first, count):
+    columns = lax.broadcasted_iota(jnp.int32, logits.shape, 1)
+    return soft_max(jnp.where((columns >= first) & (columns < first + count), logits, masked_score))
+
+
+def back_kernel(
+    groups, lanes, experts,
+    tokens, cot, meta, small, attention_out, attn_mixed, place, meta_all, lse, grad_small,
+    mix_part, dense_part, back_part, tok_part, grad_up, grad_down, qkv_in, output_in, attend_in, normed_in,
+    layer_out, grad_tokens, small_out, all_attend, all_output, all_up, all_down,
+    qkv, output_all, attend_all, normed, bk_h, bk_c, bk_y, tk_h, tk_c, tk_y, mx_h, mx_c, mx_y, dn_h, dn_c, dn_y,
+    go, go_c, go_y, gn, gn_c, gn_y, up_h, up_x, up_z, dw_h, dw_x, dw_z, ga, ga_x, ga_z, gl, gl_x, gl_z,
+    sm, sm_x, sm_z, sm_mine, sm_all, ret_back, got_back, ret_tok, got_tok, grad_mix, grad_mid, grad_attn, grad_mixed,
+    grad_heads, grad_qkv, mask, dk, dv, valid_cols, mine_attend, mine_output, mine_up, mine_down, stage_sem, *sems,
+):
+    s = Spot(groups, lanes)
+    rows, width = tokens.shape
+    head_cols = width // lanes
+    slots = place.shape[1] // groups
+    shard = width // groups
+    take = take_from(sems)
+    step = 64
+
+    def blocks(ref, n):
+        return lambda i: ref.at[pl.ds(pl.multiple_of(i * n, n), n)]
+
+    def cols(i):
+        return pl.ds(pl.multiple_of(i * head_cols, head_cols), head_cols)
+
+    loads = [
+        pltpu.make_async_copy(src, dst, stage_sem.at[i])
+        for i, (src, dst) in enumerate(
+            [(output_in, output_all), (qkv_in, qkv), (attend_in, attend_all), (normed_in, normed)])
+    ]
+    bk = GroupScatter(s, lambda l: back_part.at[l], bk_h, bk_c, bk_y, take(5), True)
+    tk = GroupScatter(s, lambda l: tok_part.at[l], tk_h, tk_c, tk_y, take(5), True)
+    mx = GroupScatter(s, lambda l: mix_part.at[l], mx_h, mx_c, mx_y, take(5), False)
+    dn = GroupScatter(s, lambda l: dense_part.at[l], dn_h, dn_c, dn_y, take(5), False)
+    gos = GroupScatter(s, lambda l: go.at[l], None, go_c, go_y, take(5), False)
+    gns = GroupScatter(s, lambda l: gn.at[l], None, gn_c, gn_y, take(5), False)
+    ups = LaneScatter(s, blocks(grad_up, shard), up_h, up_x, up_z, take(5))
+    dws = LaneScatter(s, blocks(grad_down, shard), dw_h, dw_x, dw_z, take(5))
+    gas = LaneScatter(s, blocks(ga, shard), None, ga_x, ga_z, take(5))
+    gls = LaneScatter(s, blocks(gl, shard), None, gl_x, gl_z, take(5))
+    sms = LaneScatter(s, lambda w: sm.at[w], None, sm_x, sm_z, take(5))
+    back_swap = LaneSwap(s, blocks(ret_back, slots), blocks(got_back, slots), take(2))
+    tok_swap = LaneSwap(s, blocks(ret_tok, slots), blocks(got_tok, slots), take(2))
+    heads = GroupSwap(s, lambda l: grad_mixed.at[:, cols(l)], blocks(grad_heads, rows), take(2))
+    f_attend = GroupGather(s, mine_attend, lambda l: all_attend.at[l], take(4))
+    f_output = GroupGather(s, mine_output, lambda l: all_output.at[l], take(4))
+    f_up = GroupGather(s, mine_up, lambda l: all_up.at[l], take(4))
+    f_down = GroupGather(s, mine_down, lambda l: all_down.at[l], take(4))
+    f_small = GroupGather(s, sm_mine, lambda l: sm_all.at[l], take(4))
+    order = [(d, s.w_peer(d)) for d in [*range(1, groups), 0]]
+
+    def pass_on(scatter):
+        for _, w in order:
+            scatter.relay(w)
+
+    def hand_back(scatter, swap, ret):
+        for d, w in order:
+            scatter.got(w)
+            ret[pl.ds(pl.multiple_of(w * slots, slots), slots), :] = scatter.total(w).astype(bf16)
+            if d:
+                swap.copy(d).start()
+            else:
+                swap.own().start()
+
+    def totals(scatter, dst):
+        scatter.got()
+
+        def body(k, carry):
+            dst[pl.ds(pl.multiple_of(k * step, step), step), :] = scatter.total(k).astype(dst.dtype)
+            return carry
+
+        lax.fori_loop(0, scatter.chunks, body, 0)
+
+    def over_rows(body, init):
+        return lax.fori_loop(0, rows // step, lambda i, c: body(pl.ds(pl.multiple_of(i * step, step), step), c), init)
+
+    s.greet()
+    bk.start()
+    mx.start()
+    ups.start()
+    for c in loads:
+        c.start()
+    dk[...] = jnp.zeros_like(dk)
+    dv[...] = jnp.zeros_like(dv)
+    gains = small[...].astype(f32).T
+    mine = meta[...].T
+    valid_cols[...] = jnp.broadcast_to(mine[:, 1:2], valid_cols.shape)
+    bk.ready()
+    pass_on(bk)
+    mx.ready()
+    mx.relay()
+    dws.start()
+    hand_back(bk, back_swap, ret_back)
+    tk.start()
+    dn.start()
+    ups.relay()
+    totals(mx, grad_mix)
+    for c in loads:
+        c.wait()
+    back_swap.arrive()
+    grad_mix[...] += mm(place[...], got_back[...])
+
+    def mid(at, gain_sum):
+        normed_v, scale = norm_stats(tokens[at, :].astype(f32) + attention_out[at, :])
+        grad = grad_mix[at, :]
+        value = cot[at, :].astype(f32) * valid_cols[at, 0:1] + norm_back(normed_v, scale, gains[1:2, :], grad)
+        grad_mid[at, :] = value
+        grad_attn[at, :] = value.astype(bf16)
+        return gain_sum + jnp.sum(grad * normed_v, axis=0, keepdims=True)
+
+    mixer_gain_grad = over_rows(mid, jnp.zeros((1, width), f32))
+    grad_mixed[...] = mm(grad_attn[...], output_all[...], 1, 1).astype(bf16)
+    for l in range(lanes):
+        heads.send(l)
+
+    def out_grad(m, carry):
+        value = mm(attn_mixed[:, cols(m)], grad_attn[...], 0, 0).astype(bf16)
+        parts = head_cols // step
+        for l in range(lanes):
+            go[l, pl.ds(m * parts, parts)] = value[:, l * head_cols : (l + 1) * head_cols].reshape(parts, step, head_cols)
+        return carry
+
+    lax.fori_loop(0, lanes, out_grad, 0)
+    gos.start()
+    tk.ready()
+    dws.relay()
+    heads.arrive()
+    doc_cols = [meta_all[l].T[:, 0:1] for l in range(lanes)]
+    for tile in range(lanes):
+        attend_back_tile(tile, qkv, doc_cols, lse, grad_heads, grad_qkv, mask, dk, dv)
+        if tile == 0:
+            pass_on(tk)
+        if tile == 1:
+            gos.ready()
+            gos.relay()
+        if tile == 2:
+            dn.ready()
+            dn.relay()
+    for pair in range(head_cols // PAIR):
+        grad_qkv[:, head_cols + pair * PAIR : head_cols + (pair + 1) * PAIR] = dk[pair].astype(bf16)
+        grad_qkv[:, 2 * head_cols + pair * PAIR : 2 * head_cols + (pair + 1) * PAIR] = dv[pair].astype(bf16)
+
+    def weight_grad(m, carry):
+        ga[pl.ds(pl.multiple_of(m * head_cols, head_cols), head_cols), :] = mm(normed[:, cols(m)], grad_qkv[...], 0, 0).astype(bf16)
+        return carry
+
+    lax.fori_loop(0, lanes, weight_grad, 0)
+    gas.start()
+
+    def rows_grad(l, carry):
+        value = mm(grad_qkv[pl.ds(pl.multiple_of(l * rows, rows), rows), :], attend_all[...], 1, 1)
+        gn[l] = value.astype(bf16).reshape(rows // step, step, width)
+        return carry
+
+    lax.fori_loop(0, lanes, rows_grad, 0)
+    gns.start()
+    hand_back(tk, tok_swap, ret_tok)
+    gns.ready()
+    gns.relay()
+    totals(gos, gl)
+    gls.start()
+    ups.finish(mine_up)
+    f_up.start()
+    gas.relay()
+    totals(dn, grad_mix)
+    tok_swap.arrive()
+    gls.relay()
+
+    def layer(at, sums):
+        attention = attention_out[at, :]
+        residual = tokens[at, :].astype(f32) + attention
+        normed_v, _ = norm_stats(residual)
+        mix = (normed_v * gains[1:2, :]).astype(bf16)
+        logits = mm(mix, small[...])
+        blend, router = picked(logits, 2, 2), picked(logits, 4, experts)
+        columns = lax.broadcasted_iota(jnp.int32, logits.shape, 1)
+        route = valid_cols[at, 1:2].astype(jnp.int32)
+        chosen = jnp.sum(jnp.where(columns == 4 + route, router, 0.0), axis=1, keepdims=True)
+        ffn = blend[:, 2:3] * chosen * mm(place[at, :], got_tok[...]) + blend[:, 3:4] * grad_mix[at, :]
+        full = residual + ffn
+        layer_out[at, :] = full.astype(bf16)
+        valid = valid_cols[at, 0:1]
+        got = [jnp.sum(valid * v * v, axis=(0, 1), keepdims=True) for v in (residual, full, attention, ffn)]
+        got.append(jnp.sum(valid, axis=(0, 1), keepdims=True))
+        return tuple(a + b for a, b in zip(sums, got))
+
+    lane_of = lax.broadcasted_iota(jnp.int32, valid_cols.shape, 1)
+    valid_cols[...] = jnp.where(lane_of == 1, mine[:, 2:3], mine[:, 1:2])
+    sums = over_rows(layer, tuple(jnp.zeros((1, 1), f32) for _ in range(5)))
+    totals(gns, grad_mix)
+
+    def first(at, gain_sum):
+        normed_v, scale = norm_stats(tokens[at, :].astype(f32))
+        grad = grad_mix[at, :]
+        grad_tokens[at, :] = (grad_mid[at, :] + norm_back(normed_v, scale, gains[0:1, :], grad)).astype(bf16)
+        return gain_sum + jnp.sum(grad * normed_v, axis=0, keepdims=True)
+
+    attend_gain_grad = over_rows(first, jnp.zeros((1, width), f32))
+    feature = lax.broadcasted_iota(jnp.int32, (SMALL, shard), 0)
+    place_of = lax.broadcasted_iota(jnp.int32, (SMALL, shard), 1)
+    tail = jnp.zeros((SMALL, shard), f32)
+    for i, v in enumerate(sums):
+        tail = jnp.where(place_of == i, v, tail)
+    for w in range(groups):
+        here = slice(w * shard, (w + 1) * shard)
+        value = jnp.where(feature == SMALL - 1, tail, grad_small[:, here])
+        value = jnp.where(feature == 0, attend_gain_grad[:, here], value)
+        sm[w] = jnp.where(feature == 1, mixer_gain_grad[:, here], value)
+    sms.start()
+    f_up.forward()
+    dws.finish(mine_down)
+    f_down.start()
+    sms.relay()
+    gas.finish(mine_attend)
+    f_attend.start()
+    gls.finish(mine_output)
+    f_output.start()
+    sms.finish(sm_mine)
+    f_small.start()
+    gathers = [f_up, f_down, f_attend, f_output, f_small]
+    for task in gathers[1:]:
+        task.forward()
+    for task in gathers:
+        task.arrive()
+    small_out[...] = sum([sm_all[l] for l in range(1, lanes)], sm_all[0])
+    for task in [bk, tk, mx, dn, gos, gns, ups, dws, gas, gls, sms, back_swap, tok_swap, heads] + gathers:
+        task.sent()
+
+
+def back(groups, lanes, experts, slots, inputs, placed):
+    tokens = inputs[0]
+    rows, width = tokens.shape
+    X = 1 << ((groups.bit_length() - 1) // 2)
+    Y, Z = lanes // 2, groups // X
+    everyone = rows * lanes
+    head_cols = width // lanes
+    shard = width // groups
+    hidden = placed[4].shape[1]
+    vmem, anywhere = pl.BlockSpec(memory_space=pltpu.VMEM), pl.BlockSpec(memory_space=pl.ANY)
+    dma = pltpu.SemaphoreType.DMA
+    of = jax.ShapeDtypeStruct
+    pairs = head_cols // PAIR
+    low = lambda *shape: pltpu.VMEM(shape, bf16)
+    wide = lambda *shape: pltpu.VMEM(shape, f32)
+
+    def group_bufs(c, r, n, held=True):
+        return ([low(Y, c, r, n)] if held else [low(lanes, c, r, n)]) + [low(Y, c, r, n), low(Y - 1, c, r, n)]
+
+    def lane_bufs(n, held=True):
+        return ([low(Z, shard, n)] if held else [low(width, n)]) + [low(X - 1, Z, shard, n), low(Z - 1, shard, n)]
+
+    scratch = [low(everyone, 3 * head_cols), low(width, width), low(width, 3 * head_cols), low(everyone, width)]
+    scratch[0], scratch[1] = low(everyone, 3 * head_cols), low(width, width)
+    scratch += group_bufs(groups, slots, width) * 2 + group_bufs(rows // 64, 64, width) * 2
+    scratch += group_bufs(width // 64, 64, head_cols, False) + group_bufs(rows // 64, 64, width, False)
+    scratch += lane_bufs(hidden) + lane_bufs(width) + lane_bufs(3 * head_cols, False) + lane_bufs(head_cols, False)
+    scratch += [wide(groups, SMALL, shard), wide(X - 1, Z, SMALL, shard), wide(Z - 1, SMALL, shard)]
+    scratch += [wide(SMALL, shard), wide(lanes, SMALL, shard)]
+    scratch += [low(groups * slots, width)] * 4
+    scratch += [wide(rows, width), wide(rows, width), low(rows, width), low(rows, width)]
+    scratch += [low(everyone, head_cols), low(everyone, 3 * head_cols), wide(everyone, Q_TILE)]
+    scratch += [wide(pairs, everyone, PAIR)] * 2 + [wide(rows, SMALL)]
+    scratch += [low(shard, 3 * head_cols), low(shard, head_cols), low(shard, hidden), low(shard, width)]
+    scratch += [dma((4,))]
+    scratch += GroupScatter.sems(lanes, groups) * 2 + GroupScatter.sems(lanes, 1) * 4
+    scratch += LaneScatter.sems(groups, X) * 5
+    scratch += LaneSwap.sems(groups) * 2 + GroupSwap.sems(lanes)
+    scratch += GroupGather.sems(lanes) * 5
+    outs = [
+        (of((rows, width), bf16), vmem),
+        (of((rows, width), bf16), vmem),
+        (of((SMALL, shard), f32), vmem),
+        (of((lanes, shard, 3 * head_cols), bf16), anywhere),
+        (of((lanes, shard, head_cols), bf16), anywhere),
+        (of((lanes, shard, hidden), bf16), anywhere),
+        (of((lanes, shard, width), bf16), anywhere),
+    ]
+    return pl.pallas_call(
+        functools.partial(back_kernel, groups, lanes, experts),
+        out_shape=[o for o, _ in outs],
+        in_specs=[vmem] * len(inputs) + [anywhere] * len(placed),
+        out_specs=[p for _, p in outs],
+        scratch_shapes=scratch,
+        compiler_params=pltpu.CompilerParams(collective_id=1, has_side_effects=True, vmem_limit_bytes=62 * 2**20),
+        cost_estimate=pl.CostEstimate(flops=8 * 10**9, bytes_accessed=10**8, transcendentals=0),
+        name="back",
+    )(*inputs, *placed)
+
+
 def lane_gather(part):
     return lax.all_gather(part, "wide", axis=0, tiled=True)
 
@@ -705,7 +1186,7 @@
     grad_up_pre = (up_slope * grad_up_act).astype(bf16)
     dense_logits = (jnp.where(columns == 3, 1.0, 0.0) - jnp.where(columns == 2, 1.0, 0.0)) * (blend_0 * dense_dot)
     grad_mix_part = mm(grad_up_pre, up_full, 1, 1) + mm(dense_logits.astype(bf16), mix_cols, 1, 1)
-    grad_small = mm(mix_all, dense_logits.astype(bf16), 0, 0)
+    grad_small = mm(dense_logits.astype(bf16), mix_all, 0, 0)
     grad_up = mm(mix_all, grad_up_pre, 0, 0)
     grad_down = mm(up_act, grad_dense, 0, 0)
 
@@ -736,10 +1217,34 @@
         logits += dot * blend[:, 3:4] * (jnp.where(columns == 2, 1.0, 0.0) - jnp.where(columns == 3, 1.0, 0.0))
         logits = logits.astype(bf16)
         back_parts.append(mm(grad_hidden, expert_up[e], 1, 1) + mm(logits, mix_cols, 1, 1))
-        grad_small += mm(mix_e[e], logits, 0, 0)
+        grad_small += mm(logits, mix_e[e], 0, 0)
         down_grads.append(mm(act, grad_tok, 0, 0))
         up_grads.append(mm(mix_e[e], grad_hidden, 0, 0))
     grad_expert_up, grad_expert_down = jnp.stack(up_grads), jnp.stack(down_grads)
+    def widen(gathered, parts):
+        full = gathered.reshape(lanes, shard, parts, -1)
+        return full.transpose(1, 2, 0, 3).reshape(shard, -1).astype(f32)
+
+    if all_rows * width <= 2**20 and shard % 128 == 0:
+        def chunked(part):
+            return part.astype(bf16).reshape(lanes, rows // 64, 64, width)
+
+        def slotted(parts):
+            return by_slot(jnp.stack(parts).astype(bf16)).reshape(lanes, groups, slots, width)
+
+        layer_out, grad_tokens, small_out, out_attend, out_output, out_up, out_down = back(
+            groups, lanes, experts, slots,
+            (tokens, cotangent, meta, small, attention_out, attn_mixed, place, meta_all, lse, grad_small),
+            (chunked(grad_mix_part), chunked(dense_part), slotted(back_parts), slotted(tok_parts), grad_up.astype(bf16),
+             grad_down.astype(bf16), qkv, output_full, attend_full, normed_attend))
+        sums, small_out = small_out[SMALL - 1], small_out.T
+        root_means = jnp.sqrt(sums[:4] / (jnp.maximum(sums[4], 1.0) * width))
+        return (
+            layer_out, grad_tokens, small_out[:, 0], widen(out_attend, 3), widen(out_output, 1), small_out[:, 1],
+            small_out[:, 4 : 4 + experts], small_out[:, 2:4], widen(out_up, groups),
+            out_down.reshape(-1, width).astype(f32), grad_expert_up, grad_expert_down, root_means,
+        )
+    grad_small = grad_small.T
     expert_back = give_back(by_slot(jnp.stack(back_parts)))
     expert_tok = give_back(by_slot(jnp.stack(tok_parts)))
 
@@ -771,14 +1276,12 @@
     sums = lax.psum(sums, ("wide", "narrow"))
     root_means = jnp.sqrt(sums[:4] / (jnp.maximum(sums[4], 1.0) * width))
 
-    def widen(part, parts):
-        full = group_gather(part.astype(bf16)[None])
-        full = full.reshape(lanes, part.shape[0], parts, -1)
-        return full.transpose(1, 2, 0, 3).reshape(part.shape[0], -1).astype(f32)
-
-    out_attend = widen(lane_scatter(grad_attend), 3)
-    out_output = widen(lane_scatter(group_scatter(grad_output, axis=1)), 1)
-    out_up = widen(lane_scatter(grad_up), groups)
+    def share(part):
+        return group_gather(part.astype(bf16)[None])
+
+    out_attend = widen(share(lane_scatter(grad_attend)), 3)
+    out_output = widen(share(lane_scatter(group_scatter(grad_output, axis=1))), 1)
+    out_up = widen(share(lane_scatter(grad_up)), groups)
     out_down = group_gather(lane_scatter(grad_down).astype(bf16)).astype(f32)
     return (
         layer_full.astype(bf16), grad_tokens, small_out[:, 0], out_attend, out_output, small_out[:, 1],

time: 858 us -> 431 us (0.50)
  waiting for transfers between devices: 407 us -> 0 us
  Pallas kernels: 160 us -> 300 us
  blocking collectives: 54.8 us -> 0 us
  matrix products: 102 us -> 66.7 us
  starting transfers between devices: 23.6 us -> 0 us
  other arithmetic: 43.8 us -> 20.6 us
  between operations: 16.1 us -> 2.53 us
  local copies, waits for them, and re-layouts: 44.5 us -> 34.9 us
    reduce_scatter x11 -> x0, waiting for transfers between devices: 363 us -> none  [the longest x4 218 us: lane_scatter(): lax.psum_scatter(part.astype(bf16), 'wide', scatter_dimension=0, tiled=True)]
    pallas_call x1, Pallas kernels: 16.4 us -> 157 us  [back(): pl.pallas_call(functools.partial(back_kernel, groups, lanes, experts), ou...]
    psum x1 -> x0, blocking collectives: 39.4 us -> none  [per_device(): sums = lax.psum(sums, ('wide', 'narrow'))]
    dot_general x34 -> x27, matrix products: 102 us -> 66.7 us  [mm(): lax.dot_general(a, b, (((ca,), (cb,)), ((), ())), preferred_element_type=...]
    psum x1 -> x0, waiting for transfers between devices: 31.1 us -> none  [per_device(): lax.psum(lax.psum_scatter(grad_small, 'wide', scatter_dimension=0, tiled=...]
    all_to_all x3 -> x0, starting transfers between devices: 21.9 us -> none  [the longest x2 17.7 us: lane_swap(): return lax.all_to_all(part, 'wide', split_axis=0, concat_axis=0, tiled=True)]
    all_gather x2 -> x0, blocking collectives: 15.4 us -> none  [group_gather(): return lax.all_gather(part, 'narrow', axis=axis, tiled=True)]
    all_to_all x3 -> x0, waiting for transfers between devices: 12.1 us -> none  [the longest x1 12.1 us: per_device(): lax.all_to_all(grad_mixed, 'narrow', split_axis=1, concat_axis=0, tiled=T...]
  transfers between devices with their start and end apart: 17 -> 0, of which waited for: 10 -> 0; matrix products, arithmetic and copies ran while one was open for 16% -> 0% of each run, Pallas kernels for 2% -> 0%
where the time goes in v2:
time: 431 us; the launch traced here: 425 us
  Pallas kernels  300 us (70%)
  matrix products  66.7 us (15%)
  local copies, waits for them, and re-layouts  34.9 us (8%)
  other arithmetic  20.6 us (5%)
    pallas_call x1, Pallas kernels, back(): pl.pallas_call(functools.partial(back_kernel, groups, lanes, experts), ou...  157 us
    pallas_call x1, Pallas kernels, front(): pl.pallas_call(functools.partial(front_kernel, groups, lanes, local, cap,...  144 us
    dot_general x27, matrix products, mm(): lax.dot_general(a, b, (((ca,), (cb,)), ((), ())), preferred_element_type=...  66.7 us
    unnamed x89, local copies, waits for them, and re-layouts  18 us

profile of v2, /device:TPU:0, one launch (start us, length us, event | category | flops | bytes accessed | tf_op | source)
XLA Modules:
  0.0 425.1 jit_solution(18076117365043151706)
XLA Ops:
  0.6 0.7 add_convert_fusion.5
  2.0 0.8 copy.48
  2.8 0.8 copy.49
  3.5 0.8 copy.50
  4.3 0.8 copy.51
  5.1 0.7 concatenate.7.small
  5.9 143.8 %front.1 = (bf16[1024,1024]{1,0:T(8,128)(2,1)}, bf16[1024,768]{1,0:T(8,128)(2,1)}, f32[2,2,1024]{2,1,0:T(2,128)}, bf16[256,1024]{1,0:T(8,128)(2,1)}, f32[256,102...) custom-call(bf16[256,1024]{1,0:T(8,128)(2,1)} %tokens.3, ...), custom_call_target="tpu_custom_call" | custom-call | flops 8000000000 | bytes 100000000 | tf_op jit(solution)/shard_map/front/pallas_call | solution.py:600
  149.8 4.8 %fusion.94 = f32[1024,1024]{0,1:T(8,128)S(1)} fusion(bf16[1024,1024]{1,0:T(8,128)(2,1)} %get-tuple-element.42, bf16[1024,1024]{1,0:T(8,128)(2,1)} %get-tuple-element.43), kind=kOutput, calls=%fused_computation.158 | convolution fusion | flops 2147483648 | bytes 8388608 | tf_op jit(solution)/shard_map/dot_general | solution.py:21
  154.6 0.9 slice.84
  155.5 0.8 fusion.93
  156.6 1.1 copy-done.37
  158.3 6.4 %fusion.7 = (bf16[1024,1024]{0,1:T(8,128)(2,1)}, f32[1024]{0:T(1024)S(1)}) fusion(f32[1024,1024]{0,1:T(8,128)S(1)} %fusion.94, bf16[1024,1024]{1,0:T(8,128)(2,1)S(1)} %copy-done.37, bf16[1024,1024]{1,0:T(8,128)(2,1)S(1)} %copy-done.39, f32[1024]{0:T(1024)S(1)} %bitcast.175, f32[1024]{0:T(1024)S(1)} %bitcast.177), kind=kOutput, calls=%fused_computation.15 | convolution fusion | flops 2176842752 | bytes 10498048 | tf_op jit(solution)/shard_map/dot_general | solution.py:21
  164.7 1.5 fusion.64
  167.4 0.7 fusion.72
  168.9 0.9 fusion.65
  170.5 5.0 %fusion.40 = f32[768,1024]{1,0:T(8,128)} fusion(bf16[768,1024]{1,0:T(8,128)(2,1)} %bitcast.166, bf16[2,1024,1024]{2,1,0:T(8,128)(2,1)S(1)} %copy-done.22), kind=kOutput, calls=%fused_computation.69 | convolution fusion | flops 1610612736 | bytes 6815744 | tf_op jit(solution)/shard_map/dot_general | solution.py:21
  175.6 0.8 fusion.82
  177.0 1.6 copy-done.24
  178.7 6.1 %multiply_reduce_fusion.2 = (f32[768]{0:T(1024)S(1)}, bf16[768,1024]{1,0:T(8,128)(2,1)S(1)}, bf16[768,1024]{1,0:T(8,128)(2,1)S(1)}) fusion(f32[768,1024]{1,0:T(8,128)} %fusion.40, bf16[768,1024]{1,0:T(8,128)(2,1)S(1)} %bitcast.170, bf16[2,1024,1024]{2,1,0:T(8,128)(2,1)S(1)} %copy-done.24), kind=kOutput, calls=%fused_computation.47 | convolution fusion | flops 1629486336 | bytes 9964544 | tf_op jit(solution)/shard_map/dot_general | solution.py:21
  184.8 0.9 fusion.81
  186.3 1.1 copy-done.10
  187.4 1.8 fusion.34
  189.2 4.0 multiply_reduce_fusion.1
  193.3 1.0 fusion.79
  194.2 1.3 convolution_add_fusion.grad_small
  196.2 2.4 fusion.95
  198.6 2.1 add_convert_fusion
  200.7 0.8 copy-done.34
  202.2 4.1 convolution_convert_fusion.2
  206.3 1.8 fusion.32
  208.1 0.8 add_convert_fusion.1
  208.9 1.8 fusion.38
  210.7 0.8 add_convert_fusion.2
  211.5 2.0 pad_maximum_fusion.2
  213.4 2.0 fusion.56
  215.5 1.8 fusion.59
  217.6 2.1 copy.54
  219.7 3.8 convolution_convert_fusion.1.grad_up
  223.5 4.3 %convolution_convert_fusion.grad_down = bf16[1024,1024]{1,0:T(8,128)(2,1)} fusion(bf16[1024,1024]{1,0:T(8,128)(2,1)S(1)} %copy-done.40, f32[1024]{0:T(1024)S(1)} %bitcast.176, f32[1024]{0:T(1024)S(1)} %bitcast.178, f32[1024,1024]{0,1:T(8,128)S(1)} %copy-done.34), kind=kOutput, calls=%fused_computation.71 | convolution fusion | flops 2162163712 | bytes 8396800 | tf_op jit(solution)/shard_map/dot_general | solution.py:21
  227.8 156.5 %back.1 = (bf16[256,1024]{1,0:T(8,128)(2,1)}, bf16[256,1024]{1,0:T(8,128)(2,1)}, f32[128,128]{1,0:T(8,128)}, bf16[4,128,768]{2,1,0:T(8,128)(2,1)}, bf16[4,128,25...) custom-call(bf16[256,1024]{1,0:T(8,128)(2,1)} %tokens.3, bf16[256,1024]{1,0:T(8,128)(2,1)} %cot.3, ...), custom_call_target="tpu_custom_call" | custom-call | flops 8000000000 | bytes 100000000 | tf_op jit(solution)/shard_map/back/pallas_call | solution.py:1094
  384.3 1.3 slice_bitcast_fusion
  385.6 1.4 copy.55
  387.1 1.6 copy.59
  389.0 1.0 copy.60
  390.0 1.3 slice.115
  391.3 1.2 slice.116
  392.5 1.5 copy.61
  394.2 1.4 copy.58
  395.5 2.1 reshape.202
  397.7 1.6 bitcast_convert_fusion
  399.3 0.9 copy-done.32
  400.3 1.9 convolution_bitcast_fusion.2
  402.2 1.9 convolution_bitcast_fusion.3
  404.1 4.3 %pad_maximum_fusion = f32[2,1024,1024]{2,1,0:T(8,128)} fusion(f32[1,1024,1024]{2,1,0:T(8,128)S(1)} %convolution_bitcast_fusion.2, f32[1,1024,1024]{2,1,0:T(8,128)S(1)} %convolution_bitcast_fusion.3), kind=kLoop, calls=%fused_computation | loop fusion | flops 2097152 | bytes 16777216 | tf_op jit(solution)/shard_map/stack | solution.py:1223
  408.3 0.7 slice_convert_fusion.1
  409.3 1.2 copy-done.28
  410.5 1.9 convolution_bitcast_fusion
  412.6 1.2 copy-done.26
  413.7 1.9 convolution_bitcast_fusion.1
  415.6 4.3 %pad_maximum_fusion.1 = f32[2,1024,1024]{2,1,0:T(8,128)} fusion(f32[1,1024,1024]{2,1,0:T(8,128)S(1)} %convolution_bitcast_fusion, f32[1,1024,1024]{2,1,0:T(8,128)S(1)} %convolution_bitcast_fusion.1), kind=kLoop, calls=%fused_computation.1 | loop fusion | flops 2097152 | bytes 16777216 | tf_op jit(solution)/shard_map/stack | solution.py:1223
  419.9 1.3 slice.102
  421.8 1.2 sqrt_bitcast_fusion
  423.0 0.8 copy.64
  423.8 0.8 copy.65
  (103 shorter events, 7.9 us)
Async XLA Ops:
  149.7 5.8 %copy-start.2 = (bf16[1024,1024]{1,0:T(8,128)(2,1)S(1)}, bf16[1024,1024]{1,0:T(8,128)(2,1)}, u32[]{:S(2)}) copy-start(bf16[1024,1024]{1,0:T(8,128)(2,1)} %get-tuple-element.42) | copy-start | bytes 6291460
  149.7 5.8 %copy-start.4 = (bf16[1024,128]{1,0:T(8,128)(2,1)S(1)}, bf16[1024,128]{1,0:T(8,128)(2,1)}, u32[]{:S(2)}) copy-start(bf16[1024,128]{1,0:T(8,128)(2,1)} %get-tuple-element.36.small) | copy-start | bytes 786436
  154.5 10.2 %copy-start.33 = (f32[1024,1024]{0,1:T(8,128)}, f32[1024,1024]{0,1:T(8,128)S(1)}, u32[]{:S(2)}) copy-start(f32[1024,1024]{0,1:T(8,128)S(1)} %fusion.94) | copy-start | bytes 12582916
  154.5 3.1 copy-start.37
  154.5 3.7 copy-start.39
  158.3 7.9 %copy-start.12 = (bf16[4,8,48,1024]{3,2,1,0:T(8,128)(2,1)S(1)}, bf16[4,8,48,1024]{3,2,1,0:T(8,128)(2,1)}, u32[]{:S(2)}) copy-start(bf16[4,8,48,1024]{3,2,1,0:T(8,128)(2,1)} %get-tuple-element.46) | copy-start | bytes 9437188
  166.6 2.2 copy-start.9
  166.6 2.2 copy-start.13
  167.3 1.5 copy-start.7
  167.4 3.1 copy-start.22
  168.1 0.8 copy-start.5
  168.8 6.7 %copy-start.20 = (f32[768,128]{0,1:T(8,128)}, f32[768,128]{0,1:T(8,128)S(1)}, u32[]{:S(2)}) copy-start(f32[768,128]{0,1:T(8,128)S(1)} %get-tuple-element.112) | copy-start | bytes 1179652
  170.5 6.0 %copy-start = (bf16[4,8,48,1024]{3,2,1,0:T(8,128)(2,1)S(1)}, bf16[4,8,48,1024]{3,2,1,0:T(8,128)(2,1)}, u32[]{:S(2)}) copy-start(bf16[4,8,48,1024]{3,2,1,0:T(8,128)(2,1)} %get-tuple-element.47) | copy-start | bytes 9437188
  176.5 2.2 copy-start.24
  178.6 7.1 %copy-start.6 = (f32[768,128]{0,1:T(8,128)S(1)}, f32[768,128]{0,1:T(8,128)}, u32[]{:S(2)}) copy-start(f32[768,128]{0,1:T(8,128)} %copy-done.5) | copy-start | bytes 1179652
  178.6 7.1 %copy-start.14 = (bf16[1,32,24,1024]{3,2,0,1:T(8,128)(2,1)S(1)}, bf16[1,32,24,1024]{3,2,0,1:T(8,128)(2,1)}, u32[]{:S(2)}) copy-start(bf16[1,32,24,1024]{3,2,0,1:T(8,128)(2,1)} %copy-done.13) | copy-start | bytes 4718596
  178.7 7.1 %copy-start.19 = (f32[128,1024]{1,0:T(8,128)S(1)}, f32[128,1024]{1,0:T(8,128)}, u32[]{:S(2)}) copy-start(f32[128,1024]{1,0:T(8,128)} %fusion.64) | copy-start | bytes 1572868
  178.7 7.6 %copy-start.23 = (bf16[2,1024,1024]{2,1,0:T(8,128)(2,1)S(1)}, bf16[2,1024,1024]{2,1,0:T(8,128)(2,1)}, u32[]{:S(2)}) copy-start(bf16[2,1024,1024]{2,1,0:T(8,128)(2,1)} %param.28) | copy-start | bytes 12582916
  184.8 24.1 %copy-start.29 = (bf16[768,1024]{1,0:T(8,128)(2,1)}, bf16[768,1024]{1,0:T(8,128)(2,1)S(1)}, u32[]{:S(2)}) copy-start(bf16[768,1024]{1,0:T(8,128)(2,1)S(1)} %get-tuple-element.102) | copy-start | bytes 4718596
  184.8 30.7 %copy-start.25 = (bf16[768,1024]{1,0:T(8,128)(2,1)}, bf16[768,1024]{1,0:T(8,128)(2,1)S(1)}, u32[]{:S(2)}) copy-start(bf16[768,1024]{1,0:T(8,128)(2,1)S(1)} %get-tuple-element.99) | copy-start | bytes 4718596
  184.8 2.6 copy-start.10
  189.2 5.1 %copy-start.8 = (f32[768,128]{0,1:T(8,128)S(1)}, f32[768,128]{0,1:T(8,128)}, u32[]{:S(2)}) copy-start(f32[768,128]{0,1:T(8,128)} %copy-done.7) | copy-start | bytes 1179652
  189.2 6.3 %copy-start.36 = (bf16[1024,1024]{1,0:T(8,128)(2,1)S(1)}, bf16[1024,1024]{1,0:T(8,128)(2,1)}, u32[]{:S(2)}) copy-start(bf16[1024,1024]{1,0:T(8,128)(2,1)} %get-tuple-element.43) | copy-start | bytes 6291460
  193.2 13.1 %copy-start.31 = (bf16[768,1024]{1,0:T(8,128)(2,1)}, bf16[768,1024]{1,0:T(8,128)(2,1)S(1)}, u32[]{:S(2)}) copy-start(bf16[768,1024]{1,0:T(8,128)(2,1)S(1)} %get-tuple-element.103) | copy-start | bytes 4718596
  193.2 20.2 %copy-start.27 = (bf16[768,1024]{1,0:T(8,128)(2,1)}, bf16[768,1024]{1,0:T(8,128)(2,1)S(1)}, u32[]{:S(2)}) copy-start(bf16[768,1024]{1,0:T(8,128)(2,1)S(1)} %get-tuple-element.97) | copy-start | bytes 4718596
  193.2 2.9 copy-start.35
  198.6 2.9 copy-start.34
  198.6 3.6 copy-start.38
  217.6 2.1 copy-start.3
  219.7 3.8 copy-start.40
  387.0 1.7 copy-start.21
  395.5 2.1 copy-start.16
  397.6 1.7 copy-start.11
  397.6 2.6 copy-start.32
  400.3 1.9 copy-start.15
  400.3 1.9 copy-start.30
  404.0 4.3 %copy-start.1 = (bf16[4,8,48,1024]{3,2,1,0:T(8,128)(2,1)S(1)}, bf16[4,8,48,1024]{3,2,1,0:T(8,128)(2,1)}, u32[]{:S(2)}) copy-start(bf16[4,8,48,1024]{3,2,1,0:T(8,128)(2,1)} %get-tuple-element.47) | copy-start | bytes 9437188
  409.1 1.4 copy-start.28
  412.3 1.4 copy-start.26
  415.6 7.4 %copy-start.18 = (bf16[256,1024]{1,0:T(8,128)(2,1)S(1)}, bf16[256,1024]{1,0:T(8,128)(2,1)}, u32[]{:S(2)}) copy-start(bf16[256,1024]{1,0:T(8,128)(2,1)} %get-tuple-element.137) | copy-start | bytes 1572868
  415.6 8.2 %copy-start.17 = (bf16[256,1024]{1,0:T(8,128)(2,1)S(1)}, bf16[256,1024]{1,0:T(8,128)(2,1)}, u32[]{:S(2)}) copy-start(bf16[256,1024]{1,0:T(8,128)(2,1)} %get-tuple-element.138) | copy-start | bytes 1572868

commit v3 on v2

--- a/solution.py
+++ b/solution.py
@@ -406,8 +406,8 @@
     groups, lanes, local, cap, slots,
     tokens, cot, meta, small, attend_w, output_w, up_w, down_w,
     normed_out, qkv, lse, attn_mixed, attention_out, mix_all, small_all, meta_all, place,
-    attend_all, output_all, got_mix, got_cot, cot_all, up_all, down_all,
-    tok_all, attend_mine, up_mine, mixed, mask, vt, packed_mix, packed_cot, stage_sem, spread_y, spread_c, spread_r, *sems,
+    attend_all, output_all, packed_cot, got_mix, cot_all, up_all, down_all,
+    tok_all, attend_mine, up_mine, mixed, mask, vt, packed_mix, stage_sem, spread_y, spread_c, spread_r, *sems,
 ):
     s = Spot(groups, lanes)
     rows, width = tokens.shape
@@ -451,7 +451,6 @@
     cots = GroupGather(s, cot, blocks(cot_all, rows), take(4))
     mix = GroupGather(s, blocks(mix_all, rows)(s.l), blocks(mix_all, rows), take(4), own=False)
     outs = GroupGather(s, output_all.at[:, cols(s.l)], lambda l: output_all.at[:, cols(l)], take(4), own=False)
-    cot_spread = GroupGather(s, got_cot.at[s.l], lambda l: got_cot.at[l], take(4), own=False)
     att = LaneGather(s, attend_mine, blocks(attend_all, shard), take(4))
     sml = LaneGather(s, small, blocks(small_all, shard), take(4))
     out = LaneGather(s, output_w.at[:, cols(s.l)],
@@ -460,7 +459,6 @@
     down = LaneGather(s, down_w.at[pl.ds(pl.multiple_of(s.l * depth, depth), depth)], blocks(down_all, depth), take(4))
     swap = GroupSwap(s, blocks(mixed, rows), lambda l: attn_mixed.at[:, cols(l)], take(2))
     mix_swap = LaneSwap(s, blocks(packed_mix, slots), lambda w: got_mix.at[s.l, w], take(2))
-    cot_swap = LaneSwap(s, blocks(packed_cot, slots), lambda w: got_cot.at[s.l, w], take(2))
 
     def spread(d):
         w = s.w_peer(groups - d)
@@ -537,7 +535,6 @@
     mix.start()
     packed_mix[...] = mm(place[...], mix_all[pl.ds(base, rows), :], 0, 0).astype(bf16)
     mix_swap.start()
-    cot_swap.start()
     down.forward()
     mix.forward()
     for d in range(groups):
@@ -546,19 +543,15 @@
         else:
             mix_swap.own().wait()
         mix_spread[d].start()
-    cot_swap.arrive()
-    cot_spread.start()
     for task in mix_spread:
         task.forward()
-    cot_spread.forward()
     mix.arrive()
     for task in mix_spread:
         task.arrive()
-    cot_spread.arrive()
     cots.arrive()
     up.arrive()
     down.arrive()
-    for task in [tok, met, cots, mix, outs, cot_spread, att, sml, out, up, down, swap, mix_swap, cot_swap] + mix_spread:
+    for task in [tok, met, cots, mix, outs, att, sml, out, up, down, swap, mix_swap] + mix_spread:
         task.sent()
 
 
@@ -574,11 +567,11 @@
     dma = pltpu.SemaphoreType.DMA
     of = jax.ShapeDtypeStruct
     sems = []
-    for _ in range(6):
+    for _ in range(5):
         sems += GroupGather.sems(lanes)
     for _ in range(5):
         sems += LaneGather.sems(groups, X)
-    sems += GroupSwap.sems(lanes) + LaneSwap.sems(groups) + LaneSwap.sems(groups)
+    sems += GroupSwap.sems(lanes) + LaneSwap.sems(groups)
     outs = [
         (of((everyone, width), bf16), vmem),
         (of((everyone, 3 * head_cols), bf16), vmem),
@@ -591,7 +584,7 @@
         (of((rows, groups * slots), bf16), vmem),
         (of((width, 3 * head_cols), bf16), vmem),
         (of((width, width), bf16), vmem),
-        (of((lanes, groups, slots, width), bf16), anywhere),
+        (of((groups * slots, width), bf16), vmem),
         (of((lanes, groups, slots, width), bf16), anywhere),
         (of((everyone, width), bf16), anywhere),
         (of((width, hidden), bf16), anywhere),
@@ -610,7 +603,6 @@
             pltpu.VMEM((everyone, Q_TILE), f32),
             pltpu.VMEM((head_cols // PAIR, PAIR, everyone), bf16),
             pltpu.VMEM((groups * slots, width), bf16),
-            pltpu.VMEM((groups * slots, width), bf16),
             dma((3 + groups,)),
             dma((groups, Y)),
             dma((groups, Y)),
@@ -759,10 +751,37 @@
         add_rows(dst, [self.held(0)] + [self.from_x.at[e - 1, 0] for e in range(1, self.s.X)]
                  + [self.from_z.at[d - 1] for d in range(1, self.s.Z)])
 
-    def sent(self):
+    def fold(self, dst):
+        for d in range(self.s.Z):
+            self.ready(d)
+            add_rows(dst.at[d], [self.held(d)] + [self.from_x.at[e - 1, d] for e in range(1, self.s.X)])
+
+    def x_sent(self):
         for d in range(self.s.Z):
             for e in range(1, self.s.X):
                 self.x_copy(e, d).wait_send()
+
+    def sent(self):
+        self.x_sent()
+        for d in range(1, self.s.Z):
+            self.z_copy(d).wait_send()
+
+
+class ZScatter(LaneScatter):
+    def __init__(self, spot, held, from_z, sems):
+        self.s, self.held, self.from_z = spot, held, from_z
+        self.zs_sem, self.zr_sem = sems
+
+    def start(self):
+        for d in range(1, self.s.Z):
+            self.z_copy(d).start()
+
+    def finish(self, dst):
+        for d in range(1, self.s.Z):
+            self.z_copy(d).wait_recv()
+        add_rows(dst, [self.held(0)] + [self.from_z.at[d - 1] for d in range(1, self.s.Z)])
+
+    def sent(self):
         for d in range(1, self.s.Z):
             self.z_copy(d).wait_send()
 
@@ -815,15 +834,303 @@
     return soft_max(jnp.where((columns >= first) & (columns < first + count), logits, masked_score))
 
 
+def middle_kernel(
+    groups, lanes, local, cap, experts,
+    small, meta_all, place,
+    mix_in, cot_in, up_in, down_in, got_mix_in, packed_cot, expert_up, expert_down,
+    grad_mix, dense_out, grad_small, mine_up, down_half, tok_part, mix_e_out, grad_e_out, act_e_out, hidden_e_out,
+    mix, cot, up, down, act, hidden, got_mix, got_cot, mix_e, grad_e, act_e, hidden_e, expert_in, expert_to,
+    mx, mx_c, mx_y, dn, dn_c, dn_y, bk_c, bk_y, gu, gu_x, gu_z, gd, gd_x, ret_back, got_back, dots, coefs,
+    load_sem, out_sem, spread_y, spread_c, spread_r, *sems,
+):
+    s = Spot(groups, lanes)
+    everyone, width = mix.shape
+    rows = everyone // lanes
+    units = up.shape[1]
+    slots = got_mix.shape[2]
+    shard = width // groups
+    rows_e = mix_e.shape[1]
+    tile = 256
+    step = 64
+    take = take_from(sems)
+
+    def blocks(ref, n):
+        return lambda i: ref.at[pl.ds(pl.multiple_of(i * n, n), n)]
+
+    def part(i, n=tile):
+        return pl.ds(pl.multiple_of(i * n, n), n)
+
+    def load(i, src, dst):
+        return pltpu.make_async_copy(src, dst, load_sem.at[i])
+
+    cot_swap = LaneSwap(s, blocks(packed_cot, slots), lambda w: got_cot.at[s.l, w], take(2))
+    mxs = GroupScatter(s, lambda l: mx.at[l], None, mx_c, mx_y, take(5), False)
+    dns = GroupScatter(s, lambda l: dn.at[l], None, dn_c, dn_y, take(5), False)
+    bks = GroupScatter(s, lambda l: got_cot.at[l], None, bk_c, bk_y, take(5), True)
+    ups = LaneScatter(s, blocks(gu, shard), None, gu_x, gu_z, take(5))
+    dws = LaneScatter(s, blocks(gd, shard), None, gd_x, None, take(5))
+    back_swap = LaneSwap(s, blocks(ret_back, slots), blocks(got_back, slots), take(2))
+    order = [(d, s.w_peer(d)) for d in [*range(1, groups), 0]]
+
+    def spread(w):
+        return GroupGather(s, got_cot.at[s.l, w], lambda l: got_cot.at[l, w],
+                           [spread_y.at[w], spread_c.at[w], spread_r.at[w], None], own=False)
+
+    spreads = [(d, s.w_peer(groups - d)) for d in range(groups)]
+    loads = [load(i, a, b) for i, (a, b) in enumerate([
+        (mix_in, mix), (up_in, up), (cot_in, cot), (down_in, down), (got_mix_in, got_mix),
+        (expert_up.at[0], expert_in), (expert_down.at[0], expert_to)])]
+    more_loads = [load(7, expert_up.at[1], up), load(8, expert_down.at[1], down)]
+
+    def branch(x, grad, w_in, w_to, act_ref, hidden_ref, count):
+        dots[pl.ds(0, count), :] = jnp.zeros((count, SMALL), f32)
+
+        def body(n, carry):
+            value, slope = gelu_both(mm(x[...], w_in[:, part(n)]))
+            value = value.astype(bf16)
+            act_ref[pl.ds(0, count), part(n)] = value
+            back = mm(grad[...], w_to[part(n), :], 1, 1)
+            hidden_ref[pl.ds(0, count), part(n)] = (slope * back).astype(bf16)
+            both = value.astype(f32) * back
+            dots[pl.ds(0, count), :] += sum([both[:, i * SMALL : (i + 1) * SMALL] for i in range(1, tile // SMALL)], both[:, :SMALL])
+            return carry
+
+        lax.fori_loop(0, units // tile, body, 0)
+        return jnp.sum(dots[pl.ds(0, count), :], axis=1, keepdims=True)
+
+    s.greet()
+    cot_swap.start()
+    for c in loads:
+        c.start()
+    for c in loads[:4]:
+        c.wait()
+    columns = lax.broadcasted_iota(jnp.int32, (everyone, SMALL), 1)
+
+    coefs[...] = picked(mm(mix[...], small[...]), 2, 2)
+    for l in range(lanes):
+        at = pl.ds(l * rows, rows)
+        valid = meta_all[l].T[:, 1:2]
+        cot[at, :] = (coefs[at, 3:4] * (cot[at, :].astype(f32) * valid)).astype(bf16)
+    dot = branch(mix, cot, up, down, act, hidden, everyone)
+    sign = jnp.where(columns == 3, 1.0, 0.0) - jnp.where(columns == 2, 1.0, 0.0)
+    logits = (sign * (coefs[:, 2:3] * dot)).astype(bf16)
+    grad_small[...] = mm(logits, mix[...], 0, 0)
+
+    def up_grad(m, carry):
+        gu[part(m), :] = mm(mix[:, part(m)], hidden[...], 0, 0).astype(bf16)
+        return carry
+
+    lax.fori_loop(0, width // tile, up_grad, 0)
+    ups.start()
+    for d, w in spreads:
+        if d:
+            cot_swap.got(w)
+        else:
+            cot_swap.own().wait()
+        spread(w).start()
+
+    def down_grad(m, carry):
+        gd[part(m), :] = mm(act[:, part(m)], cot[...], 0, 0).astype(bf16)
+        return carry
+
+    lax.fori_loop(0, units // tile, down_grad, 0)
+    dws.start()
+
+    def mix_grad(n, carry):
+        value = mm(hidden[...], up[part(n), :], 1, 1) + mm(logits, small[part(n), :], 1, 1)
+        mx[:, :, :, part(n)] = value.astype(bf16).reshape(lanes, rows // step, step, tile)
+        return carry
+
+    lax.fori_loop(0, width // tile, mix_grad, 0)
+    mxs.start()
+
+    def out_part(n, carry):
+        value = mm(act[...], down[:, part(n)])
+        dn[:, :, :, part(n)] = value.astype(bf16).reshape(lanes, rows // step, step, tile)
+        return carry
+
+    lax.fori_loop(0, width // tile, out_part, 0)
+    dns.start()
+    for c in more_loads:
+        c.start()
+    for c in loads[4:]:
+        c.wait()
+
+    def apart(src, dst):
+        def body(j, carry):
+            pair = []
+            for i in range(2):
+                b = 2 * j + i
+                pair.append(src[b // groups, b % groups].astype(f32))
+            for e in range(local):
+                both = [p[e * cap : (e + 1) * cap] for p in pair]
+                dst[e, part(j, 2 * cap), :] = jnp.concatenate(both, axis=0).astype(bf16)
+            return carry
+
+        lax.fori_loop(0, lanes * groups // 2, body, 0)
+
+    def together(sources, dst):
+        def body(j, carry):
+            values = [src[part(j, 2 * cap), :].astype(f32) for src in sources]
+            for i in range(2):
+                b = 2 * j + i
+                dst[b // groups, b % groups] = jnp.concatenate([v[i * cap : (i + 1) * cap] for v in values], axis=0).astype(bf16)
+            return carry
+
+        lax.fori_loop(0, lanes * groups // 2, body, 0)
+
+    apart(got_mix, mix_e)
+    for _, w in spreads:
+        spread(w).forward()
+    mxs.ready()
+    mxs.relay()
+    for _, w in spreads:
+        spread(w).arrive()
+    apart(got_cot, grad_e)
+
+    backs, toks = [act, hidden], [mix, cot]
+    columns = lax.broadcasted_iota(jnp.int32, (rows_e, SMALL), 1)
+    outs = []
+    for e in range(local):
+        w_in, w_to = (expert_in, expert_to) if e == 0 else (up, down)
+        if e:
+            for c in more_loads:
+                c.wait()
+        x, grad = mix_e.at[e], grad_e.at[e]
+        scores = mm(x[...], small[...])
+        blend, router = picked(scores, 2, 2), picked(scores, 4, experts)
+        own = columns == 4 + s.g * local + e
+        chosen = jnp.sum(jnp.where(own, router, 0.0), axis=1, keepdims=True)
+        grad[...] = (blend[:, 2:3] * chosen * grad[...].astype(f32)).astype(bf16)
+        shares = jnp.where(own, 1.0, 0.0) - router
+        shares += blend[:, 3:4] * (jnp.where(columns == 2, 1.0, 0.0) - jnp.where(columns == 3, 1.0, 0.0))
+        coefs[pl.ds(0, rows_e), :] = shares
+        dot = branch(x, grad, w_in, w_to, act_e.at[e], hidden_e.at[e], rows_e)
+        logits = (dot * coefs[pl.ds(0, rows_e), :]).astype(bf16)
+        grad_small[...] += mm(logits, x[...], 0, 0)
+        if e == 0:
+            ups.relay()
+
+        def rows_back(n, carry, e=e, w_in=w_in, logits=logits):
+            value = mm(hidden_e[e], w_in[part(n), :], 1, 1) + mm(logits, small[part(n), :], 1, 1)
+            backs[e][pl.ds(0, rows_e), part(n)] = value.astype(bf16)
+            return carry
+
+        lax.fori_loop(0, width // tile, rows_back, 0)
+        if e == 0:
+            dns.ready()
+            dns.relay()
+        if e == local - 1:
+            for _, w in spreads:
+                spread(w).sent()
+            together([b.at[pl.ds(0, rows_e)] for b in backs], got_cot)
+            bks.start()
+
+        def rows_out(n, carry, e=e, w_to=w_to):
+            toks[e][pl.ds(0, rows_e), part(n)] = mm(act_e[e], w_to[:, part(n)]).astype(bf16)
+            return carry
+
+        lax.fori_loop(0, width // tile, rows_out, 0)
+        if e == local - 1:
+            bks.ready()
+            for _, w in order:
+                bks.relay(w)
+        for i, (a, b) in enumerate([(mix_e, mix_e_out), (grad_e, grad_e_out), (act_e, act_e_out), (hidden_e, hidden_e_out)]):
+            outs.append(pltpu.make_async_copy(a.at[e], b.at[e], out_sem.at[4 * e + i]))
+            outs[-1].start()
+    together([t.at[pl.ds(0, rows_e)] for t in toks], got_mix)
+    outs.append(pltpu.make_async_copy(got_mix, tok_part, out_sem.at[4 * local]))
+    outs[-1].start()
+
+    def totals(scatter, dst):
+        scatter.got()
+
+        def body(k, carry):
+            dst[pl.ds(pl.multiple_of(k * step, step), step), :] = scatter.total(k).astype(dst.dtype)
+            return carry
+
+        lax.fori_loop(0, scatter.chunks, body, 0)
+
+    totals(mxs, grad_mix)
+    for d, w in order:
+        bks.got(w)
+        ret_back[pl.ds(pl.multiple_of(w * slots, slots), slots), :] = bks.total(w).astype(bf16)
+        if d:
+            back_swap.copy(d).start()
+        else:
+            back_swap.own().start()
+    dws.fold(down_half)
+    totals(dns, dense_out)
+    ups.finish(mine_up)
+    back_swap.arrive()
+    grad_mix[...] += mm(place[...], got_back[...])
+    for c in outs:
+        c.wait()
+    dws.x_sent()
+    for task in [cot_swap, mxs, dns, bks, ups, back_swap]:
+        task.sent()
+
+
+def middle(groups, lanes, local, cap, experts, slots, inputs, placed):
+    rows, width = inputs[2].shape[0], inputs[0].shape[0]
+    X = 1 << ((groups.bit_length() - 1) // 2)
+    Y, Z = lanes // 2, groups // X
+    everyone = rows * lanes
+    shard = width // groups
+    units = placed[2].shape[1]
+    rows_e = lanes * groups * cap
+    vmem, anywhere = pl.BlockSpec(memory_space=pltpu.VMEM), pl.BlockSpec(memory_space=pl.ANY)
+    dma = pltpu.SemaphoreType.DMA
+    of = jax.ShapeDtypeStruct
+    low = lambda *shape: pltpu.VMEM(shape, bf16)
+    wide = lambda *shape: pltpu.VMEM(shape, f32)
+    expert_rows = (local, rows_e, width)
+    outs = [
+        (of((rows, width), f32), vmem),
+        (of((rows, width), bf16), vmem),
+        (of((SMALL, width), f32), vmem),
+        (of((shard, units), bf16), vmem),
+        (of((Z, shard, width), bf16), vmem),
+        (of((lanes, groups, slots, width), bf16), anywhere),
+        (of(expert_rows, bf16), anywhere),
+        (of(expert_rows, bf16), anywhere),
+        (of((local, rows_e, units), bf16), anywhere),
+        (of((local, rows_e, units), bf16), anywhere),
+    ]
+    scratch = [low(everyone, width), low(everyone, width), low(width, units), low(units, width)]
+    scratch += [low(everyone, units), low(everyone, units)]
+    scratch += [low(lanes, groups, slots, width)] * 2
+    scratch += [low(*expert_rows), low(*expert_rows), low(local, rows_e, units), low(local, rows_e, units)]
+    scratch += [low(width, units), low(units, width)]
+    scratch += [low(lanes, rows // 64, 64, width), low(Y, rows // 64, 64, width), low(Y - 1, rows // 64, 64, width)] * 2
+    scratch += [low(Y, groups, slots, width), low(Y - 1, groups, slots, width)]
+    scratch += [low(width, units), low(X - 1, Z, shard, units), low(Z - 1, shard, units)]
+    scratch += [low(units, width), low(X - 1, Z, shard, width)]
+    scratch += [low(groups * slots, width)] * 2 + [wide(everyone, SMALL)] * 2
+    scratch += [dma((9,)), dma((4 * local + 1,)), dma((groups, Y)), dma((groups, Y)), dma((groups, lanes))]
+    scratch += LaneSwap.sems(groups) + GroupScatter.sems(lanes, 1) * 2 + GroupScatter.sems(lanes, groups)
+    scratch += LaneScatter.sems(groups, X) * 2 + LaneSwap.sems(groups)
+    return pl.pallas_call(
+        functools.partial(middle_kernel, groups, lanes, local, cap, experts),
+        out_shape=[o for o, _ in outs],
+        in_specs=[vmem] * len(inputs) + [anywhere] * len(placed),
+        out_specs=[p for _, p in outs],
+        scratch_shapes=scratch,
+        compiler_params=pltpu.CompilerParams(collective_id=2, has_side_effects=True, vmem_limit_bytes=62 * 2**20),
+        cost_estimate=pl.CostEstimate(flops=35 * 10**9, bytes_accessed=10**8, transcendentals=0),
+        name="middle",
+    )(*inputs, *placed)
+
+
 def back_kernel(
     groups, lanes, experts,
-    tokens, cot, meta, small, attention_out, attn_mixed, place, meta_all, lse, grad_small,
-    mix_part, dense_part, back_part, tok_part, grad_up, grad_down, qkv_in, output_in, attend_in, normed_in,
+    tokens, cot, meta, small, attention_out, attn_mixed, place, meta_all, lse, grad_small, grad_mix_in, dense_out,
+    mine_up, down_half, tok_part, qkv_in, output_in, attend_in, normed_in,
     layer_out, grad_tokens, small_out, all_attend, all_output, all_up, all_down,
-    qkv, output_all, attend_all, normed, bk_h, bk_c, bk_y, tk_h, tk_c, tk_y, mx_h, mx_c, mx_y, dn_h, dn_c, dn_y,
-    go, go_c, go_y, gn, gn_c, gn_y, up_h, up_x, up_z, dw_h, dw_x, dw_z, ga, ga_x, ga_z, gl, gl_x, gl_z,
-    sm, sm_x, sm_z, sm_mine, sm_all, ret_back, got_back, ret_tok, got_tok, grad_mix, grad_mid, grad_attn, grad_mixed,
-    grad_heads, grad_qkv, mask, dk, dv, valid_cols, mine_attend, mine_output, mine_up, mine_down, stage_sem, *sems,
+    qkv, output_all, attend_all, normed, tk_h, tk_c, tk_y,
+    go, go_c, go_y, gn, gn_c, gn_y, dw_z, ga, ga_x, ga_z, gl, gl_x, gl_z,
+    sm, sm_x, sm_z, sm_mine, sm_all, ret_tok, got_tok, grad_mix, grad_mid, grad_attn, grad_mixed,
+    grad_heads, grad_qkv, mask, dk, dv, valid_cols, mine_attend, mine_output, mine_down, stage_sem, *sems,
 ):
     s = Spot(groups, lanes)
     rows, width = tokens.shape
@@ -844,18 +1151,13 @@
         for i, (src, dst) in enumerate(
             [(output_in, output_all), (qkv_in, qkv), (attend_in, attend_all), (normed_in, normed)])
     ]
-    bk = GroupScatter(s, lambda l: back_part.at[l], bk_h, bk_c, bk_y, take(5), True)
     tk = GroupScatter(s, lambda l: tok_part.at[l], tk_h, tk_c, tk_y, take(5), True)
-    mx = GroupScatter(s, lambda l: mix_part.at[l], mx_h, mx_c, mx_y, take(5), False)
-    dn = GroupScatter(s, lambda l: dense_part.at[l], dn_h, dn_c, dn_y, take(5), False)
     gos = GroupScatter(s, lambda l: go.at[l], None, go_c, go_y, take(5), False)
     gns = GroupScatter(s, lambda l: gn.at[l], None, gn_c, gn_y, take(5), False)
-    ups = LaneScatter(s, blocks(grad_up, shard), up_h, up_x, up_z, take(5))
-    dws = LaneScatter(s, blocks(grad_down, shard), dw_h, dw_x, dw_z, take(5))
+    dws = ZScatter(s, lambda d: down_half.at[d], dw_z, take(2))
     gas = LaneScatter(s, blocks(ga, shard), None, ga_x, ga_z, take(5))
     gls = LaneScatter(s, blocks(gl, shard), None, gl_x, gl_z, take(5))
     sms = LaneScatter(s, lambda w: sm.at[w], None, sm_x, sm_z, take(5))
-    back_swap = LaneSwap(s, blocks(ret_back, slots), blocks(got_back, slots), take(2))
     tok_swap = LaneSwap(s, blocks(ret_tok, slots), blocks(got_tok, slots), take(2))
     heads = GroupSwap(s, lambda l: grad_mixed.at[:, cols(l)], blocks(grad_heads, rows), take(2))
     f_attend = GroupGather(s, mine_attend, lambda l: all_attend.at[l], take(4))
@@ -891,9 +1193,9 @@
         return lax.fori_loop(0, rows // step, lambda i, c: body(pl.ds(pl.multiple_of(i * step, step), step), c), init)
 
     s.greet()
-    bk.start()
-    mx.start()
-    ups.start()
+    tk.start()
+    dws.start()
+    f_up.start()
     for c in loads:
         c.start()
     dk[...] = jnp.zeros_like(dk)
@@ -901,30 +1203,17 @@
     gains = small[...].astype(f32).T
     mine = meta[...].T
     valid_cols[...] = jnp.broadcast_to(mine[:, 1:2], valid_cols.shape)
-    bk.ready()
-    pass_on(bk)
-    mx.ready()
-    mx.relay()
-    dws.start()
-    hand_back(bk, back_swap, ret_back)
-    tk.start()
-    dn.start()
-    ups.relay()
-    totals(mx, grad_mix)
-    for c in loads:
-        c.wait()
-    back_swap.arrive()
-    grad_mix[...] += mm(place[...], got_back[...])
 
     def mid(at, gain_sum):
         normed_v, scale = norm_stats(tokens[at, :].astype(f32) + attention_out[at, :])
-        grad = grad_mix[at, :]
+        grad = grad_mix_in[at, :]
         value = cot[at, :].astype(f32) * valid_cols[at, 0:1] + norm_back(normed_v, scale, gains[1:2, :], grad)
         grad_mid[at, :] = value
         grad_attn[at, :] = value.astype(bf16)
         return gain_sum + jnp.sum(grad * normed_v, axis=0, keepdims=True)
 
     mixer_gain_grad = over_rows(mid, jnp.zeros((1, width), f32))
+    loads[0].wait()
     grad_mixed[...] = mm(grad_attn[...], output_all[...], 1, 1).astype(bf16)
     for l in range(lanes):
         heads.send(l)
@@ -939,7 +1228,8 @@
     lax.fori_loop(0, lanes, out_grad, 0)
     gos.start()
     tk.ready()
-    dws.relay()
+    for c in loads[1:]:
+        c.wait()
     heads.arrive()
     doc_cols = [meta_all[l].T[:, 0:1] for l in range(lanes)]
     for tile in range(lanes):
@@ -950,8 +1240,7 @@
             gos.ready()
             gos.relay()
         if tile == 2:
-            dn.ready()
-            dn.relay()
+            f_up.forward()
     for pair in range(head_cols // PAIR):
         grad_qkv[:, head_cols + pair * PAIR : head_cols + (pair + 1) * PAIR] = dk[pair].astype(bf16)
         grad_qkv[:, 2 * head_cols + pair * PAIR : 2 * head_cols + (pair + 1) * PAIR] = dv[pair].astype(bf16)
@@ -975,10 +1264,7 @@
     gns.relay()
     totals(gos, gl)
     gls.start()
-    ups.finish(mine_up)
-    f_up.start()
     gas.relay()
-    totals(dn, grad_mix)
     tok_swap.arrive()
     gls.relay()
 
@@ -992,7 +1278,7 @@
         columns = lax.broadcasted_iota(jnp.int32, logits.shape, 1)
         route = valid_cols[at, 1:2].astype(jnp.int32)
         chosen = jnp.sum(jnp.where(columns == 4 + route, router, 0.0), axis=1, keepdims=True)
-        ffn = blend[:, 2:3] * chosen * mm(place[at, :], got_tok[...]) + blend[:, 3:4] * grad_mix[at, :]
+        ffn = blend[:, 2:3] * chosen * mm(place[at, :], got_tok[...]) + blend[:, 3:4] * dense_out[at, :].astype(f32)
         full = residual + ffn
         layer_out[at, :] = full.astype(bf16)
         valid = valid_cols[at, 0:1]
@@ -1023,7 +1309,6 @@
         value = jnp.where(feature == 0, attend_gain_grad[:, here], value)
         sm[w] = jnp.where(feature == 1, mixer_gain_grad[:, here], value)
     sms.start()
-    f_up.forward()
     dws.finish(mine_down)
     f_down.start()
     sms.relay()
@@ -1039,7 +1324,7 @@
     for task in gathers:
         task.arrive()
     small_out[...] = sum([sm_all[l] for l in range(1, lanes)], sm_all[0])
-    for task in [bk, tk, mx, dn, gos, gns, ups, dws, gas, gls, sms, back_swap, tok_swap, heads] + gathers:
+    for task in [tk, gos, gns, dws, gas, gls, sms, tok_swap, heads] + gathers:
         task.sent()
 
 
@@ -1051,7 +1336,7 @@
     everyone = rows * lanes
     head_cols = width // lanes
     shard = width // groups
-    hidden = placed[4].shape[1]
+    hidden = inputs[-2].shape[1]
     vmem, anywhere = pl.BlockSpec(memory_space=pltpu.VMEM), pl.BlockSpec(memory_space=pl.ANY)
     dma = pltpu.SemaphoreType.DMA
     of = jax.ShapeDtypeStruct
@@ -1066,21 +1351,20 @@
         return ([low(Z, shard, n)] if held else [low(width, n)]) + [low(X - 1, Z, shard, n), low(Z - 1, shard, n)]
 
     scratch = [low(everyone, 3 * head_cols), low(width, width), low(width, 3 * head_cols), low(everyone, width)]
-    scratch[0], scratch[1] = low(everyone, 3 * head_cols), low(width, width)
-    scratch += group_bufs(groups, slots, width) * 2 + group_bufs(rows // 64, 64, width) * 2
+    scratch += group_bufs(groups, slots, width)
     scratch += group_bufs(width // 64, 64, head_cols, False) + group_bufs(rows // 64, 64, width, False)
-    scratch += lane_bufs(hidden) + lane_bufs(width) + lane_bufs(3 * head_cols, False) + lane_bufs(head_cols, False)
+    scratch += [low(Z - 1, shard, width)] + lane_bufs(3 * head_cols, False) + lane_bufs(head_cols, False)
     scratch += [wide(groups, SMALL, shard), wide(X - 1, Z, SMALL, shard), wide(Z - 1, SMALL, shard)]
     scratch += [wide(SMALL, shard), wide(lanes, SMALL, shard)]
-    scratch += [low(groups * slots, width)] * 4
+    scratch += [low(groups * slots, width)] * 2
     scratch += [wide(rows, width), wide(rows, width), low(rows, width), low(rows, width)]
     scratch += [low(everyone, head_cols), low(everyone, 3 * head_cols), wide(everyone, Q_TILE)]
     scratch += [wide(pairs, everyone, PAIR)] * 2 + [wide(rows, SMALL)]
-    scratch += [low(shard, 3 * head_cols), low(shard, head_cols), low(shard, hidden), low(shard, width)]
+    scratch += [low(shard, 3 * head_cols), low(shard, head_cols), low(shard, width)]
     scratch += [dma((4,))]
-    scratch += GroupScatter.sems(lanes, groups) * 2 + GroupScatter.sems(lanes, 1) * 4
-    scratch += LaneScatter.sems(groups, X) * 5
-    scratch += LaneSwap.sems(groups) * 2 + GroupSwap.sems(lanes)
+    scratch += GroupScatter.sems(lanes, groups) + GroupScatter.sems(lanes, 1) * 2
+    scratch += [dma((Z,))] * 2 + LaneScatter.sems(groups, X) * 3
+    scratch += LaneSwap.sems(groups) + GroupSwap.sems(lanes)
     scratch += GroupGather.sems(lanes) * 5
     outs = [
         (of((rows, width), bf16), vmem),
@@ -1142,16 +1426,16 @@
     small = jnp.concatenate(
         [attend_gain[:, None], mixer_gain[:, None], blend_weight, router_weight,
          jnp.zeros((shard, SMALL - 4 - experts), bf16)], axis=1)
-    meta = jnp.stack([doc_ids, valid_mask, routes[:, 0]]).astype(f32)
-    meta = jnp.pad(meta, ((0, 5), (0, 0)))
+    meta_in = jnp.stack([doc_ids, valid_mask, routes[:, 0]]).astype(f32)
+    meta_in = jnp.pad(meta_in, ((0, 5), (0, 0)))
     up_mine = up_weight
     if fine % 128:
         up_mine = lax.dynamic_index_in_dim(up_weight.reshape(shard, groups, lanes, fine), lane, 2, keepdims=False)
         up_mine = up_mine.reshape(shard, groups * fine)
     (
         normed_attend, qkv, lse, attn_mixed, attention_out, mix_all, small, meta_all, place,
-        attend_full, output_full, got_mix, got_cot, cot_all, up_full, down_full,
-    ) = front(groups, lanes, local, cap, slots, tokens, cotangent, meta, small, attend_weight, output_weight, up_mine, down_weight)
+        attend_full, output_full, packed_cot, got_mix, cot_all, up_full, down_full,
+    ) = front(groups, lanes, local, cap, slots, tokens, cotangent, meta_in, small, attend_weight, output_weight, up_mine, down_weight)
     doc_col = meta_all[:, 0].reshape(all_rows, 1)
     valid_all = meta_all[:, 1].reshape(all_rows, 1)
     attend_gain_row = small[:, 0].astype(f32)
@@ -1167,6 +1451,31 @@
 
     valid = valid_mask.astype(f32)[:, None]
     grad_layer = cotangent.astype(f32) * valid
+
+    def widen(gathered, parts):
+        full = gathered.reshape(lanes, shard, parts, -1)
+        return full.transpose(1, 2, 0, 3).reshape(shard, -1).astype(f32)
+
+    if all_rows * width <= 2**20 and shard % 128 == 0 and cap % 8 == 0 and slots == local * cap and local == 2 and lanes * groups * cap <= all_rows:
+        grad_mix, dense_out, grad_small, mine_up, down_half, tok_part, mix_e, grad_e, act_e, hidden_e = middle(
+            groups, lanes, local, cap, experts, slots, (small, meta_all, place),
+            (mix_all, cot_all, up_full, down_full, got_mix, packed_cot, expert_up, expert_down))
+        layer_out, grad_tokens, small_out, out_attend, out_output, out_up, out_down = back(
+            groups, lanes, experts, slots,
+            (tokens, cotangent, meta_in, small, attention_out, attn_mixed, place, meta_all, lse, grad_small, grad_mix,
+             dense_out, mine_up, down_half),
+            (tok_part, qkv, output_full, attend_full, normed_attend))
+        grad_expert_up = jnp.einsum("etd,etf->edf", mix_e, hidden_e, preferred_element_type=f32)
+        grad_expert_down = jnp.einsum("etf,etd->efd", act_e, grad_e, preferred_element_type=f32)
+        sums, small_out = small_out[SMALL - 1], small_out.T
+        root_means = jnp.sqrt(sums[:4] / (jnp.maximum(sums[4], 1.0) * width))
+        return (
+            layer_out, grad_tokens, small_out[:, 0], widen(out_attend, 3), widen(out_output, 1), small_out[:, 1],
+            small_out[:, 4 : 4 + experts], small_out[:, 2:4], widen(out_up, groups),
+            out_down.reshape(-1, width).astype(f32), grad_expert_up, grad_expert_down, root_means,
+        )
+
+    got_cot = group_gather(lane_swap(packed_cot.reshape(groups, slots, width))[None])
 
     def coefficients(mix_rows):
         logits = mm(mix_rows, mix_cols)
@@ -1221,29 +1530,6 @@
         down_grads.append(mm(act, grad_tok, 0, 0))
         up_grads.append(mm(mix_e[e], grad_hidden, 0, 0))
     grad_expert_up, grad_expert_down = jnp.stack(up_grads), jnp.stack(down_grads)
-    def widen(gathered, parts):
-        full = gathered.reshape(lanes, shard, parts, -1)
-        return full.transpose(1, 2, 0, 3).reshape(shard, -1).astype(f32)
-
-    if all_rows * width <= 2**20 and shard % 128 == 0:
-        def chunked(part):
-            return part.astype(bf16).reshape(lanes, rows // 64, 64, width)
-
-        def slotted(parts):
-            return by_slot(jnp.stack(parts).astype(bf16)).reshape(lanes, groups, slots, width)
-
-        layer_out, grad_tokens, small_out, out_attend, out_output, out_up, out_down = back(
-            groups, lanes, experts, slots,
-            (tokens, cotangent, meta, small, attention_out, attn_mixed, place, meta_all, lse, grad_small),
-            (chunked(grad_mix_part), chunked(dense_part), slotted(back_parts), slotted(tok_parts), grad_up.astype(bf16),
-             grad_down.astype(bf16), qkv, output_full, attend_full, normed_attend))
-        sums, small_out = small_out[SMALL - 1], small_out.T
-        root_means = jnp.sqrt(sums[:4] / (jnp.maximum(sums[4], 1.0) * width))
-        return (
-            layer_out, grad_tokens, small_out[:, 0], widen(out_attend, 3), widen(out_output, 1), small_out[:, 1],
-            small_out[:, 4 : 4 + experts], small_out[:, 2:4], widen(out_up, groups),
-            out_down.reshape(-1, width).astype(f32), grad_expert_up, grad_expert_down, root_means,
-        )
     grad_small = grad_small.T
     expert_back = give_back(by_slot(jnp.stack(back_parts)))
     expert_tok = give_back(by_slot(jnp.stack(tok_parts)))

time: 431 us -> 362 us (0.84)
  matrix products: 66.7 us -> 13.5 us
  Pallas kernels: 300 us -> 317 us
  other arithmetic: 20.6 us -> 4.55 us
  local copies, waits for them, and re-layouts: 34.9 us -> 19.1 us
    pallas_call x0 -> x1, Pallas kernels: none -> 104 us  [middle(): pl.pallas_call(functools.partial(middle_kernel, groups, lanes, local, cap...]
    pallas_call x1, Pallas kernels: 157 us -> 91.3 us  [back(): pl.pallas_call(functools.partial(back_kernel, groups, lanes, experts), ou...]
    dot_general x27 -> x2, matrix products: 66.7 us -> 13.5 us  [the longest x1 7.76 us: per_device(): jnp.einsum('etd,etf->edf', mix_e, hidden_e, preferred_element_type=f32)]
    pallas_call x1, Pallas kernels: 144 us -> 122 us  [front(): pl.pallas_call(functools.partial(front_kernel, groups, lanes, local, cap,...]
    unnamed x89 -> x23, local copies, waits for them, and re-layouts: 18 us -> 7.09 us
    another operation x3 -> x0, other arithmetic: 10.5 us -> none  [the longest x1 4.27 us: per_device(): jnp.stack(up_grads)]
where the time goes in v3:
time: 362 us; the launch traced here: 356 us
  Pallas kernels  317 us (88%)
  local copies, waits for them, and re-layouts  19.1 us (5%)
  matrix products  13.5 us (4%)
  other arithmetic  4.55 us (1%)
    pallas_call x1, Pallas kernels, front(): pl.pallas_call(functools.partial(front_kernel, groups, lanes, local, cap,...  122 us
    pallas_call x1, Pallas kernels, middle(): pl.pallas_call(functools.partial(middle_kernel, groups, lanes, local, cap...  104 us
    pallas_call x1, Pallas kernels, back(): pl.pallas_call(functools.partial(back_kernel, groups, lanes, experts), ou...  91.3 us
    dot_general x1, matrix products, per_device(): jnp.einsum('etd,etf->edf', mix_e, hidden_e, preferred_element_type=f32)  7.76 us

profile of v3, /device:TPU:0, one launch (start us, length us, event | category | flops | bytes accessed | tf_op | source)
XLA Modules:
  0.0 355.7 jit_solution(11698815192157028427)
XLA Ops:
  0.6 0.7 add_convert_fusion
  1.4 0.6 pad.4.meta
  2.0 0.8 copy.46
  2.8 0.8 copy.47
  3.5 0.8 copy.49
  4.3 0.8 copy.48
  5.1 0.7 concatenate.3.small
  5.9 122.0 %front.1 = (bf16[1024,1024]{1,0:T(8,128)(2,1)}, bf16[1024,768]{1,0:T(8,128)(2,1)}, f32[2,2,1024]{2,1,0:T(2,128)}, bf16[256,1024]{1,0:T(8,128)(2,1)}, f32[256,102...) custom-call(bf16[256,1024]{1,0:T(8,128)(2,1)} %tokens.3, ...), custom_call_target="tpu_custom_call" | custom-call | flops 8000000000 | bytes 100000000 | tf_op jit(solution)/shard_map/front/pallas_call | solution.py:593
  127.9 103.5 %middle.1 = (f32[256,1024]{1,0:T(8,128)}, bf16[256,1024]{1,0:T(8,128)(2,1)}, f32[128,1024]{1,0:T(8,128)}, bf16[128,1024]{1,0:T(8,128)(2,1)}, bf16[4,128,1024]{2,...) custom-call(bf16[1024,128]{1,0:T(8,128)(2,1)} %get-tuple-element.46., ...), custom_call_target="tpu_custom_call" | custom-call | flops 35000000512 | bytes 100000000 | tf_op jit(solution)/shard_map/middle/pallas_call | solution.py:1113
  231.4 91.3 %back.1 = (bf16[256,1024]{1,0:T(8,128)(2,1)}, bf16[256,1024]{1,0:T(8,128)(2,1)}, f32[128,128]{1,0:T(8,128)}, bf16[4,128,768]{2,1,0:T(8,128)(2,1)}, bf16[4,128,25...) custom-call(bf16[256,1024]{1,0:T(8,128)(2,1)} %tokens.3, bf16[256,1024]{1,0:T(8,128)(2,1)} %cot.3, ...), custom_call_target="tpu_custom_call" | custom-call | flops 8000000000 | bytes 100000000 | tf_op jit(solution)/shard_map/back/pallas_call | solution.py:1378
  322.7 0.0 copy-start.2
  322.8 1.3 slice.28
  324.7 1.2 sqrt_bitcast_fusion
  325.9 1.2 slice.32
  327.2 1.3 slice_bitcast_fusion
  328.5 1.3 slice.31
  329.8 1.0 convert_bitcast_fusion
  330.8 0.2 copy.52
  331.0 1.0 copy.57
  332.0 0.0 copy-done.2
  332.0 0.3 copy.50
  332.2 0.1 copy.51
  332.4 0.0 copy-start.1
  332.4 1.6 copy.56
  334.0 0.0 copy-done.1
  334.0 0.3 copy.60
  334.3 0.1 bitcast_bitcast_fusion
  334.4 1.4 copy.53
  335.8 0.0 copy-start
  335.8 1.9 reshape.59
  337.6 0.0 copy-done
  337.6 0.0 copy-start.7
  337.6 1.6 bitcast_convert_fusion
  339.3 1.0 copy-done.7
  340.3 0.0 copy-start.5
  340.3 0.0 copy-start.6
  340.3 7.8 %fusion = f32[2,1024,1024]{2,1,0:T(8,128)} fusion(bf16[2,768,1024]{2,1,0:T(8,128)(2,1)S(1)} %copy-done.7, bf16[2,768,1024]{2,1,0:T(8,128)(2,1)} %get-tuple-element.76), kind=kOutput, calls=%fused_computation.7 | convolution fusion | flops 3221225472 | bytes 14680064 | tf_op jit(solution)/shard_map/etd,etf->edf/dot_general | solution.py:1468
  348.0 0.0 copy-done.5
  348.0 0.0 copy-done.6
  348.0 0.0 copy-start.4
  348.1 0.0 copy-start.3
  348.1 5.8 %fusion.1 = f32[2,1024,1024]{2,1,0:T(8,128)} fusion(bf16[2,768,1024]{2,1,0:T(8,128)(2,1)S(1)} %copy-done.6, bf16[2,768,1024]{2,1,0:T(8,128)(2,1)S(1)} %copy-done.5), kind=kOutput, calls=%fused_computation.8 | convolution fusion | flops 3221225472 | bytes 14680064 | tf_op jit(solution)/shard_map/etf,etd->efd/dot_general | solution.py:1469
  353.8 0.0 copy-done.4
  353.9 0.8 copy.63
  354.6 0.0 copy-done.3
  354.6 0.8 copy.64
  (1 shorter events, 0.0 us)
Async XLA Ops:
  322.7 9.2 %copy-start.2 = (bf16[4,128,768]{2,1,0:T(8,128)(2,1)S(1)}, bf16[4,128,768]{2,1,0:T(8,128)(2,1)}, u32[]{:S(2)}) copy-start(bf16[4,128,768]{2,1,0:T(8,128)(2,1)} %get-tuple-element.71) | copy-start | bytes 2359300
  332.4 1.6 copy-start.1
  335.8 1.9 copy-start
  337.6 2.6 copy-start.7
  340.3 7.8 %copy-start.5 = (bf16[2,768,1024]{2,1,0:T(8,128)(2,1)S(1)}, bf16[2,768,1024]{2,1,0:T(8,128)(2,1)}, u32[]{:S(2)}) copy-start(bf16[2,768,1024]{2,1,0:T(8,128)(2,1)} %get-tuple-element.78) | copy-start | bytes 9437188
  340.3 7.8 %copy-start.6 = (bf16[2,768,1024]{2,1,0:T(8,128)(2,1)S(1)}, bf16[2,768,1024]{2,1,0:T(8,128)(2,1)}, u32[]{:S(2)}) copy-start(bf16[2,768,1024]{2,1,0:T(8,128)(2,1)} %get-tuple-element.77) | copy-start | bytes 9437188
  348.0 5.8 %copy-start.4 = (bf16[256,1024]{1,0:T(8,128)(2,1)S(1)}, bf16[256,1024]{1,0:T(8,128)(2,1)}, u32[]{:S(2)}) copy-start(bf16[256,1024]{1,0:T(8,128)(2,1)} %get-tuple-element.120) | copy-start | bytes 1572868
  348.1 6.6 %copy-start.3 = (bf16[256,1024]{1,0:T(8,128)(2,1)S(1)}, bf16[256,1024]{1,0:T(8,128)(2,1)}, u32[]{:S(2)}) copy-start(bf16[256,1024]{1,0:T(8,128)(2,1)} %get-tuple-element.121) | copy-start | bytes 1572868

commit v4 on v3

--- a/solution.py
+++ b/solution.py
@@ -191,6 +191,9 @@
     def w_peer(self, d):
         return lax.rem(self.g + d, self.W)
 
+    def w_at(self, p):
+        return lax.rem(self.g + 1 + p, self.W)
+
     def l_peer(self, d):
         return lax.rem(self.l + d, self.L)
 
@@ -237,12 +240,18 @@
     def own(self):
         return pltpu.make_async_copy(self.src, self.place(self.s.g), self.own_sem.at[0])
 
-    def start(self):
+    def start_z(self):
         for d in range(1, self.s.Z):
             self.z_copy(d).start()
+
+    def start_x(self):
         for e in range(1, self.s.X):
             self.x_copy(0, e).start()
         self.own().start()
+
+    def start(self):
+        self.start_z()
+        self.start_x()
 
     def forward(self):
         for d in range(1, self.s.Z):
@@ -265,6 +274,82 @@
                 self.x_copy(d, e).wait_send()
 
 
+class LineGather:
+    def __init__(self, spot, src, place, sems):
+        self.s, self.src, self.place = spot, src, place
+        self.z_sem, self.x_sem, self.r_sem, self.own_sem = sems
+
+    @staticmethod
+    def sems(W, X):
+        dma = pltpu.SemaphoreType.DMA
+        return [dma((W // X, 2)), dma((W // X, 2, X)), dma((W,)), dma((1,))]
+
+    def home(self, z):
+        return self.place(z * self.s.X + self.s.x)
+
+    def exists(self, z):
+        return (z >= 0) & (z < self.s.Z)
+
+    def z_copy(self, k, side):
+        s, sign = self.s, 2 * side - 1
+        z = s.z + sign * k
+        src = self.src if k == 0 else self.home(z)
+        return remote(src, self.home(z), self.z_sem.at[k, side], self.r_sem.at[z * s.X + s.x], (s.z - sign) * s.X + s.x, s.l)
+
+    def x_copy(self, k, side, e):
+        s = self.s
+        z = s.z + (2 * side - 1) * k
+        src = self.src if k == 0 else self.home(z)
+        return remote(src, self.home(z), self.x_sem.at[k, side, e], self.r_sem.at[z * s.X + s.x], s.x_peer(e), s.l)
+
+    def got(self, w):
+        s = self.s
+        remote(self.src, self.place(w), self.z_sem.at[0, 0], self.r_sem.at[w], s.x_peer(1), s.l).wait_recv()
+
+    def own(self):
+        return pltpu.make_async_copy(self.src, self.place(self.s.g), self.own_sem.at[0])
+
+    def each(self, k, act):
+        s = self.s
+        for side in range(2):
+            sign = 2 * side - 1
+            onward = self.exists(s.z - sign)
+            if k == 0:
+                pl.when(onward)(lambda side=side: act(self.z_copy(0, side)))
+                continue
+
+            @pl.when(self.exists(s.z + sign * k))
+            def _(side=side, sign=sign, onward=onward):
+                if act is None:
+                    self.got((s.z + sign * k) * s.X + s.x)
+                go = (lambda c: c.start()) if act is None else act
+                pl.when(onward)(lambda: go(self.z_copy(k, side)))
+                for e in range(1, s.X):
+                    go(self.x_copy(k, side, e))
+
+    def start(self):
+        self.each(0, lambda c: c.start())
+        for e in range(1, self.s.X):
+            self.x_copy(0, 0, e).start()
+        self.own().start()
+
+    def hop(self, k):
+        self.each(k, None)
+
+    def arrive(self):
+        s = self.s
+        for d in range(s.Z):
+            for e in range(1, s.X):
+                self.got(s.zx_peer(d, e))
+        self.own().wait()
+
+    def sent(self):
+        for k in range(self.s.Z):
+            self.each(k, lambda c: c.wait_send())
+        for e in range(1, self.s.X):
+            self.x_copy(0, 0, e).wait_send()
+
+
 class GroupGather:
     def __init__(self, spot, src, place, sems, own=True):
         self.s, self.src, self.place, self.has_own = spot, src, place, own
@@ -405,9 +490,9 @@
 def front_kernel(
     groups, lanes, local, cap, slots,
     tokens, cot, meta, small, attend_w, output_w, up_w, down_w,
-    normed_out, qkv, lse, attn_mixed, attention_out, mix_all, small_all, meta_all, place,
-    attend_all, output_all, packed_cot, got_mix, cot_all, up_all, down_all,
-    tok_all, attend_mine, up_mine, mixed, mask, vt, packed_mix, stage_sem, spread_y, spread_c, spread_r, *sems,
+    lse, attn_mixed, attention_out, small_all, meta_all, place,
+    normed_to, qkv_to, attend_to, output_to, mix_to, got_mix, cot_mine, cot_all, up_all, down_all,
+    normed_out, qkv, attend_all, output_all, mix_all, tok_all, up_mine, mixed, mask, vt, packed_mix, packed_cot, out_sem, stage_sem, spread_y, spread_c, spread_r, *sems,
 ):
     s = Spot(groups, lanes)
     rows, width = tokens.shape
@@ -427,22 +512,17 @@
     def cols(i):
         return pl.ds(pl.multiple_of(i * head_cols, head_cols), head_cols)
 
-    staged = [
-        pltpu.make_async_copy(
-            attend_w.at[:, pl.ds(pl.multiple_of(p * width + s.l * head_cols, head_cols), head_cols)],
-            attend_mine.at[:, pl.ds(p * head_cols, head_cols)], stage_sem.at[p])
-        for p in range(3)
-    ]
+    staged = []
     if up_w.shape[1] != up_mine.shape[1]:
         fine = up_mine.shape[1] // groups
         staged += [
             pltpu.make_async_copy(
                 up_w.at[:, pl.ds(pl.multiple_of((w * lanes + s.l) * fine, fine), fine)],
-                up_mine.at[:, pl.ds(w * fine, fine)], stage_sem.at[3 + w])
+                up_mine.at[:, pl.ds(w * fine, fine)], stage_sem.at[w])
             for w in range(groups)
         ]
     else:
-        staged += [pltpu.make_async_copy(up_w, up_mine, stage_sem.at[3])]
+        staged += [pltpu.make_async_copy(up_w, up_mine, stage_sem.at[0])]
     for c in staged:
         c.start()
 
@@ -451,13 +531,20 @@
     cots = GroupGather(s, cot, blocks(cot_all, rows), take(4))
     mix = GroupGather(s, blocks(mix_all, rows)(s.l), blocks(mix_all, rows), take(4), own=False)
     outs = GroupGather(s, output_all.at[:, cols(s.l)], lambda l: output_all.at[:, cols(l)], take(4), own=False)
-    att = LaneGather(s, attend_mine, blocks(attend_all, shard), take(4))
+    atts = [
+        LineGather(
+            s, attend_w.at[:, pl.ds(pl.multiple_of(p * width + s.l * head_cols, head_cols), head_cols)],
+            lambda w, p=p: attend_all.at[pl.ds(pl.multiple_of(w * shard, shard), shard), pl.ds(p * head_cols, head_cols)],
+            take(4))
+        for p in range(3)
+    ]
     sml = LaneGather(s, small, blocks(small_all, shard), take(4))
-    out = LaneGather(s, output_w.at[:, cols(s.l)],
+    out = LineGather(s, output_w.at[:, cols(s.l)],
                      lambda w: output_all.at[pl.ds(pl.multiple_of(w * shard, shard), shard), cols(s.l)], take(4))
-    up = LaneGather(s, up_mine, blocks(up_all, shard), take(4))
-    down = LaneGather(s, down_w.at[pl.ds(pl.multiple_of(s.l * depth, depth), depth)], blocks(down_all, depth), take(4))
+    up = LineGather(s, up_mine, blocks(up_all, shard), take(4))
+    down = LineGather(s, down_w.at[pl.ds(pl.multiple_of(s.l * depth, depth), depth)], blocks(down_all, depth), take(4))
     swap = GroupSwap(s, blocks(mixed, rows), lambda l: attn_mixed.at[:, cols(l)], take(2))
+    cot_swap = LaneSwap(s, blocks(packed_cot, slots), lambda w: cot_mine.at[w], take(2))
     mix_swap = LaneSwap(s, blocks(packed_mix, slots), lambda w: got_mix.at[s.l, w], take(2))
 
     def spread(d):
@@ -468,13 +555,12 @@
     mix_spread = [spread(d) for d in range(groups)]
 
     s.greet()
-    for c in staged[:3]:
-        c.wait()
     sml.start()
     met.start()
     tok.start()
-    att.start()
-    for c in staged[3:]:
+    for att in atts:
+        att.start()
+    for c in staged:
         c.wait()
     mine = meta[...].T
     valid, route = mine[:, 1:2], mine[:, 2:3].astype(jnp.int32)
@@ -486,27 +572,43 @@
     spots = (slot == lax.broadcasted_iota(jnp.int32, (rows, groups * slots), 1)).astype(f32)
     place[...] = spots.astype(bf16)
     packed_cot[...] = mm((spots * valid).astype(bf16), cot[...], 0, 0).astype(bf16)
+    def give(ref, to, k):
+        done.append(pltpu.make_async_copy(ref, to, out_sem.at[k]))
+        done[-1].start()
+
+    done = []
     sml.forward()
+    for att in atts:
+        att.hop(1)
     met.forward()
+    tok.forward()
+    cots.start()
+    for k in range(2, s.Z):
+        for att in atts:
+            att.hop(k)
+    out.start()
+    up.start()
     sml.arrive()
     met.arrive()
-    tok.forward()
-    att.forward()
-    cots.start()
+    gains = small_all[...].astype(f32).T
     tok.arrive()
-    gains = small_all[...].astype(f32).T
     rows_norm(tok_all, gains[0:1, :], normed_out, rows * lanes)
-    att.arrive()
-    out.start()
-    up.start()
+    give(normed_out, normed_to, 0)
+    for att in atts:
+        att.arrive()
+    give(attend_all, attend_to, 1)
 
     def project(i, carry):
         at = pl.ds(pl.multiple_of(i * Q_TILE, Q_TILE), Q_TILE)
         qkv[at, :] = mm(normed_out[at, :], attend_all[...]).astype(bf16)
         return carry
 
+    for k in range(1, s.Z - 1):
+        out.hop(k)
     lax.fori_loop(0, rows * lanes // Q_TILE, project, 0)
-    out.forward()
+    give(qkv, qkv_to, 2)
+    out.hop(s.Z - 1)
+    up.hop(1)
     doc_cols = [meta_all[l].T[:, 0:1] for l in range(lanes)]
     for tile in range(lanes):
         attend_tile(tile, qkv, doc_cols, mixed, lse, mask, vt)
@@ -514,12 +616,17 @@
         if tile == 0:
             out.arrive()
             outs.start()
-        if tile == 1:
+        if tile == lanes - 3:
+            up.hop(2)
+            down.start()
+        if tile == lanes - 2:
+            for k in range(3, s.Z):
+                up.hop(k)
             cots.forward()
+    down.hop(1)
     outs.forward()
-    up.forward()
-    down.start()
     outs.arrive()
+    give(output_all, output_to, 3)
     swap.arrive()
     attention_out[...] = mm(attn_mixed[...], output_all[...])
     gain = small_all[...].astype(f32).T[1:2, :]
@@ -533,25 +640,34 @@
 
     lax.fori_loop(0, rows // 64, mid, 0)
     mix.start()
+    down.hop(2)
     packed_mix[...] = mm(place[...], mix_all[pl.ds(base, rows), :], 0, 0).astype(bf16)
     mix_swap.start()
-    down.forward()
     mix.forward()
+    for k in range(3, s.Z):
+        down.hop(k)
     for d in range(groups):
         if d:
             mix_swap.got(s.w_peer(groups - d))
         else:
             mix_swap.own().wait()
         mix_spread[d].start()
+    cot_swap.start()
+    mix.arrive()
+    give(mix_all, mix_to, 4)
+    for task in [tok, met, cots, outs, sml, out, up, swap, *atts]:
+        task.sent()
     for task in mix_spread:
         task.forward()
-    mix.arrive()
     for task in mix_spread:
         task.arrive()
     cots.arrive()
     up.arrive()
     down.arrive()
-    for task in [tok, met, cots, mix, outs, att, sml, out, up, down, swap, mix_swap] + mix_spread:
+    cot_swap.arrive()
+    for c in done:
+        c.wait()
+    for task in [mix, down, mix_swap, cot_swap] + mix_spread:
         task.sent()
 
 
@@ -569,23 +685,25 @@
     sems = []
     for _ in range(5):
         sems += GroupGather.sems(lanes)
-    for _ in range(5):
-        sems += LaneGather.sems(groups, X)
-    sems += GroupSwap.sems(lanes) + LaneSwap.sems(groups)
+    for _ in range(3):
+        sems += LineGather.sems(groups, X)
+    sems += LaneGather.sems(groups, X)
+    for _ in range(3):
+        sems += LineGather.sems(groups, X)
+    sems += GroupSwap.sems(lanes) + LaneSwap.sems(groups) * 2
     outs = [
-        (of((everyone, width), bf16), vmem),
-        (of((everyone, 3 * head_cols), bf16), vmem),
         (of((head_cols // PAIR, 2, everyone), f32), vmem),
         (of((rows, width), bf16), vmem),
         (of((rows, width), f32), vmem),
-        (of((everyone, width), bf16), vmem),
         (of((width, SMALL), bf16), vmem),
         (of((lanes, 8, rows), f32), vmem),
         (of((rows, groups * slots), bf16), vmem),
-        (of((width, 3 * head_cols), bf16), vmem),
-        (of((width, width), bf16), vmem),
-        (of((groups * slots, width), bf16), vmem),
+    ]
+    big = [(everyone, width), (everyone, 3 * head_cols), (width, 3 * head_cols), (width, width), (everyone, width)]
+    outs += [(of(shape, bf16), anywhere) for shape in big]
+    outs += [
         (of((lanes, groups, slots, width), bf16), anywhere),
+        (of((groups, slots, width), bf16), anywhere),
         (of((everyone, width), bf16), anywhere),
         (of((width, hidden), bf16), anywhere),
         (of((hidden, width), bf16), anywhere),
@@ -595,15 +713,16 @@
         out_shape=[o for o, _ in outs],
         in_specs=[vmem] * 4 + [anywhere] * 4,
         out_specs=[p for _, p in outs],
-        scratch_shapes=[
+        scratch_shapes=[pltpu.VMEM(shape, bf16) for shape in big] + [
             pltpu.VMEM((everyone, width), bf16),
-            pltpu.VMEM((shard, 3 * head_cols), bf16),
             pltpu.VMEM((shard, hidden), bf16),
             pltpu.VMEM((everyone, head_cols), bf16),
             pltpu.VMEM((everyone, Q_TILE), f32),
             pltpu.VMEM((head_cols // PAIR, PAIR, everyone), bf16),
             pltpu.VMEM((groups * slots, width), bf16),
-            dma((3 + groups,)),
+            pltpu.VMEM((groups * slots, width), bf16),
+            dma((5,)),
+            dma((groups,)),
             dma((groups, Y)),
             dma((groups, Y)),
             dma((groups, lanes)),
@@ -623,16 +742,17 @@
         dst[at, :] = total.astype(dst.dtype)
         return carry
 
+    step = step if dst.shape[0] % step == 0 else dst.shape[0]
     lax.fori_loop(0, dst.shape[0] // step, body, 0)
 
 
 class GroupScatter:
-    def __init__(self, spot, part, held, from_core, from_y, sems, fine):
+    def __init__(self, spot, part, held, from_core, from_y, sems, fine, chunks=None):
         self.s, self.part, self.from_core, self.from_y, self.fine = spot, part, from_core, from_y, fine
         self.staged = held is not None
         self.held = (lambda d: held.at[d]) if self.staged else (lambda d: part(spot.y_peer(d)))
         self.stage_sem, self.cs_sem, self.cr_sem, self.ys_sem, self.yr_sem = sems
-        self.chunks = from_core.shape[1]
+        self.chunks = chunks or from_core.shape[1]
 
     @staticmethod
     def sems(L, chunks):
@@ -818,6 +938,31 @@
     lax.fori_loop(0, cols // PAIR, pair_step, 0)
 
 
+def expert_grads_kernel(x_ref, hidden_ref, act_ref, grad_ref, up_ref, down_ref):
+    up_ref[0] = mm(x_ref[0], hidden_ref[0], 0, 0)
+    down_ref[0] = mm(act_ref[0], grad_ref[0], 0, 0)
+
+
+def expert_grads(x, hidden, act, grad):
+    local, rows, width = x.shape
+    units = hidden.shape[2]
+    tile = 256
+    tall = lambda: pl.BlockSpec((1, rows, tile), lambda e, m: (e, 0, m))
+    return pl.pallas_call(
+        expert_grads_kernel,
+        grid=(local, width // tile),
+        out_shape=[jax.ShapeDtypeStruct((local, width, units), f32), jax.ShapeDtypeStruct((local, units, width), f32)],
+        in_specs=[
+            tall(), pl.BlockSpec((1, rows, units), lambda e, m: (e, 0, 0)),
+            tall(), pl.BlockSpec((1, rows, width), lambda e, m: (e, 0, 0)),
+        ],
+        out_specs=[pl.BlockSpec((1, tile, units), lambda e, m: (e, m, 0)), pl.BlockSpec((1, tile, width), lambda e, m: (e, m, 0))],
+        compiler_params=pltpu.CompilerParams(vmem_limit_bytes=40 * 2**20),
+        cost_estimate=pl.CostEstimate(flops=4 * local * rows * width * units, bytes_accessed=3 * 10**7, transcendentals=0),
+        name="expert_grads",
+    )(x, hidden, act, grad)
+
+
 def take_from(sems):
     sems = list(sems)
 
@@ -837,11 +982,11 @@
 def middle_kernel(
     groups, lanes, local, cap, experts,
     small, meta_all, place,
-    mix_in, cot_in, up_in, down_in, got_mix_in, packed_cot, expert_up, expert_down,
+    mix_in, cot_in, up_in, down_in, got_mix_in, cot_mine, expert_up, expert_down,
     grad_mix, dense_out, grad_small, mine_up, down_half, tok_part, mix_e_out, grad_e_out, act_e_out, hidden_e_out,
     mix, cot, up, down, act, hidden, got_mix, got_cot, mix_e, grad_e, act_e, hidden_e, expert_in, expert_to,
     mx, mx_c, mx_y, dn, dn_c, dn_y, bk_c, bk_y, gu, gu_x, gu_z, gd, gd_x, ret_back, got_back, dots, coefs,
-    load_sem, out_sem, spread_y, spread_c, spread_r, *sems,
+    load_sem, out_sem, *sems,
 ):
     s = Spot(groups, lanes)
     everyone, width = mix.shape
@@ -863,20 +1008,18 @@
     def load(i, src, dst):
         return pltpu.make_async_copy(src, dst, load_sem.at[i])
 
-    cot_swap = LaneSwap(s, blocks(packed_cot, slots), lambda w: got_cot.at[s.l, w], take(2))
+    cot_spread = GroupGather(s, cot_mine, lambda l: got_cot.at[l], take(4))
     mxs = GroupScatter(s, lambda l: mx.at[l], None, mx_c, mx_y, take(5), False)
     dns = GroupScatter(s, lambda l: dn.at[l], None, dn_c, dn_y, take(5), False)
-    bks = GroupScatter(s, lambda l: got_cot.at[l], None, bk_c, bk_y, take(5), True)
+    near = groups // 2
+    bks = [
+        GroupScatter(s, lambda l, h=h: got_cot.at[l, pl.ds(h * near, near)], None, bk_c.at[h], bk_y.at[h], take(5), True, near)
+        for h in range(2)
+    ]
     ups = LaneScatter(s, blocks(gu, shard), None, gu_x, gu_z, take(5))
     dws = LaneScatter(s, blocks(gd, shard), None, gd_x, None, take(5))
     back_swap = LaneSwap(s, blocks(ret_back, slots), blocks(got_back, slots), take(2))
-    order = [(d, s.w_peer(d)) for d in [*range(1, groups), 0]]
-
-    def spread(w):
-        return GroupGather(s, got_cot.at[s.l, w], lambda l: got_cot.at[l, w],
-                           [spread_y.at[w], spread_c.at[w], spread_r.at[w], None], own=False)
-
-    spreads = [(d, s.w_peer(groups - d)) for d in range(groups)]
+
     loads = [load(i, a, b) for i, (a, b) in enumerate([
         (mix_in, mix), (up_in, up), (cot_in, cot), (down_in, down), (got_mix_in, got_mix),
         (expert_up.at[0], expert_in), (expert_down.at[0], expert_to)])]
@@ -899,7 +1042,7 @@
         return jnp.sum(dots[pl.ds(0, count), :], axis=1, keepdims=True)
 
     s.greet()
-    cot_swap.start()
+    cot_spread.start()
     for c in loads:
         c.start()
     for c in loads[:4]:
@@ -922,13 +1065,6 @@
 
     lax.fori_loop(0, width // tile, up_grad, 0)
     ups.start()
-    for d, w in spreads:
-        if d:
-            cot_swap.got(w)
-        else:
-            cot_swap.own().wait()
-        spread(w).start()
-
     def down_grad(m, carry):
         gd[part(m), :] = mm(act[:, part(m)], cot[...], 0, 0).astype(bf16)
         return carry
@@ -961,7 +1097,7 @@
             pair = []
             for i in range(2):
                 b = 2 * j + i
-                pair.append(src[b // groups, b % groups].astype(f32))
+                pair.append(src[b % lanes, s.w_at(b // lanes)].astype(f32))
             for e in range(local):
                 both = [p[e * cap : (e + 1) * cap] for p in pair]
                 dst[e, part(j, 2 * cap), :] = jnp.concatenate(both, axis=0).astype(bf16)
@@ -969,72 +1105,97 @@
 
         lax.fori_loop(0, lanes * groups // 2, body, 0)
 
-    def together(sources, dst):
+    def together(sources, dst, first=0, last=lanes * groups // 2):
         def body(j, carry):
             values = [src[part(j, 2 * cap), :].astype(f32) for src in sources]
             for i in range(2):
                 b = 2 * j + i
-                dst[b // groups, b % groups] = jnp.concatenate([v[i * cap : (i + 1) * cap] for v in values], axis=0).astype(bf16)
+                dst[b % lanes, b // lanes] = jnp.concatenate([v[i * cap : (i + 1) * cap] for v in values], axis=0).astype(bf16)
             return carry
 
-        lax.fori_loop(0, lanes * groups // 2, body, 0)
+        lax.fori_loop(first, last, body, 0)
 
     apart(got_mix, mix_e)
-    for _, w in spreads:
-        spread(w).forward()
+    cot_spread.forward()
     mxs.ready()
     mxs.relay()
-    for _, w in spreads:
-        spread(w).arrive()
+    cot_spread.arrive()
     apart(got_cot, grad_e)
 
     backs, toks = [act, hidden], [mix, cot]
-    columns = lax.broadcasted_iota(jnp.int32, (rows_e, SMALL), 1)
     outs = []
+    few = rows_e // 2
+    columns = lax.broadcasted_iota(jnp.int32, (few, SMALL), 1)
+
+    def rows_out(h, e):
+        w_to = expert_to if e == 0 else down
+        at = pl.ds(h * few, few)
+
+        def body(n, carry):
+            toks[e][at, part(n)] = mm(act_e[e, at, :], w_to[:, part(n)]).astype(bf16)
+            return carry
+
+        lax.fori_loop(0, width // tile, body, 0)
+
+    for h in range(2):
+        at = pl.ds(h * few, few)
+        for e in range(local):
+            w_in, w_to = (expert_in, expert_to) if e == 0 else (up, down)
+            if h == 0 and e:
+                for c in more_loads:
+                    c.wait()
+            x, grad = mix_e.at[e, at], grad_e.at[e, at]
+            scores = mm(x[...], small[...])
+            blend, router = picked(scores, 2, 2), picked(scores, 4, experts)
+            own = columns == 4 + s.g * local + e
+            chosen = jnp.sum(jnp.where(own, router, 0.0), axis=1, keepdims=True)
+            grad[...] = (blend[:, 2:3] * chosen * grad[...].astype(f32)).astype(bf16)
+            shares = jnp.where(own, 1.0, 0.0) - router
+            shares += blend[:, 3:4] * (jnp.where(columns == 2, 1.0, 0.0) - jnp.where(columns == 3, 1.0, 0.0))
+            coefs[pl.ds(0, few), :] = shares
+            dot = branch(x, grad, w_in, w_to, act_e.at[e, at], hidden_e.at[e, at], few)
+            logits = (dot * coefs[pl.ds(0, few), :]).astype(bf16)
+            grad_small[...] += mm(logits, x[...], 0, 0)
+
+            def rows_back(n, carry, e=e, w_in=w_in, logits=logits, at=at):
+                value = mm(hidden_e[e, at, :], w_in[part(n), :], 1, 1) + mm(logits, small[part(n), :], 1, 1)
+                backs[e][at, part(n)] = value.astype(bf16)
+                return carry
+
+            lax.fori_loop(0, width // tile, rows_back, 0)
+            if h == 0 and e == 0:
+                ups.relay()
+                dns.ready()
+                dns.relay()
+            if h == 1 and e == 0:
+                bks[0].ready()
+                for k in range(near):
+                    bks[0].relay(k)
+        if h == 0:
+            cot_spread.sent()
+        together([b.at[pl.ds(0, rows_e)] for b in backs], got_cot, h * lanes * groups // 4, (h + 1) * lanes * groups // 4)
+        bks[h].start()
+
+    def hand_back(h):
+        for k in range(near):
+            p = h * near + k
+            w = s.w_at(p)
+            bks[h].got(k)
+            ret_back[pl.ds(pl.multiple_of(w * slots, slots), slots), :] = bks[h].total(k).astype(bf16)
+            if p < groups - 1:
+                back_swap.copy(p + 1).start()
+            else:
+                back_swap.own().start()
+
+    rows_out(0, 0)
+    bks[1].ready()
+    for k in range(near):
+        bks[1].relay(k)
+    hand_back(0)
+    rows_out(0, 1)
+    rows_out(1, 0)
+    rows_out(1, 1)
     for e in range(local):
-        w_in, w_to = (expert_in, expert_to) if e == 0 else (up, down)
-        if e:
-            for c in more_loads:
-                c.wait()
-        x, grad = mix_e.at[e], grad_e.at[e]
-        scores = mm(x[...], small[...])
-        blend, router = picked(scores, 2, 2), picked(scores, 4, experts)
-        own = columns == 4 + s.g * local + e
-        chosen = jnp.sum(jnp.where(own, router, 0.0), axis=1, keepdims=True)
-        grad[...] = (blend[:, 2:3] * chosen * grad[...].astype(f32)).astype(bf16)
-        shares = jnp.where(own, 1.0, 0.0) - router
-        shares += blend[:, 3:4] * (jnp.where(columns == 2, 1.0, 0.0) - jnp.where(columns == 3, 1.0, 0.0))
-        coefs[pl.ds(0, rows_e), :] = shares
-        dot = branch(x, grad, w_in, w_to, act_e.at[e], hidden_e.at[e], rows_e)
-        logits = (dot * coefs[pl.ds(0, rows_e), :]).astype(bf16)
-        grad_small[...] += mm(logits, x[...], 0, 0)
-        if e == 0:
-            ups.relay()
-
-        def rows_back(n, carry, e=e, w_in=w_in, logits=logits):
-            value = mm(hidden_e[e], w_in[part(n), :], 1, 1) + mm(logits, small[part(n), :], 1, 1)
-            backs[e][pl.ds(0, rows_e), part(n)] = value.astype(bf16)
-            return carry
-
-        lax.fori_loop(0, width // tile, rows_back, 0)
-        if e == 0:
-            dns.ready()
-            dns.relay()
-        if e == local - 1:
-            for _, w in spreads:
-                spread(w).sent()
-            together([b.at[pl.ds(0, rows_e)] for b in backs], got_cot)
-            bks.start()
-
-        def rows_out(n, carry, e=e, w_to=w_to):
-            toks[e][pl.ds(0, rows_e), part(n)] = mm(act_e[e], w_to[:, part(n)]).astype(bf16)
-            return carry
-
-        lax.fori_loop(0, width // tile, rows_out, 0)
-        if e == local - 1:
-            bks.ready()
-            for _, w in order:
-                bks.relay(w)
         for i, (a, b) in enumerate([(mix_e, mix_e_out), (grad_e, grad_e_out), (act_e, act_e_out), (hidden_e, hidden_e_out)]):
             outs.append(pltpu.make_async_copy(a.at[e], b.at[e], out_sem.at[4 * e + i]))
             outs[-1].start()
@@ -1052,13 +1213,7 @@
         lax.fori_loop(0, scatter.chunks, body, 0)
 
     totals(mxs, grad_mix)
-    for d, w in order:
-        bks.got(w)
-        ret_back[pl.ds(pl.multiple_of(w * slots, slots), slots), :] = bks.total(w).astype(bf16)
-        if d:
-            back_swap.copy(d).start()
-        else:
-            back_swap.own().start()
+    hand_back(1)
     dws.fold(down_half)
     totals(dns, dense_out)
     ups.finish(mine_up)
@@ -1067,7 +1222,7 @@
     for c in outs:
         c.wait()
     dws.x_sent()
-    for task in [cot_swap, mxs, dns, bks, ups, back_swap]:
+    for task in [mxs, dns, *bks, ups, back_swap]:
         task.sent()
 
 
@@ -1103,12 +1258,12 @@
     scratch += [low(*expert_rows), low(*expert_rows), low(local, rows_e, units), low(local, rows_e, units)]
     scratch += [low(width, units), low(units, width)]
     scratch += [low(lanes, rows // 64, 64, width), low(Y, rows // 64, 64, width), low(Y - 1, rows // 64, 64, width)] * 2
-    scratch += [low(Y, groups, slots, width), low(Y - 1, groups, slots, width)]
+    scratch += [low(2, Y, groups // 2, slots, width), low(2, Y - 1, groups // 2, slots, width)]
     scratch += [low(width, units), low(X - 1, Z, shard, units), low(Z - 1, shard, units)]
     scratch += [low(units, width), low(X - 1, Z, shard, width)]
     scratch += [low(groups * slots, width)] * 2 + [wide(everyone, SMALL)] * 2
-    scratch += [dma((9,)), dma((4 * local + 1,)), dma((groups, Y)), dma((groups, Y)), dma((groups, lanes))]
-    scratch += LaneSwap.sems(groups) + GroupScatter.sems(lanes, 1) * 2 + GroupScatter.sems(lanes, groups)
+    scratch += [dma((9,)), dma((4 * local + 1,))]
+    scratch += GroupGather.sems(lanes) + GroupScatter.sems(lanes, 1) * 2 + GroupScatter.sems(lanes, groups // 2) * 2
     scratch += LaneScatter.sems(groups, X) * 2 + LaneSwap.sems(groups)
     return pl.pallas_call(
         functools.partial(middle_kernel, groups, lanes, local, cap, experts),
@@ -1155,7 +1310,7 @@
     gos = GroupScatter(s, lambda l: go.at[l], None, go_c, go_y, take(5), False)
     gns = GroupScatter(s, lambda l: gn.at[l], None, gn_c, gn_y, take(5), False)
     dws = ZScatter(s, lambda d: down_half.at[d], dw_z, take(2))
-    gas = LaneScatter(s, blocks(ga, shard), None, ga_x, ga_z, take(5))
+    gas = [LaneScatter(s, blocks(ga.at[p], shard), None, ga_x.at[p], ga_z.at[p], take(5)) for p in range(3)]
     gls = LaneScatter(s, blocks(gl, shard), None, gl_x, gl_z, take(5))
     sms = LaneScatter(s, lambda w: sm.at[w], None, sm_x, sm_z, take(5))
     tok_swap = LaneSwap(s, blocks(ret_tok, slots), blocks(got_tok, slots), take(2))
@@ -1165,20 +1320,20 @@
     f_up = GroupGather(s, mine_up, lambda l: all_up.at[l], take(4))
     f_down = GroupGather(s, mine_down, lambda l: all_down.at[l], take(4))
     f_small = GroupGather(s, sm_mine, lambda l: sm_all.at[l], take(4))
-    order = [(d, s.w_peer(d)) for d in [*range(1, groups), 0]]
-
-    def pass_on(scatter):
-        for _, w in order:
-            scatter.relay(w)
-
-    def hand_back(scatter, swap, ret):
-        for d, w in order:
-            scatter.got(w)
-            ret[pl.ds(pl.multiple_of(w * slots, slots), slots), :] = scatter.total(w).astype(bf16)
-            if d:
-                swap.copy(d).start()
+
+    def pass_on(first, last):
+        for p in range(first, last):
+            tk.relay(p)
+
+    def hand_back(first, last):
+        for p in range(first, last):
+            w = s.w_at(p)
+            tk.got(p)
+            ret_tok[pl.ds(pl.multiple_of(w * slots, slots), slots), :] = tk.total(p).astype(bf16)
+            if p < groups - 1:
+                tok_swap.copy(p + 1).start()
             else:
-                swap.own().start()
+                tok_swap.own().start()
 
     def totals(scatter, dst):
         scatter.got()
@@ -1227,30 +1382,33 @@
 
     lax.fori_loop(0, lanes, out_grad, 0)
     gos.start()
-    tk.ready()
     for c in loads[1:]:
         c.wait()
     heads.arrive()
+    tk.ready()
+    pass_on(0, groups)
     doc_cols = [meta_all[l].T[:, 0:1] for l in range(lanes)]
     for tile in range(lanes):
         attend_back_tile(tile, qkv, doc_cols, lse, grad_heads, grad_qkv, mask, dk, dv)
         if tile == 0:
-            pass_on(tk)
-        if tile == 1:
             gos.ready()
             gos.relay()
         if tile == 2:
             f_up.forward()
+            hand_back(0, groups // 2)
     for pair in range(head_cols // PAIR):
         grad_qkv[:, head_cols + pair * PAIR : head_cols + (pair + 1) * PAIR] = dk[pair].astype(bf16)
         grad_qkv[:, 2 * head_cols + pair * PAIR : 2 * head_cols + (pair + 1) * PAIR] = dv[pair].astype(bf16)
 
-    def weight_grad(m, carry):
-        ga[pl.ds(pl.multiple_of(m * head_cols, head_cols), head_cols), :] = mm(normed[:, cols(m)], grad_qkv[...], 0, 0).astype(bf16)
-        return carry
-
-    lax.fori_loop(0, lanes, weight_grad, 0)
-    gas.start()
+    for p in range(3):
+
+        def weight_grad(m, carry, p=p):
+            value = mm(normed[:, cols(m)], grad_qkv[:, p * head_cols : (p + 1) * head_cols], 0, 0)
+            ga[p, pl.ds(pl.multiple_of(m * head_cols, head_cols), head_cols), :] = value.astype(bf16)
+            return carry
+
+        lax.fori_loop(0, lanes, weight_grad, 0)
+        gas[p].start()
 
     def rows_grad(l, carry):
         value = mm(grad_qkv[pl.ds(pl.multiple_of(l * rows, rows), rows), :], attend_all[...], 1, 1)
@@ -1259,14 +1417,15 @@
 
     lax.fori_loop(0, lanes, rows_grad, 0)
     gns.start()
-    hand_back(tk, tok_swap, ret_tok)
     gns.ready()
     gns.relay()
+    hand_back(groups // 2, groups)
+    gas[0].relay()
     totals(gos, gl)
     gls.start()
-    gas.relay()
+    gas[1].relay()
+    gas[2].relay()
     tok_swap.arrive()
-    gls.relay()
 
     def layer(at, sums):
         attention = attention_out[at, :]
@@ -1298,21 +1457,24 @@
         return gain_sum + jnp.sum(grad * normed_v, axis=0, keepdims=True)
 
     attend_gain_grad = over_rows(first, jnp.zeros((1, width), f32))
-    feature = lax.broadcasted_iota(jnp.int32, (SMALL, shard), 0)
-    place_of = lax.broadcasted_iota(jnp.int32, (SMALL, shard), 1)
-    tail = jnp.zeros((SMALL, shard), f32)
+    used = sm_mine.shape[0]
+    feature = lax.broadcasted_iota(jnp.int32, (used, shard), 0)
+    place_of = lax.broadcasted_iota(jnp.int32, (used, shard), 1)
+    tail = jnp.zeros((used, shard), f32)
     for i, v in enumerate(sums):
         tail = jnp.where(place_of == i, v, tail)
     for w in range(groups):
         here = slice(w * shard, (w + 1) * shard)
-        value = jnp.where(feature == SMALL - 1, tail, grad_small[:, here])
+        value = jnp.where(feature == used - 1, tail, grad_small[0:used, here])
         value = jnp.where(feature == 0, attend_gain_grad[:, here], value)
         sm[w] = jnp.where(feature == 1, mixer_gain_grad[:, here], value)
     sms.start()
+    gls.relay()
     dws.finish(mine_down)
     f_down.start()
     sms.relay()
-    gas.finish(mine_attend)
+    for p in range(3):
+        gas[p].finish(mine_attend.at[:, pl.ds(p * head_cols, head_cols)])
     f_attend.start()
     gls.finish(mine_output)
     f_output.start()
@@ -1324,7 +1486,7 @@
     for task in gathers:
         task.arrive()
     small_out[...] = sum([sm_all[l] for l in range(1, lanes)], sm_all[0])
-    for task in [tk, gos, gns, dws, gas, gls, sms, tok_swap, heads] + gathers:
+    for task in [tk, gos, gns, dws, *gas, gls, sms, tok_swap, heads] + gathers:
         task.sent()
 
 
@@ -1353,9 +1515,10 @@
     scratch = [low(everyone, 3 * head_cols), low(width, width), low(width, 3 * head_cols), low(everyone, width)]
     scratch += group_bufs(groups, slots, width)
     scratch += group_bufs(width // 64, 64, head_cols, False) + group_bufs(rows // 64, 64, width, False)
-    scratch += [low(Z - 1, shard, width)] + lane_bufs(3 * head_cols, False) + lane_bufs(head_cols, False)
-    scratch += [wide(groups, SMALL, shard), wide(X - 1, Z, SMALL, shard), wide(Z - 1, SMALL, shard)]
-    scratch += [wide(SMALL, shard), wide(lanes, SMALL, shard)]
+    scratch += [low(Z - 1, shard, width)] + [low(3, width, head_cols), low(3, X - 1, Z, shard, head_cols), low(3, Z - 1, shard, head_cols)] + lane_bufs(head_cols, False)
+    used = -(-(5 + experts) // 8) * 8
+    scratch += [wide(groups, used, shard), wide(X - 1, Z, used, shard), wide(Z - 1, used, shard)]
+    scratch += [wide(used, shard), wide(lanes, used, shard)]
     scratch += [low(groups * slots, width)] * 2
     scratch += [wide(rows, width), wide(rows, width), low(rows, width), low(rows, width)]
     scratch += [low(everyone, head_cols), low(everyone, 3 * head_cols), wide(everyone, Q_TILE)]
@@ -1363,13 +1526,13 @@
     scratch += [low(shard, 3 * head_cols), low(shard, head_cols), low(shard, width)]
     scratch += [dma((4,))]
     scratch += GroupScatter.sems(lanes, groups) + GroupScatter.sems(lanes, 1) * 2
-    scratch += [dma((Z,))] * 2 + LaneScatter.sems(groups, X) * 3
+    scratch += [dma((Z,))] * 2 + LaneScatter.sems(groups, X) * 5
     scratch += LaneSwap.sems(groups) + GroupSwap.sems(lanes)
     scratch += GroupGather.sems(lanes) * 5
     outs = [
         (of((rows, width), bf16), vmem),
         (of((rows, width), bf16), vmem),
-        (of((SMALL, shard), f32), vmem),
+        (of((used, shard), f32), vmem),
         (of((lanes, shard, 3 * head_cols), bf16), anywhere),
         (of((lanes, shard, head_cols), bf16), anywhere),
         (of((lanes, shard, hidden), bf16), anywhere),
@@ -1433,8 +1596,8 @@
         up_mine = lax.dynamic_index_in_dim(up_weight.reshape(shard, groups, lanes, fine), lane, 2, keepdims=False)
         up_mine = up_mine.reshape(shard, groups * fine)
     (
-        normed_attend, qkv, lse, attn_mixed, attention_out, mix_all, small, meta_all, place,
-        attend_full, output_full, packed_cot, got_mix, cot_all, up_full, down_full,
+        lse, attn_mixed, attention_out, small, meta_all, place, normed_attend, qkv, attend_full, output_full, mix_all,
+        got_mix, cot_mine, cot_all, up_full, down_full,
     ) = front(groups, lanes, local, cap, slots, tokens, cotangent, meta_in, small, attend_weight, output_weight, up_mine, down_weight)
     doc_col = meta_all[:, 0].reshape(all_rows, 1)
     valid_all = meta_all[:, 1].reshape(all_rows, 1)
@@ -1456,18 +1619,17 @@
         full = gathered.reshape(lanes, shard, parts, -1)
         return full.transpose(1, 2, 0, 3).reshape(shard, -1).astype(f32)
 
-    if all_rows * width <= 2**20 and shard % 128 == 0 and cap % 8 == 0 and slots == local * cap and local == 2 and lanes * groups * cap <= all_rows:
+    if all_rows * width <= 2**20 and shard % 128 == 0 and cap % 8 == 0 and slots == local * cap and local == 2 and width == groups * fine and lanes * groups * cap <= all_rows:
         grad_mix, dense_out, grad_small, mine_up, down_half, tok_part, mix_e, grad_e, act_e, hidden_e = middle(
             groups, lanes, local, cap, experts, slots, (small, meta_all, place),
-            (mix_all, cot_all, up_full, down_full, got_mix, packed_cot, expert_up, expert_down))
+            (mix_all, cot_all, up_full, down_full, got_mix, cot_mine, expert_up, expert_down))
         layer_out, grad_tokens, small_out, out_attend, out_output, out_up, out_down = back(
             groups, lanes, experts, slots,
             (tokens, cotangent, meta_in, small, attention_out, attn_mixed, place, meta_all, lse, grad_small, grad_mix,
              dense_out, mine_up, down_half),
             (tok_part, qkv, output_full, attend_full, normed_attend))
-        grad_expert_up = jnp.einsum("etd,etf->edf", mix_e, hidden_e, preferred_element_type=f32)
-        grad_expert_down = jnp.einsum("etf,etd->efd", act_e, grad_e, preferred_element_type=f32)
-        sums, small_out = small_out[SMALL - 1], small_out.T
+        grad_expert_up, grad_expert_down = expert_grads(mix_e, hidden_e, act_e, grad_e)
+        sums, small_out = small_out[-1], small_out.T
         root_means = jnp.sqrt(sums[:4] / (jnp.maximum(sums[4], 1.0) * width))
         return (
             layer_out, grad_tokens, small_out[:, 0], widen(out_attend, 3), widen(out_output, 1), small_out[:, 1],
@@ -1475,7 +1637,7 @@
             out_down.reshape(-1, width).astype(f32), grad_expert_up, grad_expert_down, root_means,
         )
 
-    got_cot = group_gather(lane_swap(packed_cot.reshape(groups, slots, width))[None])
+    got_cot = group_gather(cot_mine[None])
 
     def coefficients(mix_rows):
         logits = mm(mix_rows, mix_cols)

time: 362 us -> 327 us (0.903)
  Pallas kernels: 317 us -> 289 us
  matrix products: 13.5 us -> 0 us
  local copies, waits for them, and re-layouts: 19.1 us -> 24.5 us
    pallas_call x1, Pallas kernels: 122 us -> 102 us  [front(): pl.pallas_call(functools.partial(front_kernel, groups, lanes, local, cap,...]
    pallas_call x1, Pallas kernels: 104 us -> 89.5 us  [middle(): pl.pallas_call(functools.partial(middle_kernel, groups, lanes, local, cap...]
    dot_general x2 -> x0, matrix products: 13.5 us -> none  [the longest x1 7.76 us: per_device(): jnp.einsum('etd,etf->edf', mix_e, hidden_e, preferred_element_type=f32)]
    pallas_call x0 -> x1, Pallas kernels: none -> 10.2 us  [expert_grads(): pl.pallas_call(expert_grads_kernel, grid=(local, width // tile), out_shap...]
    pallas_call x1, Pallas kernels: 91.3 us -> 87.3 us  [back(): pl.pallas_call(functools.partial(back_kernel, groups, lanes, experts), ou...]
where the time goes in v4:
time: 327 us; the launch traced here: 321 us
  Pallas kernels  289 us (88%)
  local copies, waits for them, and re-layouts  24.5 us (7%)
  other arithmetic  5.85 us (2%)
    pallas_call x1, Pallas kernels, front(): pl.pallas_call(functools.partial(front_kernel, groups, lanes, local, cap,...  102 us
    pallas_call x1, Pallas kernels, middle(): pl.pallas_call(functools.partial(middle_kernel, groups, lanes, local, cap...  89.5 us
    pallas_call x1, Pallas kernels, back(): pl.pallas_call(functools.partial(back_kernel, groups, lanes, experts), ou...  87.3 us
    pallas_call x1, Pallas kernels, expert_grads(): pl.pallas_call(expert_grads_kernel, grid=(local, width // tile), out_shap...  10.2 us
    unnamed x23, local copies, waits for them, and re-layouts  9.86 us
    convert_element_type x6, local copies, waits for them, and re-layouts, widen(): return full.transpose(1, 2, 0, 3).reshape(shard, -1).astype(f32)  6.58 us

profile of v4, /device:TPU:0, one launch (start us, length us, event | category | flops | bytes accessed | tf_op | source)
XLA Modules:
  0.0 321.3 jit_solution(12545689330006088071)
XLA Ops:
  0.6 0.7 add_convert_fusion
  1.4 0.6 pad.4.meta
  2.0 0.8 copy.42
  2.8 0.8 copy.43
  3.5 0.8 copy.45
  4.3 0.8 copy.44
  5.1 0.7 concatenate.3.small
  5.9 102.1 %front.1 = (f32[2,2,1024]{2,1,0:T(2,128)}, bf16[256,1024]{1,0:T(8,128)(2,1)}, f32[256,1024]{1,0:T(8,128)}, bf16[1024,128]{1,0:T(8,128)(2,1)}, f32[4,8,256]{2,1,0...) custom-call(bf16[256,1024]{1,0:T(8,128)(2,1)} %tokens.3, ...), custom_call_target="tpu_custom_call" | custom-call | flops 8000000000 | bytes 100000000 | tf_op jit(solution)/shard_map/front/pallas_call | solution.py:711
  108.0 89.5 %middle.1 = (f32[256,1024]{1,0:T(8,128)}, bf16[256,1024]{1,0:T(8,128)(2,1)}, f32[128,1024]{1,0:T(8,128)}, bf16[128,1024]{1,0:T(8,128)(2,1)}, bf16[4,128,1024]{2,...) custom-call(bf16[1024,128]{1,0:T(8,128)(2,1)} %get-tuple-element.48., ...), custom_call_target="tpu_custom_call" | custom-call | flops 35000000512 | bytes 100000000 | tf_op jit(solution)/shard_map/middle/pallas_call | solution.py:1268
  197.5 87.3 %back.1 = (bf16[256,1024]{1,0:T(8,128)(2,1)}, bf16[256,1024]{1,0:T(8,128)(2,1)}, f32[24,128]{1,0:T(8,128)}, bf16[4,128,768]{2,1,0:T(8,128)(2,1)}, bf16[4,128,256...) custom-call(bf16[256,1024]{1,0:T(8,128)(2,1)} %tokens.3, bf16[256,1024]{1,0:T(8,128)(2,1)} %cot.3, ...), custom_call_target="tpu_custom_call" | custom-call | flops 8000000000 | bytes 100000000 | tf_op jit(solution)/shard_map/back/pallas_call | solution.py:1541
  284.8 0.0 copy-start.5
  284.8 1.3 slice.28
  286.8 1.2 sqrt_bitcast_fusion
  288.0 1.2 slice.32
  289.3 1.3 slice_bitcast_fusion
  290.5 1.3 slice.31
  291.8 1.0 convert_bitcast_fusion
  292.8 0.2 copy.48
  293.0 1.0 copy.51
  294.0 0.0 copy-done.5
  294.0 0.3 copy.46
  294.3 0.1 copy.47
  294.4 0.0 copy-start.4
  294.4 1.6 copy.50
  296.1 0.0 copy-done.4
  296.1 0.3 copy.52
  296.3 0.1 bitcast_bitcast_fusion
  296.5 2.7 copy.49
  299.1 0.0 copy-start.1
  299.1 3.2 reshape.59
  302.4 0.0 copy-start
  302.4 2.9 bitcast_convert_fusion
  305.3 0.0 copy-done.1
  305.3 0.0 copy-done
  305.3 0.0 copy-start.2
  305.3 1.9 copy-done.2
  307.2 0.0 copy-start.3
  307.2 1.9 copy-done.3
  309.1 0.0 copy-start.7
  309.1 0.0 copy-start.6
  309.1 10.2 %expert_grads.1 = (f32[2,1024,1024]{2,1,0:T(8,128)}, f32[2,1024,1024]{2,1,0:T(8,128)}) custom-call(bf16[2,768,1024]{2,1,0:T(8,128)(2,1)S(1)} %copy-done, bf16[2,768,1024]{2,1,0:T(8,128)(2,1)S(1)} %copy-done.3, bf16[2,768,1024]{2,1,0:T(8,128)(2,1)S(1)} %copy-done.2, bf16[2,768,1024]{2,1,0:T(8,128)(2,1)S(1)} %copy-done.1), custom_call_target="tpu_custom_call" | custom-call | flops 6442450944 | bytes 30000000 | tf_op jit(solution)/shard_map/expert_grads/pallas_call | solution.py:951
  319.2 0.0 copy-done.7
  319.2 0.8 copy.55
  320.0 0.0 copy-done.6
  320.0 0.8 copy.56
  (1 shorter events, 0.0 us)
Async XLA Ops:
  284.8 9.2 %copy-start.5 = (bf16[4,128,768]{2,1,0:T(8,128)(2,1)S(1)}, bf16[4,128,768]{2,1,0:T(8,128)(2,1)}, u32[]{:S(2)}) copy-start(bf16[4,128,768]{2,1,0:T(8,128)(2,1)} %get-tuple-element.73) | copy-start | bytes 2359300
  294.4 1.6 copy-start.4
  299.1 6.2 %copy-start.1 = (bf16[2,768,1024]{2,1,0:T(8,128)(2,1)S(1)}, bf16[2,768,1024]{2,1,0:T(8,128)(2,1)}, u32[]{:S(2)}) copy-start(bf16[2,768,1024]{2,1,0:T(8,128)(2,1)} %get-tuple-element.80.grad_ref) | copy-start | bytes 9437188
  302.4 2.9 copy-start
  305.3 1.9 copy-start.2
  307.2 1.9 copy-start.3
  309.1 10.2 %copy-start.7 = (bf16[256,1024]{1,0:T(8,128)(2,1)S(1)}, bf16[256,1024]{1,0:T(8,128)(2,1)}, u32[]{:S(2)}) copy-start(bf16[256,1024]{1,0:T(8,128)(2,1)} %get-tuple-element.124) | copy-start | bytes 1572868
  309.1 11.0 %copy-start.6 = (bf16[256,1024]{1,0:T(8,128)(2,1)S(1)}, bf16[256,1024]{1,0:T(8,128)(2,1)}, u32[]{:S(2)}) copy-start(bf16[256,1024]{1,0:T(8,128)(2,1)} %get-tuple-element.125) | copy-start | bytes 1572868

commit v5 on v4

--- a/solution.py
+++ b/solution.py
@@ -197,16 +197,15 @@
     def l_peer(self, d):
         return lax.rem(self.l + d, self.L)
 
-    def greet(self, lane_peers=True):
+    def greet(self):
         barrier = pltpu.get_barrier_semaphore()
-        met = self.L - 1
         for d in range(1, self.L):
             pl.semaphore_signal(barrier, 1, device_id=(self.g, self.l_peer(d)), device_id_type=MESH)
-        if lane_peers:
-            met += self.W - 1
-            for d in range(1, self.W):
-                pl.semaphore_signal(barrier, 1, device_id=(self.w_peer(d), self.l), device_id_type=MESH)
-        pl.semaphore_wait(barrier, met)
+        for d in range(1, self.W):
+            pl.semaphore_signal(barrier, 1, device_id=(self.w_peer(d), self.l), device_id_type=MESH)
+
+    def met(self):
+        pl.semaphore_wait(pltpu.get_barrier_semaphore(), self.L + self.W - 2)
 
 
 def remote(src, dst, send_sem, recv_sem, group, lane):
@@ -404,8 +403,9 @@
 
 
 class LaneSwap:
-    def __init__(self, spot, src, dst, sems):
+    def __init__(self, spot, src, dst, sems, distances=None):
         self.s, self.src, self.dst = spot, src, dst
+        self.distances = range(spot.W) if distances is None else distances
         self.s_sem, self.r_sem = sems
 
     @staticmethod
@@ -421,22 +421,30 @@
         return pltpu.make_async_copy(self.src(self.s.g), self.dst(self.s.g), self.s_sem.at[0])
 
     def start(self):
-        for d in range(1, self.s.W):
-            self.copy(d).start()
-        self.own().start()
+        for d in self.distances:
+            if d:
+                self.copy(d).start()
+            else:
+                self.own().start()
 
     def got(self, w):
         s = self.s
         remote(self.src(w), self.dst(w), self.s_sem.at[0], self.r_sem.at[w], s.w_peer(1), s.l).wait_recv()
 
     def arrive(self):
-        for d in range(1, self.s.W):
+        for d in self.distances:
+            self.due(d)
+
+    def due(self, d):
+        if d:
             self.got(self.s.w_peer(self.s.W - d))
-        self.own().wait()
+        else:
+            self.own().wait()
 
     def sent(self):
-        for d in range(1, self.s.W):
-            self.copy(d).wait_send()
+        for d in self.distances:
+            if d:
+                self.copy(d).wait_send()
 
 
 class GroupSwap:
@@ -489,12 +497,13 @@
 
 def front_kernel(
     groups, lanes, local, cap, slots,
-    tokens, cot, meta, small, attend_w, output_w, up_w, down_w,
+    tokens, cot, facts, mixers, attend_w, output_w, up_w, down_w,
     lse, attn_mixed, attention_out, small_all, meta_all, place,
-    normed_to, qkv_to, attend_to, output_to, mix_to, got_mix, cot_mine, cot_all, up_all, down_all,
-    normed_out, qkv, attend_all, output_all, mix_all, tok_all, up_mine, mixed, mask, vt, packed_mix, packed_cot, out_sem, stage_sem, spread_y, spread_c, spread_r, *sems,
+    packed_cot, normed_to, qkv_to, attend_to, output_to, mix_to, got_mix, cot_mine, cot_all, up_all, down_all,
+    normed_out, qkv, attend_all, output_all, mix_all, tok_all, up_mine, mixed, mask, vt, packed_mix, meta, small, out_sem, stage_sem, spread_y, spread_c, spread_r, *sems,
 ):
     s = Spot(groups, lanes)
+    s.greet()
     rows, width = tokens.shape
     head_cols = width // lanes
     shard = attend_w.shape[0]
@@ -526,6 +535,11 @@
     for c in staged:
         c.start()
 
+    meta[...] = jnp.zeros_like(meta)
+    meta[0 : facts.shape[0], :] = facts[...]
+    known = mixers.shape[0]
+    rest = jnp.zeros((SMALL - known, shard), f32)
+    small[...] = jnp.concatenate([mixers[...].astype(f32), rest], axis=0).T.astype(bf16)
     tok = GroupGather(s, tokens, blocks(tok_all, rows), take(4))
     met = GroupGather(s, meta, lambda l: meta_all.at[l], take(4))
     cots = GroupGather(s, cot, blocks(cot_all, rows), take(4))
@@ -544,7 +558,7 @@
     up = LineGather(s, up_mine, blocks(up_all, shard), take(4))
     down = LineGather(s, down_w.at[pl.ds(pl.multiple_of(s.l * depth, depth), depth)], blocks(down_all, depth), take(4))
     swap = GroupSwap(s, blocks(mixed, rows), lambda l: attn_mixed.at[:, cols(l)], take(2))
-    cot_swap = LaneSwap(s, blocks(packed_cot, slots), lambda w: cot_mine.at[w], take(2))
+    cot_swap = LaneSwap(s, blocks(packed_cot, slots), lambda w: cot_mine.at[w], take(2), range(groups // 2))
     mix_swap = LaneSwap(s, blocks(packed_mix, slots), lambda w: got_mix.at[s.l, w], take(2))
 
     def spread(d):
@@ -554,7 +568,7 @@
 
     mix_spread = [spread(d) for d in range(groups)]
 
-    s.greet()
+    s.met()
     sml.start()
     met.start()
     tok.start()
@@ -698,6 +712,7 @@
         (of((width, SMALL), bf16), vmem),
         (of((lanes, 8, rows), f32), vmem),
         (of((rows, groups * slots), bf16), vmem),
+        (of((groups * slots, width), bf16), vmem),
     ]
     big = [(everyone, width), (everyone, 3 * head_cols), (width, 3 * head_cols), (width, width), (everyone, width)]
     outs += [(of(shape, bf16), anywhere) for shape in big]
@@ -720,7 +735,8 @@
             pltpu.VMEM((everyone, Q_TILE), f32),
             pltpu.VMEM((head_cols // PAIR, PAIR, everyone), bf16),
             pltpu.VMEM((groups * slots, width), bf16),
-            pltpu.VMEM((groups * slots, width), bf16),
+            pltpu.VMEM((8, rows), f32),
+            pltpu.VMEM((shard, SMALL), bf16),
             dma((5,)),
             dma((groups,)),
             dma((groups, Y)),
@@ -938,29 +954,74 @@
     lax.fori_loop(0, cols // PAIR, pair_step, 0)
 
 
-def expert_grads_kernel(x_ref, hidden_ref, act_ref, grad_ref, up_ref, down_ref):
-    up_ref[0] = mm(x_ref[0], hidden_ref[0], 0, 0)
-    down_ref[0] = mm(act_ref[0], grad_ref[0], 0, 0)
-
-
-def expert_grads(x, hidden, act, grad):
+def finish_kernel(
+    x_ref, hidden_ref, act_ref, grad_ref, attend_ref, output_ref, up_ref, down_ref, small_ref, layer_ref, tokens_ref,
+    expert_up, expert_down, attend_out, output_out, up_out, down_out, layer_out, tokens_out, gain_0, gain_1, blend, router, root,
+):
+    expert_up[0] = mm(x_ref[0], hidden_ref[0], 0, 0)
+    expert_down[0] = mm(act_ref[0], grad_ref[0], 0, 0)
+    lanes, _, units = up_ref.shape
+    width = output_out.shape[1]
+    for ref, out, parts in ((attend_ref, attend_out, 3), (output_ref, output_out, 1), (up_ref, up_out, units // SMALL)):
+        n = ref.shape[2] // parts
+        for p in range(parts):
+            for l in range(lanes):
+                out[:, (p * lanes + l) * n : (p * lanes + l + 1) * n] = ref[l, :, p * n : (p + 1) * n].astype(f32)
+    down_out[...] = down_ref[...].astype(f32)
+    layer_out[...] = layer_ref[...]
+    tokens_out[...] = tokens_ref[...]
+    small = small_ref[...]
+    gain_0[...] = small[0:1]
+    gain_1[...] = small[1:2]
+    blend[...] = small[2:4]
+    router[...] = small[4 : 4 + router.shape[0]]
+    sums = small[small.shape[0] - 1 :]
+    root[...] = jnp.sqrt(sums / (jnp.maximum(sums[:, 4:5], 1.0) * width))[:, 0:4]
+
+
+def finish(experts, x, hidden, act, grad, attend_all, output_all, up_all, down_all, small, layer, tokens):
     local, rows, width = x.shape
     units = hidden.shape[2]
+    lanes, shard, _ = up_all.shape
     tile = 256
-    tall = lambda: pl.BlockSpec((1, rows, tile), lambda e, m: (e, 0, m))
+    steps = local * width // tile
+    turns = width // tile
+    down_all = down_all.reshape(-1, width)
+    count = lambda n: n // steps
+    of = jax.ShapeDtypeStruct
+    tall = pl.BlockSpec((1, rows, tile), lambda e, m: (e, 0, m))
+    whole = lambda n: pl.BlockSpec((1, rows, n), lambda e, m: (e, 0, 0))
+    thin = lambda a: pl.BlockSpec((lanes, count(shard), a.shape[2]), lambda e, m: (0, e * turns + m, 0))
+    flat = lambda n, c: pl.BlockSpec((count(n), c), lambda e, m: (e * turns + m, 0))
+    fixed = lambda *s: pl.BlockSpec(s, lambda e, m: (0, 0))
+    outs = [
+        (of((local, width, units), f32), pl.BlockSpec((1, tile, units), lambda e, m: (e, m, 0))),
+        (of((local, units, width), f32), pl.BlockSpec((1, tile, width), lambda e, m: (e, m, 0))),
+        (of((shard, 3 * width), f32), flat(shard, 3 * width)),
+        (of((shard, width), f32), flat(shard, width)),
+        (of((shard, lanes * units), f32), flat(shard, lanes * units)),
+        (of(down_all.shape, f32), flat(*down_all.shape)),
+        (of(layer.shape, bf16), flat(*layer.shape)),
+        (of(tokens.shape, bf16), flat(*tokens.shape)),
+        (of((1, shard), f32), fixed(1, shard)),
+        (of((1, shard), f32), fixed(1, shard)),
+        (of((2, shard), f32), fixed(2, shard)),
+        (of((experts, shard), f32), fixed(experts, shard)),
+        (of((1, 4), f32), fixed(1, 4)),
+    ]
     return pl.pallas_call(
-        expert_grads_kernel,
-        grid=(local, width // tile),
-        out_shape=[jax.ShapeDtypeStruct((local, width, units), f32), jax.ShapeDtypeStruct((local, units, width), f32)],
+        finish_kernel,
+        grid=(local, turns),
+        out_shape=[o for o, _ in outs],
         in_specs=[
-            tall(), pl.BlockSpec((1, rows, units), lambda e, m: (e, 0, 0)),
-            tall(), pl.BlockSpec((1, rows, width), lambda e, m: (e, 0, 0)),
+            tall, whole(units), tall, whole(width), thin(attend_all), thin(output_all), thin(up_all),
+            flat(*down_all.shape), fixed(*small.shape), flat(*layer.shape), flat(*tokens.shape),
         ],
-        out_specs=[pl.BlockSpec((1, tile, units), lambda e, m: (e, m, 0)), pl.BlockSpec((1, tile, width), lambda e, m: (e, m, 0))],
-        compiler_params=pltpu.CompilerParams(vmem_limit_bytes=40 * 2**20),
-        cost_estimate=pl.CostEstimate(flops=4 * local * rows * width * units, bytes_accessed=3 * 10**7, transcendentals=0),
-        name="expert_grads",
-    )(x, hidden, act, grad)
+        out_specs=[p for _, p in outs],
+        compiler_params=pltpu.CompilerParams(vmem_limit_bytes=63 * 2**20),
+        cost_estimate=pl.CostEstimate(flops=4 * local * rows * width * units, bytes_accessed=4 * 10**7, transcendentals=0),
+        name="finish",
+    )(x, hidden, act, grad, attend_all, output_all, up_all, down_all, small, layer, tokens)
 
 
 def take_from(sems):
@@ -982,13 +1043,14 @@
 def middle_kernel(
     groups, lanes, local, cap, experts,
     small, meta_all, place,
-    mix_in, cot_in, up_in, down_in, got_mix_in, cot_mine, expert_up, expert_down,
+    mix_in, cot_in, up_in, down_in, got_mix_in, cot_mine, packed_cot, expert_up, expert_down,
     grad_mix, dense_out, grad_small, mine_up, down_half, tok_part, mix_e_out, grad_e_out, act_e_out, hidden_e_out,
     mix, cot, up, down, act, hidden, got_mix, got_cot, mix_e, grad_e, act_e, hidden_e, expert_in, expert_to,
     mx, mx_c, mx_y, dn, dn_c, dn_y, bk_c, bk_y, gu, gu_x, gu_z, gd, gd_x, ret_back, got_back, dots, coefs,
-    load_sem, out_sem, *sems,
+    load_sem, out_sem, spread_y, spread_c, spread_r, spread_o, *sems,
 ):
     s = Spot(groups, lanes)
+    s.greet()
     everyone, width = mix.shape
     rows = everyone // lanes
     units = up.shape[1]
@@ -1008,7 +1070,15 @@
     def load(i, src, dst):
         return pltpu.make_async_copy(src, dst, load_sem.at[i])
 
-    cot_spread = GroupGather(s, cot_mine, lambda l: got_cot.at[l], take(4))
+    cot_swap = LaneSwap(s, blocks(packed_cot, slots), lambda w: got_cot.at[s.l, w], take(2), range(groups // 2, groups))
+
+    def spread(d):
+        w = s.w_peer(groups - d)
+        first = d < groups // 2
+        return GroupGather(s, cot_mine.at[w] if first else got_cot.at[s.l, w], lambda l: got_cot.at[l, w],
+                           [spread_y.at[w], spread_c.at[w], spread_r.at[w], spread_o.at[w]], own=first)
+
+    cot_spread = [spread(d) for d in range(groups)]
     mxs = GroupScatter(s, lambda l: mx.at[l], None, mx_c, mx_y, take(5), False)
     dns = GroupScatter(s, lambda l: dn.at[l], None, dn_c, dn_y, take(5), False)
     near = groups // 2
@@ -1041,9 +1111,13 @@
         lax.fori_loop(0, units // tile, body, 0)
         return jnp.sum(dots[pl.ds(0, count), :], axis=1, keepdims=True)
 
-    s.greet()
-    cot_spread.start()
-    for c in loads:
+    for c in loads[:4]:
+        c.start()
+    s.met()
+    cot_swap.start()
+    for task in cot_spread[: groups // 2]:
+        task.start()
+    for c in loads[4:]:
         c.start()
     for c in loads[:4]:
         c.wait()
@@ -1055,6 +1129,9 @@
         valid = meta_all[l].T[:, 1:2]
         cot[at, :] = (coefs[at, 3:4] * (cot[at, :].astype(f32) * valid)).astype(bf16)
     dot = branch(mix, cot, up, down, act, hidden, everyone)
+    for d in range(groups // 2, groups):
+        cot_swap.due(d)
+        cot_spread[d].start()
     sign = jnp.where(columns == 3, 1.0, 0.0) - jnp.where(columns == 2, 1.0, 0.0)
     logits = (sign * (coefs[:, 2:3] * dot)).astype(bf16)
     grad_small[...] = mm(logits, mix[...], 0, 0)
@@ -1116,10 +1193,12 @@
         lax.fori_loop(first, last, body, 0)
 
     apart(got_mix, mix_e)
-    cot_spread.forward()
+    for task in cot_spread:
+        task.forward()
     mxs.ready()
     mxs.relay()
-    cot_spread.arrive()
+    for task in cot_spread:
+        task.arrive()
     apart(got_cot, grad_e)
 
     backs, toks = [act, hidden], [mix, cot]
@@ -1172,7 +1251,8 @@
                 for k in range(near):
                     bks[0].relay(k)
         if h == 0:
-            cot_spread.sent()
+            for task in cot_spread:
+                task.sent()
         together([b.at[pl.ds(0, rows_e)] for b in backs], got_cot, h * lanes * groups // 4, (h + 1) * lanes * groups // 4)
         bks[h].start()
 
@@ -1222,7 +1302,7 @@
     for c in outs:
         c.wait()
     dws.x_sent()
-    for task in [mxs, dns, *bks, ups, back_swap]:
+    for task in [cot_swap, mxs, dns, *bks, ups, back_swap]:
         task.sent()
 
 
@@ -1262,8 +1342,8 @@
     scratch += [low(width, units), low(X - 1, Z, shard, units), low(Z - 1, shard, units)]
     scratch += [low(units, width), low(X - 1, Z, shard, width)]
     scratch += [low(groups * slots, width)] * 2 + [wide(everyone, SMALL)] * 2
-    scratch += [dma((9,)), dma((4 * local + 1,))]
-    scratch += GroupGather.sems(lanes) + GroupScatter.sems(lanes, 1) * 2 + GroupScatter.sems(lanes, groups // 2) * 2
+    scratch += [dma((9,)), dma((4 * local + 1,)), dma((groups, Y)), dma((groups, Y)), dma((groups, lanes)), dma((groups, 1))]
+    scratch += LaneSwap.sems(groups) + GroupScatter.sems(lanes, 1) * 2 + GroupScatter.sems(lanes, groups // 2) * 2
     scratch += LaneScatter.sems(groups, X) * 2 + LaneSwap.sems(groups)
     return pl.pallas_call(
         functools.partial(middle_kernel, groups, lanes, local, cap, experts),
@@ -1279,7 +1359,7 @@
 
 def back_kernel(
     groups, lanes, experts,
-    tokens, cot, meta, small, attention_out, attn_mixed, place, meta_all, lse, grad_small, grad_mix_in, dense_out,
+    tokens, cot, small, attention_out, attn_mixed, place, meta_all, lse, grad_small, grad_mix_in, dense_out,
     mine_up, down_half, tok_part, qkv_in, output_in, attend_in, normed_in,
     layer_out, grad_tokens, small_out, all_attend, all_output, all_up, all_down,
     qkv, output_all, attend_all, normed, tk_h, tk_c, tk_y,
@@ -1288,6 +1368,7 @@
     grad_heads, grad_qkv, mask, dk, dv, valid_cols, mine_attend, mine_output, mine_down, stage_sem, *sems,
 ):
     s = Spot(groups, lanes)
+    s.greet()
     rows, width = tokens.shape
     head_cols = width // lanes
     slots = place.shape[1] // groups
@@ -1347,16 +1428,12 @@
     def over_rows(body, init):
         return lax.fori_loop(0, rows // step, lambda i, c: body(pl.ds(pl.multiple_of(i * step, step), step), c), init)
 
-    s.greet()
-    tk.start()
-    dws.start()
-    f_up.start()
     for c in loads:
         c.start()
     dk[...] = jnp.zeros_like(dk)
     dv[...] = jnp.zeros_like(dv)
     gains = small[...].astype(f32).T
-    mine = meta[...].T
+    mine = meta_all[s.l].T
     valid_cols[...] = jnp.broadcast_to(mine[:, 1:2], valid_cols.shape)
 
     def mid(at, gain_sum):
@@ -1370,8 +1447,11 @@
     mixer_gain_grad = over_rows(mid, jnp.zeros((1, width), f32))
     loads[0].wait()
     grad_mixed[...] = mm(grad_attn[...], output_all[...], 1, 1).astype(bf16)
+    s.met()
     for l in range(lanes):
         heads.send(l)
+    tk.start()
+    dws.start()
 
     def out_grad(m, carry):
         value = mm(attn_mixed[:, cols(m)], grad_attn[...], 0, 0).astype(bf16)
@@ -1387,6 +1467,7 @@
     heads.arrive()
     tk.ready()
     pass_on(0, groups)
+    f_up.start()
     doc_cols = [meta_all[l].T[:, 0:1] for l in range(lanes)]
     for tile in range(lanes):
         attend_back_tile(tile, qkv, doc_cols, lse, grad_heads, grad_qkv, mask, dk, dv)
@@ -1394,7 +1475,6 @@
             gos.ready()
             gos.relay()
         if tile == 2:
-            f_up.forward()
             hand_back(0, groups // 2)
     for pair in range(head_cols // PAIR):
         grad_qkv[:, head_cols + pair * PAIR : head_cols + (pair + 1) * PAIR] = dk[pair].astype(bf16)
@@ -1425,6 +1505,7 @@
     gls.start()
     gas[1].relay()
     gas[2].relay()
+    f_up.forward()
     tok_swap.arrive()
 
     def layer(at, sums):
@@ -1586,19 +1667,16 @@
     slots = -(-local * cap // 16) * 16
     all_rows = rows * lanes
 
-    small = jnp.concatenate(
-        [attend_gain[:, None], mixer_gain[:, None], blend_weight, router_weight,
-         jnp.zeros((shard, SMALL - 4 - experts), bf16)], axis=1)
-    meta_in = jnp.stack([doc_ids, valid_mask, routes[:, 0]]).astype(f32)
-    meta_in = jnp.pad(meta_in, ((0, 5), (0, 0)))
+    mixers = jnp.concatenate([attend_gain[None], mixer_gain[None], blend_weight.T, router_weight.T])
+    facts = jnp.stack([doc_ids, valid_mask, routes[:, 0]]).astype(f32)
     up_mine = up_weight
     if fine % 128:
         up_mine = lax.dynamic_index_in_dim(up_weight.reshape(shard, groups, lanes, fine), lane, 2, keepdims=False)
         up_mine = up_mine.reshape(shard, groups * fine)
     (
-        lse, attn_mixed, attention_out, small, meta_all, place, normed_attend, qkv, attend_full, output_full, mix_all,
+        lse, attn_mixed, attention_out, small, meta_all, place, packed_cot, normed_attend, qkv, attend_full, output_full, mix_all,
         got_mix, cot_mine, cot_all, up_full, down_full,
-    ) = front(groups, lanes, local, cap, slots, tokens, cotangent, meta_in, small, attend_weight, output_weight, up_mine, down_weight)
+    ) = front(groups, lanes, local, cap, slots, tokens, cotangent, facts, mixers, attend_weight, output_weight, up_mine, down_weight)
     doc_col = meta_all[:, 0].reshape(all_rows, 1)
     valid_all = meta_all[:, 1].reshape(all_rows, 1)
     attend_gain_row = small[:, 0].astype(f32)
@@ -1619,25 +1697,26 @@
         full = gathered.reshape(lanes, shard, parts, -1)
         return full.transpose(1, 2, 0, 3).reshape(shard, -1).astype(f32)
 
-    if all_rows * width <= 2**20 and shard % 128 == 0 and cap % 8 == 0 and slots == local * cap and local == 2 and width == groups * fine and lanes * groups * cap <= all_rows:
+    if all_rows * width <= 2**20 and shard % 128 == 0 and cap % 8 == 0 and slots == local * cap and local == 2 and fine == 128 and width == groups * fine and lanes * groups * cap <= all_rows:
         grad_mix, dense_out, grad_small, mine_up, down_half, tok_part, mix_e, grad_e, act_e, hidden_e = middle(
             groups, lanes, local, cap, experts, slots, (small, meta_all, place),
-            (mix_all, cot_all, up_full, down_full, got_mix, cot_mine, expert_up, expert_down))
+            (mix_all, cot_all, up_full, down_full, got_mix, cot_mine, packed_cot, expert_up, expert_down))
         layer_out, grad_tokens, small_out, out_attend, out_output, out_up, out_down = back(
             groups, lanes, experts, slots,
-            (tokens, cotangent, meta_in, small, attention_out, attn_mixed, place, meta_all, lse, grad_small, grad_mix,
+            (tokens, cotangent, small, attention_out, attn_mixed, place, meta_all, lse, grad_small, grad_mix,
              dense_out, mine_up, down_half),
             (tok_part, qkv, output_full, attend_full, normed_attend))
-        grad_expert_up, grad_expert_down = expert_grads(mix_e, hidden_e, act_e, grad_e)
-        sums, small_out = small_out[-1], small_out.T
-        root_means = jnp.sqrt(sums[:4] / (jnp.maximum(sums[4], 1.0) * width))
+        (
+            grad_expert_up, grad_expert_down, out_attend, out_output, out_up, out_down, layer_out, grad_tokens, gain_0, gain_1,
+            out_blend, out_router, root,
+        ) = finish(
+            experts, mix_e, hidden_e, act_e, grad_e, out_attend, out_output, out_up, out_down, small_out, layer_out, grad_tokens)
         return (
-            layer_out, grad_tokens, small_out[:, 0], widen(out_attend, 3), widen(out_output, 1), small_out[:, 1],
-            small_out[:, 4 : 4 + experts], small_out[:, 2:4], widen(out_up, groups),
-            out_down.reshape(-1, width).astype(f32), grad_expert_up, grad_expert_down, root_means,
+            layer_out, grad_tokens, gain_0.reshape(shard), out_attend, out_output, gain_1.reshape(shard), out_router.T,
+            out_blend.T, out_up, out_down, grad_expert_up, grad_expert_down, root.reshape(4),
         )
 
-    got_cot = group_gather(cot_mine[None])
+    got_cot = group_gather(lane_swap(packed_cot.reshape(groups, slots, width))[None])
 
     def coefficients(mix_rows):
         logits = mm(mix_rows, mix_cols)

time: 327 us -> 305 us (0.933)
  local copies, waits for them, and re-layouts: 24.5 us -> 0 us
  Pallas kernels: 289 us -> 295 us
    unnamed x23 -> x0, local copies, waits for them, and re-layouts: 9.86 us -> none
    pallas_call x1, Pallas kernels: 10.2 us -> 18.2 us  [finish(): pl.pallas_call(finish_kernel, grid=(local, turns), out_shape=[o for o, _...]
    convert_element_type x6 -> x0, local copies, waits for them, and re-layouts: 6.58 us -> none  [widen(): return full.transpose(1, 2, 0, 3).reshape(shard, -1).astype(f32)]
    pallas_call x1, Pallas kernels: 102 us -> 97.8 us  [front(): pl.pallas_call(functools.partial(front_kernel, groups, lanes, local, cap,...]
    pallas_call x1, Pallas kernels: 89.5 us -> 93.5 us  [middle(): pl.pallas_call(functools.partial(middle_kernel, groups, lanes, local, cap...]
    slice x3 -> x0, local copies, waits for them, and re-layouts: 3.89 us -> none  [the longest x1 1.34 us: per_device(): root_means = jnp.sqrt(sums[:4] / (jnp.maximum(sums[4], 1.0) * width))]
    convert_element_type x3 -> x1, other arithmetic: 4.65 us -> 1.31 us  [per_device(): facts = jnp.stack([doc_ids, valid_mask, routes[:, 0]]).astype(f32)]
where the time goes in v5:
time: 305 us; the launch traced here: 299 us
  Pallas kernels  295 us (97%)
    pallas_call x1, Pallas kernels, front(): pl.pallas_call(functools.partial(front_kernel, groups, lanes, local, cap,...  97.8 us
    pallas_call x1, Pallas kernels, middle(): pl.pallas_call(functools.partial(middle_kernel, groups, lanes, local, cap...  93.5 us
    pallas_call x1, Pallas kernels, back(): pl.pallas_call(functools.partial(back_kernel, groups, lanes, experts), ou...  85.9 us
    pallas_call x1, Pallas kernels, finish(): pl.pallas_call(finish_kernel, grid=(local, turns), out_shape=[o for o, _...  18.2 us

profile of v5, /device:TPU:0, one launch (start us, length us, event | category | flops | bytes accessed | tf_op | source)
XLA Modules:
  0.0 299.1 jit_solution(4025769005792535242)
XLA Ops:
  0.6 1.3 add_convert_fusion.facts
  2.0 1.3 pad_maximum_fusion.mixers
  3.3 97.8 %front.1 = (f32[2,2,1024]{2,1,0:T(2,128)}, bf16[256,1024]{1,0:T(8,128)(2,1)}, f32[256,1024]{1,0:T(8,128)}, bf16[1024,128]{1,0:T(8,128)(2,1)}, f32[4,8,256]{2,1,0...) custom-call(bf16[256,1024]{1,0:T(8,128)(2,1)} %tokens.3, ...), custom_call_target="tpu_custom_call" | custom-call | flops 8000000000 | bytes 100000000 | tf_op jit(solution)/shard_map/front/pallas_call | solution.py:726
  101.1 93.5 %middle.1 = (f32[256,1024]{1,0:T(8,128)}, bf16[256,1024]{1,0:T(8,128)(2,1)}, f32[128,1024]{1,0:T(8,128)}, bf16[128,1024]{1,0:T(8,128)(2,1)}, bf16[4,128,1024]{2,...) custom-call(bf16[1024,128]{1,0:T(8,128)(2,1)} %get-tuple-element.60., ...), custom_call_target="tpu_custom_call" | custom-call | flops 35000000512 | bytes 100000000 | tf_op jit(solution)/shard_map/middle/pallas_call | solution.py:1348
  194.6 85.9 %back.1 = (bf16[256,1024]{1,0:T(8,128)(2,1)}, bf16[256,1024]{1,0:T(8,128)(2,1)}, f32[24,128]{1,0:T(8,128)}, bf16[4,128,768]{2,1,0:T(8,128)(2,1)}, bf16[4,128,256...) custom-call(bf16[256,1024]{1,0:T(8,128)(2,1)} %tokens.3, bf16[256,1024]{1,0:T(8,128)(2,1)} %cot.3, ...), custom_call_target="tpu_custom_call" | custom-call | flops 8000000000 | bytes 100000000 | tf_op jit(solution)/shard_map/back/pallas_call | solution.py:1622
  280.5 18.2 %finish.1 = (f32[2,1024,1024]{2,1,0:T(8,128)}, f32[2,1024,1024]{2,1,0:T(8,128)}, f32[128,3072]{1,0:T(8,128)}, f32[128,1024]{1,0:T(8,128)}, f32[128,4096]{1,0:T(8...) custom-call(bf16[2,768,1024]{2,1,0:T(8,128)(2,1)} %get-tuple-element, ...), custom_call_target="tpu_custom_call" | custom-call | flops 6442450944 | bytes 40000000 | tf_op jit(solution)/shard_map/finish/pallas_call | solution.py:1012
